TPU v7x, 128 devices: a whole 4x4x4 slice. The times are simulated.
128 devices in a mesh: batch: 16 (over y, z), seq: 8 (over x, core).
Axes of the slice: x: 4, y: 4, z: 4, core: 2. Of those that a mesh axis runs over, the one named last changes fastest.
Arguments:
- inputs: bfloat16 [32, 1024, 1088], P('batch', 'seq'), may hold values from -6 to 6
- out_grad: bfloat16 [32, 1024, 1088], P('batch', 'seq'), may hold values from -6 to 6
- segment_ids: int32 [32, 1024], P('batch', 'seq'), may hold values from 0 to 3, as said below
- qkv_weight: bfloat16 [1088, 3264], P('batch', 'seq'), may hold values from -0.1875 to 0.1875
- out_weight: bfloat16 [1088, 1088], P('batch', 'seq'), may hold values from -0.75 to 0.75
- up_weight: bfloat16 [1088, 4352], P('batch', 'seq'), may hold values from -0.1875 to 0.1875
- down_weight: bfloat16 [4352, 1088], P('batch', 'seq'), may hold values from -0.09375 to 0.09375
- norm_gains: bfloat16 [2, 1088], P(None, 'seq'), may hold values from 0.5 to 1.5
- norm_shifts: bfloat16 [2, 1088], P(None, 'seq'), may hold values from -2 to 2
- qv_bias: bfloat16 [2, 1088], P(None, 'seq'), may hold values from -2 to 2
- proj_bias: bfloat16 [2, 1088], P(None, 'seq'), may hold values from -2 to 2
- up_bias: bfloat16 [1, 4352], P(None, 'seq'), may hold values from -2 to 2
Outputs:
- layer_out: bfloat16 [32, 1024, 1088], P('batch', 'seq')
- input_grad: float32 [32, 1024, 1088], P('batch', 'seq')
- qkv_weight_grad: float32 [1088, 3264], P('batch', 'seq')
- out_weight_grad: float32 [1088, 1088], P('batch', 'seq')
- up_weight_grad: float32 [1088, 4352], P('batch', 'seq')
- down_weight_grad: float32 [4352, 1088], P('batch', 'seq')
- norm_gains_grad: float32 [2, 1088], P(None, 'seq')
- norm_shifts_grad: float32 [2, 1088], P(None, 'seq')
- qv_bias_grad: float32 [2, 1088], P(None, 'seq')
- proj_bias_grad: float32 [2, 1088], P(None, 'seq')
- up_bias_grad: float32 [1, 4352], P(None, 'seq')
Inputs may be any that keep to these rules, and one draw needn't show every extreme that they name: `segment_ids`: within each sequence the document number starts at 0 at the first token, rises by one where a document starts, never falls and is at most 3; in each aligned group of 2 sequences one sequence, drawn from the seed, is a single document, and another reaches document number 3.
All inputs are finite; a program needn't handle non-finite values.
Results may differ from a plain program's by a relative error of at most 0.0089.
Values may be sent and summed in bfloat16 or wider, within the bound.
A program may use at most 192 MiB of HBM per device.

v0:
```python
import jax
import jax.numpy as jnp
from jax import lax
from jax.sharding import PartitionSpec as P

D = 1088
HEADS = 17
HEAD_DIM = 64
FF = 4352


def layer_norm(values, gain_row, shift_row):
    center = values - jnp.mean(values, axis=-1, keepdims=True)
    spread = jnp.mean(center * center, axis=-1, keepdims=True)
    return center * lax.rsqrt(spread + 1e-05) * gain_row + shift_row


def gelu_tanh(values):
    return jax.nn.gelu(values, approximate=True)


def collect(matrices, vectors):
    by_column = (
        lax.all_gather(matrices[0], "seq", axis=1, tiled=True),
        lax.all_gather(matrices[1], "seq", axis=1, tiled=True),
        lax.all_gather(matrices[2], "seq", axis=1, tiled=True),
        lax.all_gather(matrices[3], "seq", axis=1, tiled=True),
        lax.all_gather(vectors[0], "seq", axis=1, tiled=True),
        lax.all_gather(vectors[1], "seq", axis=1, tiled=True),
        lax.all_gather(vectors[2], "seq", axis=1, tiled=True),
        lax.all_gather(vectors[3], "seq", axis=1, tiled=True),
        lax.all_gather(vectors[4], "seq", axis=1, tiled=True),
    )
    by_row = (
        lax.all_gather(by_column[0], "batch", axis=0, tiled=True),
        lax.all_gather(by_column[1], "batch", axis=0, tiled=True),
        lax.all_gather(by_column[2], "batch", axis=0, tiled=True),
        lax.all_gather(by_column[3], "batch", axis=0, tiled=True),
    )
    return (tuple(by_row), tuple((member.astype(jnp.float32) for member in by_column[4:])))


def split_heads(matrix):
    return matrix.reshape(matrix.shape[0], HEADS, HEAD_DIM)


def per_device(
    inputs,
    out_grad,
    segment_ids,
    qkv_weight,
    out_weight,
    up_weight,
    down_weight,
    norm_gains,
    norm_shifts,
    qv_bias,
    proj_bias,
    up_bias,
):
    micro_count, local_rows, model_width = inputs.shape
    total_rows = local_rows * lax.axis_size("seq")
    first_row = lax.axis_index("seq") * local_rows
    score_scale = HEAD_DIM ** (-0.5)
    documents = lax.all_gather(segment_ids, "seq", axis=1, tiled=True)
    shards = (qkv_weight, out_weight, up_weight, down_weight)
    vector_shards = (norm_gains, norm_shifts, qv_bias, proj_bias, up_bias)
    local_place = first_row + jnp.arange(local_rows)
    whole_place = jnp.arange(total_rows)

    def masked_scores(query_part, key_part, query_docs, key_docs, query_place, key_place):
        scores = (
            jnp.einsum(
                "qhd,khd->hqk",
                split_heads(query_part),
                split_heads(key_part),
                preferred_element_type=jnp.float32,
            )
            * score_scale
        )
        allowed = (query_docs[:, None] == key_docs[None, :]) & (
            key_place[None, :] <= query_place[:, None]
        )
        return jnp.where(allowed[None], scores, -1e30)

    def micro_step(step_index, loop_state):
        out_rows, grad_rows_all, kept_rows, gain_grads, shift_grads = loop_state
        hidden = lax.dynamic_index_in_dim(inputs, step_index, 0, keepdims=False).astype(jnp.float32)
        cotangent = lax.dynamic_index_in_dim(out_grad, step_index, 0, keepdims=False).astype(
            jnp.float32
        )
        key_docs = lax.dynamic_index_in_dim(documents, step_index, 0, keepdims=False)
        query_docs = lax.dynamic_slice_in_dim(key_docs, first_row, local_rows)
        matrices, vectors = collect(shards, vector_shards)
        qkv_full, out_full, up_full, down_full = matrices
        gain_rows, shift_rows, qv_rows, proj_rows, up_row = vectors
        normed = layer_norm(hidden, gain_rows[0], shift_rows[0]).astype(jnp.bfloat16)
        projected = jnp.dot(normed, qkv_full, preferred_element_type=jnp.float32)
        queries = (projected[:, :D] + qv_rows[0]).astype(jnp.bfloat16)
        key_rows = projected[:, D : 2 * D].astype(jnp.bfloat16)
        value_rows = (projected[:, 2 * D :] + qv_rows[1]).astype(jnp.bfloat16)
        key_all, value_all = (
            lax.all_gather(key_rows, "seq", axis=0, tiled=True),
            lax.all_gather(value_rows, "seq", axis=0, tiled=True),
        )
        scores = masked_scores(queries, key_all, query_docs, key_docs, local_place, whole_place)
        row_peak = jnp.max(scores, axis=-1, keepdims=True)
        exponent_rows = jnp.exp(scores - row_peak)
        row_total = jnp.sum(exponent_rows, axis=-1, keepdims=True)
        soft_low = (exponent_rows / row_total).astype(jnp.bfloat16)
        log_total = row_peak + jnp.log(row_total)
        value_heads = split_heads(value_all)
        attended = (
            jnp.einsum("hqk,khd->qhd", soft_low, value_heads, preferred_element_type=jnp.float32)
            .reshape(local_rows, D)
            .astype(jnp.bfloat16)
        )
        middle = (
            hidden + jnp.dot(attended, out_full, preferred_element_type=jnp.float32) + proj_rows[0]
        )
        normed_two = layer_norm(middle, gain_rows[1], shift_rows[1]).astype(jnp.bfloat16)
        inner_pre = jnp.dot(normed_two, up_full, preferred_element_type=jnp.float32) + up_row[0]
        active = gelu_tanh(inner_pre).astype(jnp.bfloat16)
        layer_rows = (
            middle + jnp.dot(active, down_full, preferred_element_type=jnp.float32) + proj_rows[1]
        ).astype(jnp.bfloat16)
        fresh = lax.optimization_barrier((shards, vector_shards, layer_rows))
        matrices, vectors = collect(fresh[0], fresh[1])
        qkv_full, out_full, up_full, down_full = matrices
        top_grad = cotangent.astype(jnp.bfloat16)
        down_in = jnp.einsum("td,fd->tf", top_grad, down_full, preferred_element_type=jnp.float32)
        gelu_value, gelu_pull = jax.vjp(gelu_tanh, inner_pre)
        inner_grad = gelu_pull(down_in)[0].astype(jnp.bfloat16)
        normed_two_grad = jnp.einsum(
            "tf,df->td", inner_grad, up_full, preferred_element_type=jnp.float32
        )
        norm_value, second_pull = jax.vjp(layer_norm, middle, gain_rows[1], shift_rows[1])
        middle_part, gain_two, shift_two = second_pull(normed_two_grad)
        middle_grad = cotangent + middle_part
        branch_grad = middle_grad.astype(jnp.bfloat16)
        attended_grad = jnp.einsum(
            "te,de->td", branch_grad, out_full, preferred_element_type=jnp.float32
        ).astype(jnp.bfloat16)
        scores_again = masked_scores(
            queries, key_all, query_docs, key_docs, local_place, whole_place
        )
        probs = jnp.exp(scores_again - log_total)
        attended_heads = split_heads(attended_grad)
        prob_grad = jnp.einsum(
            "qhd,khd->hqk", attended_heads, value_heads, preferred_element_type=jnp.float32
        )
        row_inner = jnp.sum(probs * prob_grad, axis=-1, keepdims=True)
        score_grad = (probs * (prob_grad - row_inner)).astype(jnp.bfloat16)
        query_grad = (
            jnp.einsum(
                "hqk,khd->qhd", score_grad, split_heads(key_all), preferred_element_type=jnp.float32
            )
            * score_scale
        ).reshape(local_rows, D)
        probs_low = probs.astype(jnp.bfloat16)
        key_terms = (
            jnp.einsum(
                "hqk,qhd->khd", score_grad, split_heads(queries), preferred_element_type=jnp.float32
            )
            * score_scale
        ).reshape(total_rows, D)
        value_terms = jnp.einsum(
            "hqk,qhd->khd", probs_low, attended_heads, preferred_element_type=jnp.float32
        ).reshape(total_rows, D)
        key_grad, value_grad = (
            lax.psum_scatter(key_terms, "seq", scatter_dimension=0, tiled=True),
            lax.psum_scatter(value_terms, "seq", scatter_dimension=0, tiled=True),
        )
        qkv_grad = jnp.concatenate(
            [
                query_grad.astype(jnp.bfloat16),
                key_grad.astype(jnp.bfloat16),
                value_grad.astype(jnp.bfloat16),
            ],
            axis=1,
        )
        normed_grad = jnp.einsum(
            "tc,dc->td", qkv_grad, qkv_full, preferred_element_type=jnp.float32
        )
        first_value, first_pull = jax.vjp(layer_norm, hidden, gain_rows[0], shift_rows[0])
        hidden_part, gain_one, shift_one = first_pull(normed_grad)
        input_rows = middle_grad + hidden_part
        fresh_rows = (
            normed,
            qkv_grad,
            attended,
            branch_grad,
            normed_two,
            inner_grad,
            active,
            top_grad,
        )
        kept_next = tuple(
            (
                lax.dynamic_update_index_in_dim(stored, update, step_index, 0)
                for stored, update in zip(kept_rows, fresh_rows)
            )
        )
        return (
            lax.dynamic_update_index_in_dim(out_rows, layer_rows, step_index, 0),
            lax.dynamic_update_index_in_dim(grad_rows_all, input_rows, step_index, 0),
            kept_next,
            gain_grads + jnp.stack([gain_one, gain_two]),
            shift_grads + jnp.stack([shift_one, shift_two]),
        )

    def zeros_rows(columns):
        return jnp.zeros((micro_count, local_rows, columns), jnp.bfloat16)

    initial = (
        jnp.zeros((micro_count, local_rows, D), jnp.bfloat16),
        jnp.zeros((micro_count, local_rows, D), jnp.float32),
        (
            zeros_rows(D),
            zeros_rows(3 * D),
            zeros_rows(D),
            zeros_rows(D),
            zeros_rows(D),
            zeros_rows(FF),
            zeros_rows(FF),
            zeros_rows(D),
        ),
        jnp.zeros((2, D), jnp.float32),
        jnp.zeros((2, D), jnp.float32),
    )
    out_rows, grad_rows_all, kept_rows, gain_grads, shift_grads = lax.fori_loop(
        0, micro_count, micro_step, initial
    )
    stacked = tuple(
        (member.reshape(micro_count * local_rows, member.shape[2]) for member in kept_rows)
    )
    (
        normed_all,
        qkv_grad_all,
        attended_all,
        branch_all,
        normed_two_all,
        inner_all,
        active_all,
        top_all,
    ) = stacked
    qkv_terms = jnp.einsum(
        "td,tc->dc", normed_all, qkv_grad_all, preferred_element_type=jnp.float32
    )
    out_terms = jnp.einsum(
        "td,te->de", attended_all, branch_all, preferred_element_type=jnp.float32
    )
    up_terms = jnp.einsum(
        "td,tf->df", normed_two_all, inner_all, preferred_element_type=jnp.float32
    )
    down_terms = jnp.einsum("tf,td->fd", active_all, top_all, preferred_element_type=jnp.float32)
    qv_terms = jnp.stack(
        [
            jnp.sum(qkv_grad_all[:, :D], axis=0, dtype=jnp.float32),
            jnp.sum(qkv_grad_all[:, 2 * D :], axis=0, dtype=jnp.float32),
        ]
    )
    proj_terms = jnp.stack(
        [
            jnp.sum(branch_all, axis=0, dtype=jnp.float32),
            jnp.sum(top_all, axis=0, dtype=jnp.float32),
        ]
    )
    up_bias_terms = jnp.sum(inner_all, axis=0, dtype=jnp.float32)[None]
    col_parts = (
        lax.psum_scatter(qkv_terms, "seq", scatter_dimension=1, tiled=True),
        lax.psum_scatter(out_terms, "seq", scatter_dimension=1, tiled=True),
        lax.psum_scatter(up_terms, "seq", scatter_dimension=1, tiled=True),
        lax.psum_scatter(down_terms, "seq", scatter_dimension=1, tiled=True),
        lax.psum_scatter(gain_grads, "seq", scatter_dimension=1, tiled=True),
        lax.psum_scatter(shift_grads, "seq", scatter_dimension=1, tiled=True),
        lax.psum_scatter(qv_terms, "seq", scatter_dimension=1, tiled=True),
        lax.psum_scatter(proj_terms, "seq", scatter_dimension=1, tiled=True),
        lax.psum_scatter(up_bias_terms, "seq", scatter_dimension=1, tiled=True),
    )
    row_parts = (
        lax.psum_scatter(col_parts[0], "batch", scatter_dimension=0, tiled=True),
        lax.psum_scatter(col_parts[1], "batch", scatter_dimension=0, tiled=True),
        lax.psum_scatter(col_parts[2], "batch", scatter_dimension=0, tiled=True),
        lax.psum_scatter(col_parts[3], "batch", scatter_dimension=0, tiled=True),
    )
    vector_parts = lax.psum(
        (col_parts[4], col_parts[5], col_parts[6], col_parts[7], col_parts[8]), "batch"
    )
    return (
        out_rows,
        grad_rows_all,
        row_parts[0],
        row_parts[1],
        row_parts[2],
        row_parts[3],
        vector_parts[0],
        vector_parts[1],
        vector_parts[2],
        vector_parts[3],
        vector_parts[4],
    )


def solution(mesh):
    return jax.shard_map(
        per_device,
        mesh=mesh,
        in_specs=(
            P("batch", "seq", None),
            P("batch", "seq", None),
            P("batch", "seq"),
            P("batch", "seq"),
            P("batch", "seq"),
            P("batch", "seq"),
            P("batch", "seq"),
            P(None, "seq"),
            P(None, "seq"),
            P(None, "seq"),
            P(None, "seq"),
            P(None, "seq"),
        ),
        out_specs=(
            P("batch", "seq", None),
            P("batch", "seq", None),
            P("batch", "seq"),
            P("batch", "seq"),
            P("batch", "seq"),
            P("batch", "seq"),
            P(None, "seq"),
            P(None, "seq"),
            P(None, "seq"),
            P(None, "seq"),
            P(None, "seq"),
        ),
        check_vma=False,
    )
```

profile of v0, /device:TPU:0, one launch (start us, length us, event | category | flops | bytes accessed | tf_op | source)
XLA Modules:
  0.0 2096.4 jit_solution(17439191814976592446)
XLA Ops:
  8.1 11.6 all_gather.256
  19.8 1492.4 %while.39 = (s32[]{:T(128)}, bf16[2,128,1088]{1,2,0:T(8,128)(2,1)}, f32[2,128,1088]{1,2,0:T(8,128)}, bf16[2,128,1088]{1,2,0:T(8,128)(2,1)}, bf16[2,128,3264]{1,2...) while((s32[]{:T(128)}, bf16[2,128,1088]{1,2,0:T(8,128)(2,1)}, ...), condition=%wide.region_18.19_spmd.clone, body=%wide.region_0.18_spmd.clone.sunk | while | flops 9063718912 | bytes 732043968 | solution.py:231
  20.2 13.5 all-gather.43
  35.5 12.9 all_gather.275
  68.2 36.1 %all-gather.67.cloned.1.call-done = bf16[16,68,3264]{2,1,0:T(8,128)(2,1)} async-done(((bf16[1,68,3264]{2,1,0:T(8,128)(2,1)}), bf16[16,68,3264]{2,1,0:T(8,128)(2,1)}) %all-gather.67.cloned.1.call-update) | async-done | bytes 7102480 | tf_op jit(solution)/shard_map/while/body/eval_jaxpr/all_gather | solution.py:35
  121.1 10.5 all-gather.47
  132.8 13.5 all-gather.49
  148.0 13.5 all_gather.276
  172.5 25.7 %all-reduce.15 = bf16[4352]{0:T(1024)(128)(2,1)S(1)} all-reduce(bf16[4352]{0:T(1024)(128)(2,1)S(1)} %dynamic-update-slice.3), channel_id=1, replica_groups=mesh['batch'=16,'seq'=8] {'seq'}, use_global_device_ids=true, to_apply=%add | all-reduce | flops 4352 | bytes 17408 | tf_op jit(solution)/shard_map/while
  220.5 74.1 %all-gather.77.cloned.1.call-done = bf16[16,68,4352]{2,1,0:T(8,128)(2,1)} async-done(((bf16[1,68,4352]{2,1,0:T(8,128)(2,1)}), bf16[16,68,4352]{2,1,0:T(8,128)(2,1)}) %all-gather.77.cloned.1.call-update) | async-done | bytes 9469968 | tf_op jit(solution)/shard_map/while/body/eval_jaxpr/all_gather | solution.py:37
  294.6 10.5 reshape.511
  312.7 62.4 %all-gather.75.cloned.1.call-done = bf16[4352,1088]{1,0:T(8,128)(2,1)} async-done(((bf16[272,1088]{1,0:T(8,128)(2,1)}), bf16[4352,1088]{1,0:T(8,128)(2,1)}) %all-gather.75.cloned.1.call-update) | async-done | bytes 9469968 | tf_op jit(solution)/shard_map/while/body/eval_jaxpr/all_gather | solution.py:38
  383.2 13.2 all_gather.280
  397.3 13.3 all-gather.51
  412.3 13.4 all_gather.278
  426.9 13.2 all-gather.53
  447.5 75.6 %all-gather.81.cloned.1.call-done = bf16[16,68,4352]{2,1,0:T(8,128)(2,1)} async-done(((bf16[1,68,4352]{2,1,0:T(8,128)(2,1)}), bf16[16,68,4352]{2,1,0:T(8,128)(2,1)}) %all-gather.81.cloned.1.call-update) | async-done | bytes 9469968 | tf_op jit(solution)/shard_map/while/body/eval_jaxpr/all_gather | solution.py:37
  533.4 70.3 %all-gather.79.cloned.1.call-done = bf16[4352,1088]{1,0:T(8,128)(2,1)} async-done(((bf16[272,1088]{1,0:T(8,128)(2,1)}), bf16[4352,1088]{1,0:T(8,128)(2,1)}) %all-gather.79.cloned.1.call-update) | async-done | bytes 9469968 | tf_op jit(solution)/shard_map/while/body/eval_jaxpr/all_gather | solution.py:38
  638.2 35.2 %all-gather.83.cloned.1.call-done = bf16[16,68,3264]{2,1,0:T(8,128)(2,1)} async-done(((bf16[1,68,3264]{2,1,0:T(8,128)(2,1)}), bf16[16,68,3264]{2,1,0:T(8,128)(2,1)}) %all-gather.83.cloned.1.call-update) | async-done | bytes 7102480 | tf_op jit(solution)/shard_map/while/body/eval_jaxpr/all_gather | solution.py:35
  688.0 25.9 %reduce-scatter.38.cloned.1.call-done = f32[128,1088]{0,1:T(8,128)} async-done(((f32[1024,1088]{0,1:T(8,128)}), f32[128,1088]{0,1:T(8,128)}) %reduce-scatter.38.cloned.1.call-update) | async-done | bytes 557072 | tf_op jit(solution)/shard_map/while/body/eval_jaxpr/reduce_scatter | solution.py:171
  715.0 38.8 %reduce-scatter.36.cloned.1.call-done = f32[128,1088]{0,1:T(8,128)} async-done(((f32[1024,1088]{0,1:T(8,128)}), f32[128,1088]{0,1:T(8,128)}) %reduce-scatter.36.cloned.1.call-update) | async-done | bytes 557072 | tf_op jit(solution)/shard_map/while/body/eval_jaxpr/reduce_scatter | solution.py:172
  763.2 13.5 all-gather.43
  778.5 12.9 all_gather.275
  811.2 35.1 %all-gather.67.cloned.1.call-done = bf16[16,68,3264]{2,1,0:T(8,128)(2,1)} async-done(((bf16[1,68,3264]{2,1,0:T(8,128)(2,1)}), bf16[16,68,3264]{2,1,0:T(8,128)(2,1)}) %all-gather.67.cloned.1.call-update) | async-done | bytes 7102480 | tf_op jit(solution)/shard_map/while/body/eval_jaxpr/all_gather | solution.py:35
  863.1 10.5 all-gather.47
  874.9 13.5 all-gather.49
  890.0 13.5 all_gather.276
  914.5 25.3 %all-reduce.15 = bf16[4352]{0:T(1024)(128)(2,1)S(1)} all-reduce(bf16[4352]{0:T(1024)(128)(2,1)S(1)} %dynamic-update-slice.3), channel_id=1, replica_groups=mesh['batch'=16,'seq'=8] {'seq'}, use_global_device_ids=true, to_apply=%add | all-reduce | flops 4352 | bytes 17408 | tf_op jit(solution)/shard_map/while
  962.2 74.1 %all-gather.77.cloned.1.call-done = bf16[16,68,4352]{2,1,0:T(8,128)(2,1)} async-done(((bf16[1,68,4352]{2,1,0:T(8,128)(2,1)}), bf16[16,68,4352]{2,1,0:T(8,128)(2,1)}) %all-gather.77.cloned.1.call-update) | async-done | bytes 9469968 | tf_op jit(solution)/shard_map/while/body/eval_jaxpr/all_gather | solution.py:37
  1036.3 10.7 reshape.511
  1054.6 62.2 %all-gather.75.cloned.1.call-done = bf16[4352,1088]{1,0:T(8,128)(2,1)} async-done(((bf16[272,1088]{1,0:T(8,128)(2,1)}), bf16[4352,1088]{1,0:T(8,128)(2,1)}) %all-gather.75.cloned.1.call-update) | async-done | bytes 9469968 | tf_op jit(solution)/shard_map/while/body/eval_jaxpr/all_gather | solution.py:38
  1124.9 13.2 all_gather.280
  1139.0 13.3 all-gather.51
  1154.0 13.4 all_gather.278
  1168.7 13.2 all-gather.53
  1189.2 75.5 %all-gather.81.cloned.1.call-done = bf16[16,68,4352]{2,1,0:T(8,128)(2,1)} async-done(((bf16[1,68,4352]{2,1,0:T(8,128)(2,1)}), bf16[16,68,4352]{2,1,0:T(8,128)(2,1)}) %all-gather.81.cloned.1.call-update) | async-done | bytes 9469968 | tf_op jit(solution)/shard_map/while/body/eval_jaxpr/all_gather | solution.py:37
  1264.7 10.3 reshape.513
  1275.0 70.3 %all-gather.79.cloned.1.call-done = bf16[4352,1088]{1,0:T(8,128)(2,1)} async-done(((bf16[272,1088]{1,0:T(8,128)(2,1)}), bf16[4352,1088]{1,0:T(8,128)(2,1)}) %all-gather.79.cloned.1.call-update) | async-done | bytes 9469968 | tf_op jit(solution)/shard_map/while/body/eval_jaxpr/all_gather | solution.py:38
  1379.6 35.6 %all-gather.83.cloned.1.call-done = bf16[16,68,3264]{2,1,0:T(8,128)(2,1)} async-done(((bf16[1,68,3264]{2,1,0:T(8,128)(2,1)}), bf16[16,68,3264]{2,1,0:T(8,128)(2,1)}) %all-gather.83.cloned.1.call-update) | async-done | bytes 7102480 | tf_op jit(solution)/shard_map/while/body/eval_jaxpr/all_gather | solution.py:35
  1429.8 25.9 %reduce-scatter.38.cloned.1.call-done = f32[128,1088]{0,1:T(8,128)} async-done(((f32[1024,1088]{0,1:T(8,128)}), f32[128,1088]{0,1:T(8,128)}) %reduce-scatter.38.cloned.1.call-update) | async-done | bytes 557072 | tf_op jit(solution)/shard_map/while/body/eval_jaxpr/reduce_scatter | solution.py:171
  1456.7 38.8 %reduce-scatter.36.cloned.1.call-done = f32[128,1088]{0,1:T(8,128)} async-done(((f32[1024,1088]{0,1:T(8,128)}), f32[128,1088]{0,1:T(8,128)}) %reduce-scatter.36.cloned.1.call-update) | async-done | bytes 557072 | tf_op jit(solution)/shard_map/while/body/eval_jaxpr/reduce_scatter | solution.py:172
  1555.1 85.9 %reduce-scatter.32.cloned.1.call-done = f32[1088,408]{0,1:T(8,128)} async-done(((f32[1088,3264]{0,1:T(8,128)}), f32[1088,408]{0,1:T(8,128)}) %reduce-scatter.32.cloned.1.call-update) | async-done | bytes 1775632
  1641.0 109.1 %reduce-scatter.24.cloned.1.call-done = f32[1088,544]{0,1:T(8,128)} async-done(((f32[1088,4352]{0,1:T(8,128)}), f32[1088,544]{0,1:T(8,128)}) %reduce-scatter.24.cloned.1.call-update) | async-done | bytes 2367504 | tf_op jit(solution)/shard_map/reduce_scatter | solution.py:273
  1750.2 104.2 %reduce-scatter.26.cloned.1.call-done = f32[4352,136]{0,1:T(8,128)} async-done(((f32[4352,1088]{0,1:T(8,128)}), f32[4352,136]{0,1:T(8,128)}) %reduce-scatter.26.cloned.1.call-update) | async-done | bytes 2367504 | tf_op jit(solution)/shard_map/reduce_scatter | solution.py:274
  1867.7 24.2 %all-reduce.13 = (f32[2,1088]{1,0:T(2,128)S(1)}, f32[2,1088]{1,0:T(2,128)S(1)}, f32[2,1088]{1,0:T(2,128)S(1)}, f32[2,1088]{1,0:T(2,128)S(1)}) all-reduce(f32[2,1088]{1,0:T(2,128)S(1)} %copy-done.47, f32[2,1088]{1,0:T(2,128)S(1)} %copy-done.50, ...), channel_id=12, replica_groups=mesh['batch'=16,'seq'=8] {'seq'}, use_global_device_ids=true, to_apply=%region_27.28.clone | all-reduce | flops 8704 | bytes 69632
  1893.2 76.4 %all-reduce.11 = (f32[2,136]{1,0:T(2,128)}, f32[2,136]{1,0:T(2,128)}, f32[2,136]{1,0:T(2,128)}, f32[2,136]{1,0:T(2,128)}, f32[1,544]{1,0:T(1,128)}) all-reduce(f32[2,136]{1,0:T(2,128)S(1)} %get-tuple-element.1065, f32[2,136]{1,0:T(2,128)S(1)} %get-tuple-element.1064, ...), channel_id=1, replica_groups=mesh['batch'=16,'seq'=8] {'batch'}, use_global_device_ids=true, to_apply=%region_28.29 | all-reduce | flops 1632 | bytes 13056 | tf_op jit(solution)/shard_map/psum | solution.py:287
  1969.6 35.8 %all-reduce.18.cloned.1.call-done = (f32[1088,408]{0,1:T(8,128)}, f32[1088,136]{0,1:T(8,128)}, f32[1088,544]{0,1:T(8,128)}) async-done(((f32[1088,408]{0,1:T(8,128)}, f32[1088,136]{0,1:T(8,128)}, f32[1088,544]{0,1:T(8,128)}), (f32[1088,408]{0,1:T(8,128)}, f32[1088,136]{0,1:T(8,128)}, f32[1088,544]{0,1:T(8,128)})) %all-reduce.18.cloned.1.call-update) | async-done | bytes 4734992
  2010.9 76.0 %reduce-scatter.28.cloned.1.call-done = f32[272,136]{1,0:T(8,128)} async-done(((f32[4352,136]{1,0:T(8,128)}), f32[272,136]{1,0:T(8,128)}) %reduce-scatter.28.cloned.1.call-update) | async-done | bytes 147984
  (567 shorter events, 392.1 us)
Async XLA Ops:
  20.1 84.1 %all-gather.67.cloned.1.call-start = ((), (), s32[]{:S(2)}) async-start(), calls=%async_computation.15 | async-start | bytes 8146944 | tf_op jit(solution)/shard_map/while/body/eval_jaxpr/all_gather | solution.py:35
  35.4 165.6 %all-gather.73.cloned.1.call-start = ((), (), s32[]{:S(2)}) async-start(), calls=%async_computation.18 | async-start | bytes 2820096 | tf_op jit(solution)/shard_map/while/body/eval_jaxpr/all_gather | solution.py:36
  49.2 154.9 %all-gather.71.cloned.1.call-start = ((), (), s32[]{:S(2)}) async-start(), calls=%async_computation.17 | async-start | bytes 2506752 | tf_op jit(solution)/shard_map/while/body/eval_jaxpr/all_gather | solution.py:103
  121.0 91.8 %all-gather.69.cloned.1.call-start = ((), (), s32[]{:S(2)}) async-start(), calls=%async_computation.16 | async-start | bytes 2506752 | tf_op jit(solution)/shard_map/while/body/eval_jaxpr/all_gather | solution.py:104
  132.7 71.4 %copy-start.10 = (bf16[128,1088]{0,1:T(8,128)(2,1)}, bf16[128,1088]{0,1:T(8,128)(2,1)S(1)}, u32[]{:S(2)}) copy-start(bf16[128,1088]{0,1:T(8,128)(2,1)S(1)} %get-tuple-element.1277) | copy-start | bytes 835588 | tf_op jit(solution)/shard_map/while
  132.8 161.8 %all-gather.77.cloned.1.call-start = ((), (), s32[]{:S(2)}) async-start(), calls=%async_computation.20 | async-start | bytes 10653696 | tf_op jit(solution)/shard_map/while/body/eval_jaxpr/all_gather | solution.py:37
  147.9 227.1 %all-gather.75.cloned.1.call-start = ((), (), s32[]{:S(2)}) async-start(), calls=%async_computation.19 | async-start | bytes 10653696 | tf_op jit(solution)/shard_map/while/body/eval_jaxpr/all_gather | solution.py:38
  162.6 280.3 %all-gather.85.cloned.1.call-start = ((), (), s32[]{:S(2)}) async-start(), calls=%async_computation.24 | async-start | bytes 2820096 | tf_op jit(solution)/shard_map/while/body/eval_jaxpr/all_gather | solution.py:36
  220.4 84.6 %copy-start.65 = (f32[128]{0:T(128)}, f32[128]{0:T(128)S(1)}, u32[]{:S(2)}) copy-start(f32[128]{0:T(128)S(1)} %multiply_reduce_fusion.7) | copy-start | bytes 1540 | tf_op jit(solution)/shard_map/while
  220.4 84.6 %copy-start.51 = (f32[128]{0:T(128)}, f32[128]{0:T(128)S(1)}, u32[]{:S(2)}) copy-start(f32[128]{0:T(128)S(1)} %fusion.167) | copy-start | bytes 1540 | tf_op jit(solution)/shard_map/while
  220.4 84.6 %copy-start.31 = (f32[1088]{0:T(1024)S(1)}, f32[1088]{0:T(1024)}, u32[]{:S(2)}) copy-start(f32[1088]{0:T(1024)} %get-tuple-element.1281) | copy-start | bytes 13060 | tf_op jit(solution)/shard_map/while
  220.4 84.6 %copy-start.38 = (f32[4352]{0:T(1024)S(1)}, f32[4352]{0:T(1024)}, u32[]{:S(2)}) copy-start(f32[4352]{0:T(1024)} %add.763) | copy-start | bytes 52228 | tf_op jit(solution)/shard_map/while
  305.1 70.0 %copy-start.55 = (f32[1088]{0:T(1024)S(1)}, f32[1088]{0:T(1024)}, u32[]{:S(2)}) copy-start(f32[1088]{0:T(1024)} %get-tuple-element.1270) | copy-start | bytes 13060 | tf_op jit(solution)/shard_map/while
  312.7 70.5 %copy-start.14 = (f32[128,4352]{1,0:T(8,128)}, f32[128,4352]{1,0:T(8,128)S(1)}, u32[]{:S(2)}) copy-start(f32[128,4352]{1,0:T(8,128)S(1)} %get-tuple-element.1284) | copy-start | bytes 6684676 | tf_op jit(solution)/shard_map/while
  397.2 125.9 %all-gather.81.cloned.1.call-start = ((), (), s32[]{:S(2)}) async-start(), calls=%async_computation.22 | async-start | bytes 10653696 | tf_op jit(solution)/shard_map/while/body/eval_jaxpr/all_gather | solution.py:37
  412.2 191.5 %all-gather.79.cloned.1.call-start = ((), (), s32[]{:S(2)}) async-start(), calls=%async_computation.21 | async-start | bytes 10653696 | tf_op jit(solution)/shard_map/while/body/eval_jaxpr/all_gather | solution.py:38
  426.8 246.6 %all-gather.83.cloned.1.call-start = ((), (), s32[]{:S(2)}) async-start(), calls=%async_computation.23 | async-start | bytes 8146944 | tf_op jit(solution)/shard_map/while/body/eval_jaxpr/all_gather | solution.py:35
  441.8 272.1 %reduce-scatter.38.cloned.1.call-start = ((), (), s32[]{:S(2)}) async-start(), calls=%async_computation.26 | async-start | bytes 5013504 | tf_op jit(solution)/shard_map/while/body/eval_jaxpr/reduce_scatter | solution.py:171
  447.5 156.3 %copy-start.7 = (bf16[2,128,1088]{1,2,0:T(8,128)(2,1)S(1)}, bf16[2,128,1088]{1,2,0:T(8,128)(2,1)}, u32[]{:S(2)}) copy-start(bf16[2,128,1088]{1,2,0:T(8,128)(2,1)} %get-tuple-element.1404) | copy-start | bytes 1671172 | tf_op jit(solution)/shard_map/while
  447.5 156.3 %copy-start.15 = (f32[128,4352]{1,0:T(8,128)S(1)}, f32[128,4352]{1,0:T(8,128)}, u32[]{:S(2)}) copy-start(f32[128,4352]{1,0:T(8,128)} %copy-done.14) | copy-start | bytes 6684676 | tf_op jit(solution)/shard_map/while
  626.0 127.8 %reduce-scatter.36.cloned.1.call-start = ((), (), s32[]{:S(2)}) async-start(), calls=%async_computation.25 | async-start | bytes 5013504 | tf_op jit(solution)/shard_map/while/body/eval_jaxpr/reduce_scatter | solution.py:172
  763.1 83.2 %all-gather.67.cloned.1.call-start = ((), (), s32[]{:S(2)}) async-start(), calls=%async_computation.15 | async-start | bytes 8146944 | tf_op jit(solution)/shard_map/while/body/eval_jaxpr/all_gather | solution.py:35
  778.5 164.3 %all-gather.73.cloned.1.call-start = ((), (), s32[]{:S(2)}) async-start(), calls=%async_computation.18 | async-start | bytes 2820096 | tf_op jit(solution)/shard_map/while/body/eval_jaxpr/all_gather | solution.py:36
  792.3 153.6 %all-gather.71.cloned.1.call-start = ((), (), s32[]{:S(2)}) async-start(), calls=%async_computation.17 | async-start | bytes 2506752 | tf_op jit(solution)/shard_map/while/body/eval_jaxpr/all_gather | solution.py:103
  863.1 91.5 %all-gather.69.cloned.1.call-start = ((), (), s32[]{:S(2)}) async-start(), calls=%async_computation.16 | async-start | bytes 2506752 | tf_op jit(solution)/shard_map/while/body/eval_jaxpr/all_gather | solution.py:104
  874.8 71.0 %copy-start.10 = (bf16[128,1088]{0,1:T(8,128)(2,1)}, bf16[128,1088]{0,1:T(8,128)(2,1)S(1)}, u32[]{:S(2)}) copy-start(bf16[128,1088]{0,1:T(8,128)(2,1)S(1)} %get-tuple-element.1277) | copy-start | bytes 835588 | tf_op jit(solution)/shard_map/while
  874.8 161.5 %all-gather.77.cloned.1.call-start = ((), (), s32[]{:S(2)}) async-start(), calls=%async_computation.20 | async-start | bytes 10653696 | tf_op jit(solution)/shard_map/while/body/eval_jaxpr/all_gather | solution.py:37
  890.0 226.8 %all-gather.75.cloned.1.call-start = ((), (), s32[]{:S(2)}) async-start(), calls=%async_computation.19 | async-start | bytes 10653696 | tf_op jit(solution)/shard_map/while/body/eval_jaxpr/all_gather | solution.py:38
  904.7 280.0 %all-gather.85.cloned.1.call-start = ((), (), s32[]{:S(2)}) async-start(), calls=%async_computation.24 | async-start | bytes 2820096 | tf_op jit(solution)/shard_map/while/body/eval_jaxpr/all_gather | solution.py:36
  962.2 84.9 %copy-start.65 = (f32[128]{0:T(128)}, f32[128]{0:T(128)S(1)}, u32[]{:S(2)}) copy-start(f32[128]{0:T(128)S(1)} %multiply_reduce_fusion.7) | copy-start | bytes 1540 | tf_op jit(solution)/shard_map/while
  962.2 84.8 %copy-start.51 = (f32[128]{0:T(128)}, f32[128]{0:T(128)S(1)}, u32[]{:S(2)}) copy-start(f32[128]{0:T(128)S(1)} %fusion.167) | copy-start | bytes 1540 | tf_op jit(solution)/shard_map/while
  962.2 84.8 %copy-start.31 = (f32[1088]{0:T(1024)S(1)}, f32[1088]{0:T(1024)}, u32[]{:S(2)}) copy-start(f32[1088]{0:T(1024)} %get-tuple-element.1281) | copy-start | bytes 13060 | tf_op jit(solution)/shard_map/while
  962.2 84.8 %copy-start.38 = (f32[4352]{0:T(1024)S(1)}, f32[4352]{0:T(1024)}, u32[]{:S(2)}) copy-start(f32[4352]{0:T(1024)} %add.763) | copy-start | bytes 52228 | tf_op jit(solution)/shard_map/while
  1054.6 70.3 %copy-start.14 = (f32[128,4352]{1,0:T(8,128)}, f32[128,4352]{1,0:T(8,128)S(1)}, u32[]{:S(2)}) copy-start(f32[128,4352]{1,0:T(8,128)S(1)} %get-tuple-element.1284) | copy-start | bytes 6684676 | tf_op jit(solution)/shard_map/while
  1139.0 125.7 %all-gather.81.cloned.1.call-start = ((), (), s32[]{:S(2)}) async-start(), calls=%async_computation.22 | async-start | bytes 10653696 | tf_op jit(solution)/shard_map/while/body/eval_jaxpr/all_gather | solution.py:37
  1153.9 191.4 %all-gather.79.cloned.1.call-start = ((), (), s32[]{:S(2)}) async-start(), calls=%async_computation.21 | async-start | bytes 10653696 | tf_op jit(solution)/shard_map/while/body/eval_jaxpr/all_gather | solution.py:38
  1168.6 246.6 %all-gather.83.cloned.1.call-start = ((), (), s32[]{:S(2)}) async-start(), calls=%async_computation.23 | async-start | bytes 8146944 | tf_op jit(solution)/shard_map/while/body/eval_jaxpr/all_gather | solution.py:35
  1183.6 272.1 %reduce-scatter.38.cloned.1.call-start = ((), (), s32[]{:S(2)}) async-start(), calls=%async_computation.26 | async-start | bytes 5013504 | tf_op jit(solution)/shard_map/while/body/eval_jaxpr/reduce_scatter | solution.py:171
  1189.2 156.1 %copy-start.7 = (bf16[2,128,1088]{1,2,0:T(8,128)(2,1)S(1)}, bf16[2,128,1088]{1,2,0:T(8,128)(2,1)}, u32[]{:S(2)}) copy-start(bf16[2,128,1088]{1,2,0:T(8,128)(2,1)} %get-tuple-element.1404) | copy-start | bytes 1671172 | tf_op jit(solution)/shard_map/while
  1189.2 156.1 %copy-start.15 = (f32[128,4352]{1,0:T(8,128)S(1)}, f32[128,4352]{1,0:T(8,128)}, u32[]{:S(2)}) copy-start(f32[128,4352]{1,0:T(8,128)} %copy-done.14) | copy-start | bytes 6684676 | tf_op jit(solution)/shard_map/while
  1367.6 127.9 %reduce-scatter.36.cloned.1.call-start = ((), (), s32[]{:S(2)}) async-start(), calls=%async_computation.25 | async-start | bytes 5013504 | tf_op jit(solution)/shard_map/while/body/eval_jaxpr/reduce_scatter | solution.py:172
  1512.2 42.9 %reduce-scatter.34.cloned.1.call-start = ((), (), s32[]{:S(2)}) async-start(), calls=%async_computation.13 | async-start | bytes 5640192
  1516.6 124.4 %reduce-scatter.32.cloned.1.call-start = ((), (), s32[]{:S(2)}) async-start(), calls=%async_computation.12 | async-start | bytes 16920576
  1526.0 224.1 %reduce-scatter.24.cloned.1.call-start = ((), (), s32[]{:S(2)}) async-start(), calls=%async_computation.8 | async-start | bytes 22560768 | tf_op jit(solution)/shard_map/reduce_scatter | solution.py:273
  1537.3 317.1 %reduce-scatter.26.cloned.1.call-start = ((), (), s32[]{:S(2)}) async-start(), calls=%async_computation.9 | async-start | bytes 21307392 | tf_op jit(solution)/shard_map/reduce_scatter | solution.py:274
  1548.1 344.0 %reduce-scatter.30.cloned.1.call-start = ((), (), s32[]{:S(2)}) async-start(), calls=%async_computation.11 | async-start | bytes 2506752
  1550.5 454.8 %all-reduce.18.cloned.1.call-start = ((), (), s32[]{:S(2)}) async-start(), calls=%async_computation.14 | async-start | bytes 10027008
  1750.2 336.8 %reduce-scatter.28.cloned.1.call-start = ((), (), s32[]{:S(2)}) async-start(), calls=%async_computation.10 | async-start | bytes 4734976
  (123 other events, 1450.6 us)
Sparse Core Ops, SparseCore 0:
  35.5 68.6 all-gather.66
  107.2 46.0 all-gather.72
  155.2 27.0 all-gather.70
  183.9 28.7 all-gather.68
  214.9 79.5 all-gather.76
  296.9 78.1 all-gather.74
  397.3 45.5 all-gather.84
  445.3 77.7 all-gather.80
  525.5 78.1 all-gather.78
  606.0 67.3 all-gather.82
  676.0 37.8 reduce-scatter.37
  716.3 37.4 reduce-scatter.35
  778.6 67.6 all-gather.66
  849.2 46.0 all-gather.72
  896.9 27.0 all-gather.70
  925.6 28.7 all-gather.68
  956.7 79.5 all-gather.76
  1038.6 78.1 all-gather.74
  1139.1 45.5 all-gather.84
  1186.9 77.7 all-gather.80
  1267.1 78.1 all-gather.78
  1347.8 67.3 all-gather.82
  1417.8 37.8 reduce-scatter.37
  1458.1 37.4 reduce-scatter.35
Sparse Core Ops, SparseCore 1:
  1516.7 38.3 reduce-scatter.33
  1557.6 83.4 reduce-scatter.31
  1643.4 106.7 reduce-scatter.23
  1752.6 101.7 reduce-scatter.25
  1856.8 33.6 reduce-scatter.29
  1894.8 110.5 all-reduce.17
  2008.9 78.0 reduce-scatter.27
where the time goes:
time: 2100 us
  waiting for transfers between devices  1250 us (60%)
  blocking collectives  449 us (21%)
  local copies, waits for them, and re-layouts  170 us (8%)
  matrix products  167 us (8%)
  other arithmetic  25.6 us (1%)
    all_gather x4, waiting for transfers between devices, collect(): lax.all_gather(by_column[2], 'batch', axis=0, tiled=True)  299 us
    all_gather x4, waiting for transfers between devices, collect(): lax.all_gather(by_column[3], 'batch', axis=0, tiled=True)  265 us
    unnamed x12, waiting for transfers between devices  202 us
    all_gather x4, waiting for transfers between devices, collect(): lax.all_gather(by_column[0], 'batch', axis=0, tiled=True)  142 us
    while x292, local copies, waits for them, and re-layouts  132 us
    reduce_scatter x1, waiting for transfers between devices, per_device(): lax.psum_scatter(up_terms, 'seq', scatter_dimension=1, tiled=True)  109 us
    reduce_scatter x1, waiting for transfers between devices, per_device(): lax.psum_scatter(down_terms, 'seq', scatter_dimension=1, tiled=True)  104 us
    reduce_scatter x2, waiting for transfers between devices, micro_step(): lax.psum_scatter(value_terms, 'seq', scatter_dimension=0, tiled=True)  77.6 us
  transfers between devices with their start and end apart: 31, of which 24 were waited for; matrix products, arithmetic and copies ran while one was open for 14% of the time, Pallas kernels for 0%

commit v1 on v0

v1 whole, which is shorter than its diff:
```python
import jax
import jax.numpy as jnp
from jax import lax
from jax.sharding import PartitionSpec as P

D = 1088
HEADS = 17
HEAD_DIM = 64
FF = 4352
F32 = jnp.float32
BF16 = jnp.bfloat16
Z_GROUPS = [[4 * y + z for z in range(4)] for y in range(4)]
Y_GROUPS = [[4 * y + z for y in range(4)] for z in range(4)]


def normalize(values):
    center = values - jnp.mean(values, axis=-1, keepdims=True)
    spread = jnp.mean(center * center, axis=-1, keepdims=True)
    scale = lax.rsqrt(spread + 1e-05)
    return center * scale, scale


def norm_pull(grad, gain, unit, scale):
    scaled = grad * gain
    return scale * (
        scaled
        - jnp.mean(scaled, axis=-1, keepdims=True)
        - unit * jnp.mean(scaled * unit, axis=-1, keepdims=True)
    )


def gelu_tanh(values):
    return jax.nn.gelu(values, approximate=True)


def dot(left, right):
    return jnp.dot(left, right, preferred_element_type=F32)


def per_device(
    inputs, out_grad, segment_ids, qkv_weight, out_weight, up_weight, down_weight,
    norm_gains, norm_shifts, qv_bias, proj_bias, up_bias,
):
    seqs, rows, _ = inputs.shape
    tokens = seqs * rows
    first_row = lax.axis_index("seq") * rows
    scale = HEAD_DIM ** (-0.5)

    vec = jnp.concatenate(
        [norm_gains, norm_shifts, qv_bias, proj_bias, up_bias.reshape(4, 136)], axis=0
    )
    vec = lax.all_gather(vec, "seq", axis=0).astype(F32)
    pairs = vec[:, :8].transpose(1, 0, 2).reshape(8, D)
    gains, shifts, qv_rows, proj_rows = pairs[0:2], pairs[2:4], pairs[4:6], pairs[6:8]
    up_row = vec[:, 8:].reshape(FF)
    documents = lax.all_gather(segment_ids, "seq", axis=1, tiled=True)

    blob_a = jnp.concatenate([qkv_weight, out_weight, up_weight], axis=1)
    blob_b = down_weight.T
    blob_a = lax.all_gather(blob_a, "batch", axis=0, tiled=True)
    blob_b = lax.all_gather(blob_b, "batch", axis=1, tiled=True)
    whole_a = lax.all_gather(blob_a, "seq", axis=0)
    whole_b = lax.all_gather(blob_b, "seq", axis=0, tiled=True)
    w_qkv, w_out, w_up = whole_a[:, :, :408], whole_a[:, :, 408:544], whole_a[:, :, 544:]

    hidden = inputs.reshape(tokens, D).astype(F32)
    top_grad = out_grad.reshape(tokens, D)
    cotangent = top_grad.astype(F32)
    unit_one, scale_one = normalize(hidden)
    normed = (unit_one * gains[0] + shifts[0]).astype(BF16)
    projected = jnp.einsum("tk,skn->tsn", normed, w_qkv, preferred_element_type=F32).reshape(
        tokens, 3 * D
    )
    queries = (projected[:, :D] + qv_rows[0]).astype(BF16)
    key_rows = projected[:, D : 2 * D].astype(BF16)
    value_rows = (projected[:, 2 * D :] + qv_rows[1]).astype(BF16)

    key_value = jnp.concatenate([key_rows, value_rows], axis=1).reshape(seqs, rows, 2 * D)
    key_value = lax.all_gather(key_value, "seq", axis=1, tiled=True)
    total = key_value.shape[1]
    key_all = key_value[:, :, :D].reshape(seqs, total, HEADS, HEAD_DIM)
    value_all = key_value[:, :, D:].reshape(seqs, total, HEADS, HEAD_DIM)
    query_heads = queries.reshape(seqs, rows, HEADS, HEAD_DIM)
    query_docs = lax.dynamic_slice_in_dim(documents, first_row, rows, axis=1)
    allowed = (query_docs[:, :, None] == documents[:, None, :]) & (
        jnp.arange(total)[None, None, :] <= (first_row + jnp.arange(rows))[None, :, None]
    )
    scores = (
        jnp.einsum("bqhd,bkhd->bhqk", query_heads, key_all, preferred_element_type=F32) * scale
    )
    scores = jnp.where(allowed[:, None], scores, -1e30)
    peak = jnp.max(scores, axis=-1, keepdims=True)
    powers = jnp.exp(scores - peak)
    probs = powers / jnp.sum(powers, axis=-1, keepdims=True)
    soft_low = probs.astype(BF16)
    attended = (
        jnp.einsum("bhqk,bkhd->bqhd", soft_low, value_all, preferred_element_type=F32)
        .reshape(tokens, D)
        .astype(BF16)
    )
    branch = jnp.einsum("tk,skn->tsn", attended, w_out, preferred_element_type=F32)
    middle = hidden + branch.reshape(tokens, D) + proj_rows[0]
    unit_two, scale_two = normalize(middle)
    normed_two = (unit_two * gains[1] + shifts[1]).astype(BF16)
    inner_pre = (
        jnp.einsum("tk,skn->tsn", normed_two, w_up, preferred_element_type=F32).reshape(tokens, FF)
        + up_row
    )
    active, gelu_pull = jax.vjp(gelu_tanh, inner_pre)
    active = active.astype(BF16)
    layer_out = (
        middle
        + jnp.einsum("tf,df->td", active, whole_b, preferred_element_type=F32)
        + proj_rows[1]
    ).astype(BF16)

    down_in = dot(top_grad, whole_b)
    inner_grad = gelu_pull(down_in)[0].astype(BF16)
    inner_blocks = inner_grad.reshape(tokens, 8, 544)
    normed_two_grad = jnp.einsum("tsn,skn->tk", inner_blocks, w_up, preferred_element_type=F32)
    middle_grad = cotangent + norm_pull(normed_two_grad, gains[1], unit_two, scale_two)
    branch_grad = middle_grad.astype(BF16)
    branch_blocks = branch_grad.reshape(tokens, 8, 136)
    attended_grad = jnp.einsum(
        "tsn,skn->tk", branch_blocks, w_out, preferred_element_type=F32
    ).astype(BF16)
    attended_heads = attended_grad.reshape(seqs, rows, HEADS, HEAD_DIM)
    prob_grad = jnp.einsum("bqhd,bkhd->bhqk", attended_heads, value_all, preferred_element_type=F32)
    row_inner = jnp.sum(probs * prob_grad, axis=-1, keepdims=True)
    score_grad = (probs * (prob_grad - row_inner)).astype(BF16)
    query_grad = (
        jnp.einsum("bhqk,bkhd->bqhd", score_grad, key_all, preferred_element_type=F32) * scale
    ).reshape(tokens, D)
    key_terms = (
        jnp.einsum("bhqk,bqhd->bkhd", score_grad, query_heads, preferred_element_type=F32) * scale
    ).reshape(seqs, total, D)
    value_terms = jnp.einsum(
        "bhqk,bqhd->bkhd", soft_low, attended_heads, preferred_element_type=F32
    ).reshape(seqs, total, D)
    terms = jnp.concatenate([key_terms, value_terms], axis=2)
    terms = lax.psum_scatter(terms, "seq", scatter_dimension=1, tiled=True)
    qkv_grad = jnp.concatenate(
        [query_grad.astype(BF16), terms.reshape(tokens, 2 * D).astype(BF16)], axis=1
    )
    qkv_blocks = qkv_grad.reshape(tokens, 8, 408)
    normed_grad = jnp.einsum("tsn,skn->tk", qkv_blocks, w_qkv, preferred_element_type=F32)
    input_grad = middle_grad + norm_pull(normed_grad, gains[0], unit_one, scale_one)

    d_qkv = jnp.einsum("tk,tsn->skn", normed, qkv_blocks, preferred_element_type=F32)
    d_out = jnp.einsum("tk,tsn->skn", attended, branch_blocks, preferred_element_type=F32)
    d_up = jnp.einsum("tk,tsn->skn", normed_two, inner_blocks, preferred_element_type=F32)
    d_a = jnp.concatenate([d_qkv.astype(BF16), d_out.astype(BF16), d_up.astype(BF16)], axis=2)
    d_b = jnp.einsum("td,tf->df", top_grad, active, preferred_element_type=F32).astype(BF16)
    d_a = lax.psum_scatter(d_a, "seq", scatter_dimension=0)
    d_b = lax.psum_scatter(d_b, "seq", scatter_dimension=0, tiled=True)
    d_a = lax.psum_scatter(d_a, "batch", scatter_dimension=0, tiled=True).astype(F32)
    d_b = d_b.reshape(136, 16, 272).transpose(1, 0, 2)
    d_b = lax.psum_scatter(d_b, "batch", scatter_dimension=0).astype(F32)

    def column_sum(values):
        return jnp.sum(values, axis=0, dtype=F32)

    sums = jnp.stack(
        [
            column_sum(normed_grad * unit_one),
            column_sum(normed_two_grad * unit_two),
            column_sum(normed_grad),
            column_sum(normed_two_grad),
            column_sum(qkv_grad[:, :D]),
            column_sum(qkv_grad[:, 2 * D :]),
            column_sum(branch_grad),
            column_sum(top_grad),
        ]
    ).reshape(8, 8, 136)
    sums = jnp.concatenate(
        [sums.transpose(1, 0, 2), column_sum(inner_grad).reshape(8, 4, 136)], axis=1
    )
    sums = lax.psum_scatter(sums, "seq", scatter_dimension=0)
    sums = lax.psum(sums, "batch")
    return (
        layer_out.reshape(seqs, rows, D),
        input_grad.reshape(seqs, rows, D),
        d_a[:, :408],
        d_a[:, 408:544],
        d_a[:, 544:],
        d_b.T,
        sums[0:2],
        sums[2:4],
        sums[4:6],
        sums[6:8],
        sums[8:12].reshape(1, 544),
    )


def solution(mesh):
    tokens = P("batch", "seq", None)
    matrix = P("batch", "seq")
    vector = P(None, "seq")
    return jax.shard_map(
        per_device,
        mesh=mesh,
        in_specs=(tokens, tokens, matrix, matrix, matrix, matrix, matrix) + (vector,) * 5,
        out_specs=(tokens, tokens, matrix, matrix, matrix, matrix) + (vector,) * 5,
        check_vma=False,
    )
```

time: 2100 us -> 972 us (0.46)
  waiting for transfers between devices: 1250 us -> 525 us
  blocking collectives: 449 us -> 98.3 us
  local copies, waits for them, and re-layouts: 170 us -> 115 us
  other arithmetic: 25.6 us -> 55.5 us
    all_gather x20 -> x5, waiting for transfers between devices: 709 us -> 216 us  [the longest x1 80.8 us: per_device(): whole_a = lax.all_gather(blob_a, 'seq', axis=0)]
    all_gather x24 -> x1, blocking collectives: 286 us -> 13 us  [per_device(): vec = lax.all_gather(vec, 'seq', axis=0).astype(F32)]
    while x293 -> x0, local copies, waits for them, and re-layouts: 135 us -> none
    reduce_scatter x6 -> x4, waiting for transfers between devices: 343 us -> 221 us  [the longest x1 87.6 us: per_device(): d_a = lax.psum_scatter(d_a, 'seq', scatter_dimension=0)]
    unnamed x12 -> x13, waiting for transfers between devices: 202 us -> 88.4 us
    while x2 -> x0, blocking collectives: 51 us -> none
    reshape x8 -> x12, local copies, waits for them, and re-layouts: 0.04 us -> 37.6 us  [the longest x1 9.52 us: per_device(): value_terms = jnp.einsum('bhqk,bqhd->bkhd', soft_low, attended_heads, pre...]
    concatenate x0 -> x5, other arithmetic: none -> 29.8 us  [the longest x1 14 us: per_device(): jnp.concatenate([d_qkv.astype(BF16), d_out.astype(BF16), d_up.astype(BF16...]
  transfers between devices with their start and end apart: 31 -> 11, of which waited for: 24 -> 10; matrix products, arithmetic and copies ran while one was open for 14% -> 21% of each run, Pallas kernels for 0% -> 0%
where the time goes in v1:
time: 972 us; the launch traced here: 962 us
  waiting for transfers between devices  525 us (54%)
  matrix products  152 us (16%)
  local copies, waits for them, and re-layouts  115 us (12%)
  blocking collectives  98.3 us (10%)
  other arithmetic  55.5 us (6%)
  between operations  15.6 us (2%)
    unnamed x13, waiting for transfers between devices  88.4 us
    reduce_scatter x1, waiting for transfers between devices, per_device(): d_a = lax.psum_scatter(d_a, 'seq', scatter_dimension=0)  87.6 us
    all_gather x1, waiting for transfers between devices, per_device(): whole_a = lax.all_gather(blob_a, 'seq', axis=0)  80.8 us
    psum x1, blocking collectives, per_device(): sums = lax.psum(sums, 'batch')  74.7 us
    reduce_scatter x1, waiting for transfers between devices, per_device(): terms = lax.psum_scatter(terms, 'seq', scatter_dimension=1, tiled=True)  71.7 us
    all_gather x1, waiting for transfers between devices, per_device(): key_value = lax.all_gather(key_value, 'seq', axis=1, tiled=True)  64.9 us
    all_gather x1, waiting for transfers between devices, per_device(): blob_a = lax.all_gather(blob_a, 'batch', axis=0, tiled=True)  49.9 us
    unnamed x61, local copies, waits for them, and re-layouts  44.8 us
  transfers between devices with their start and end apart: 11, of which 10 were waited for; matrix products, arithmetic and copies ran while one was open for 21% of the time, Pallas kernels for 0%

profile of v1, /device:TPU:0, one launch (start us, length us, event | category | flops | bytes accessed | tf_op | source)
XLA Modules:
  0.0 962.0 jit_solution(7745827733685584349)
XLA Ops:
  10.0 49.9 %all-gather.17.cloned.1.call-done = bf16[16,68,1088]{2,1,0:T(8,128)(2,1)} async-done(((bf16[1,68,1088]{2,1,0:T(8,128)(2,1)}), bf16[16,68,1088]{2,1,0:T(8,128)(2,1)}) %all-gather.17.cloned.1.call-update) | async-done | bytes 2367504 | tf_op jit(solution)/shard_map/all_gather | solution.py:60
  59.8 4.4 reshape.301
  65.2 13.0 %all-gather.2 = bf16[8,12,136]{2,1,0:T(8,128)(2,1)S(1)} all-gather(bf16[1,12,136]{2,1,0:T(8,128)(2,1)S(1)} %bitcast.211), channel_id=2, replica_groups=mesh['batch'=16,'seq'=8] {'seq'}, dimensions={0}, use_global_device_ids=true | all-gather | bytes 29376 | tf_op jit(solution)/shard_map/all_gather | solution.py:52
  81.5 80.8 %all-gather.15.cloned.1.call-done = bf16[8704,1088]{1,0:T(8,128)(2,1)} async-done(((bf16[1088,1088]{1,0:T(8,128)(2,1)}), bf16[8704,1088]{1,0:T(8,128)(2,1)}) %all-gather.15.cloned.1.call-update) | async-done | bytes 18939920 | tf_op jit(solution)/shard_map/all_gather | solution.py:62
  162.3 7.6 slice.139
  169.8 11.4 %copy.101 = bf16[8,1088,408]{1,2,0:T(8,128)(2,1)} copy(bf16[8,1088,408]{2,1,0:T(8,128)(2,1)} %slice.139) | data formatting | bytes 14204928
  181.3 5.6 fusion.106
  189.4 20.2 %all-gather.19.cloned.1.call-done = bf16[16,272,136]{1,2,0:T(8,128)(2,1)} async-done(((bf16[1,272,136]{1,2,0:T(8,128)(2,1)}), bf16[16,272,136]{1,2,0:T(8,128)(2,1)}) %all-gather.19.cloned.1.call-update) | async-done | bytes 1183760 | tf_op jit(solution)/shard_map/all_gather | solution.py:61
  214.7 10.5 %all_gather.33 = s32[2,1024]{1,0:T(2,128)S(1)} all-gather(s32[2,128]{1,0:T(2,128)S(1)} %copy-done.23), channel_id=1, replica_groups=mesh['batch'=16,'seq'=8] {'seq'}, dimensions={1}, use_global_device_ids=true | all-gather | bytes 9216 | tf_op jit(solution)/shard_map/all_gather | solution.py:56
  225.6 7.3 slice.135
  232.8 6.3 copy.100
  239.3 64.9 %all-gather.11.cloned.1.call-done = bf16[2,1024,2176]{1,0,2:T(2,128)(2,1)} async-done(((bf16[2,128,2176]{1,0,2:T(2,128)(2,1)}), bf16[2,1024,2176]{1,0,2:T(2,128)(2,1)}) %all-gather.11.cloned.1.call-update) | async-done | bytes 8912912 | tf_op jit(solution)/shard_map/all_gather | solution.py:79
  304.2 7.6 fusion.98
  311.8 3.4 copy.72
  315.2 3.7 copy.73
  318.9 12.3 %fusion.100 = (f32[2,17,128]{2,1,0:T(8,128)S(1)}, f32[2,17,128,1024]{3,2,1,0:T(8,128)}) fusion(pred[2,128,1024]{2,1,0:T(8,128)(4,1)S(1)} %compare_and_fusion, bf16[2,1024,17,64]{1,3,2,0:T(8,128)(2,1)} %bitcast.175, bf16[2,128,17,64]{1,0,3,2:T(2,128)(2,1)S(1)} %reshape.278), kind=kOutput, calls=%fused_computation.158 | convolution fusion | flops 588252160 | bytes 23118848 | tf_op jit(solution)/shard_map/sub | solution.py:93
  331.2 11.3 %fusion.52 = bf16[2,128,17,64]{1,3,2,0:T(8,128)(2,1)S(1)} fusion(bf16[2,1024,17,64]{1,3,2,0:T(8,128)(2,1)} %bitcast.193, f32[2,17,128,1024]{3,2,1,0:T(8,128)} %get-tuple-element.75, f32[2,17,128]{2,1,0:T(8,128)S(1)} %get-tuple-element.74), kind=kOutput, calls=%fused_computation.74 | convolution fusion | flops 579616768 | bytes 22856704 | tf_op jit(solution)/shard_map/bhqk,bkhd->bqhd/dot_general | solution.py:97
  344.2 16.7 %fusion.26 = (bf16[256,8,544]{0,2,1:T(8,128)(2,1)}, f32[256,8,544]{0,2,1:T(8,128)}) fusion(f32[8,544]{1,0:T(8,128)S(1)} %add.181, bf16[8,1088,1088]{2,1,0:T(8,128)(2,1)} %bitcast.179, f32[256,1088]{0,1:T(8,128)S(1)} %get-tuple-element.77, f32[1088]{0:T(1024)S(1)} %add.167, f32[1088]{0:T(1024)S(1)} %mul.204, f32[256]{0:T(256)S(1)} %add_rsqrt_fusion, ...), kind=kOutput, calls=%fused_computation.39 | convolution fusion | flops 2436841472 | bytes 18968064 | tf_op jit(solution)/shard_map/tk,skn->tsn/dot_general | solution.py:106
  360.9 5.8 copy.78
  366.7 11.6 %convert_reduce_fusion = (f32[4352]{0:T(1024)S(1)}, bf16[256,4352]{1,0:T(8,128)(2,1)}) fusion(f32[256,4352]{1,0:T(8,128)} %copy.78, f32[4352]{0:T(1024)S(1)} %add.170, bf16[1088,4352]{1,0:T(8,128)(2,1)} %all-gather.13.cloned.1.call-done, bf16[2,128,1088]{1,2,0:T(8,128)(2,1)S(1)} %copy-done.2), kind=kOutput, calls=%fused_computation.40 | convolution fusion | flops 2449927936 | bytes 16746496 | tf_op jit(solution)/shard_map/dot_general | solution.py:37
  378.3 4.5 copy.81
  382.8 10.6 %multiply_reduce_fusion.1 = (f32[1088]{0:T(1024)S(1)}, f32[256]{0:T(256)S(1)}, f32[256]{0:T(256)S(1)}, f32[1088]{0:T(1024)S(1)}, f32[256,1088]{0,1:T(8,128)S(1)}) fusion(f32[256,1088]{0,1:T(8,128)S(1)} %get-tuple-element.77, f32[256]{0:T(256)S(1)} %add_rsqrt_fusion, f32[256]{0:T(256)S(1)} %broadcast_multiply_fusion.5, f32[1088]{0:T(1024)S(1)} %mul.204, ...), kind=kOutput, calls=%fused_computation.93 | convolution fusion | flops 2426811904 | bytes 15614720 | tf_op jit(solution)/shard_map/tsn,skn->tk/dot_general | solution.py:120
  394.9 6.7 fusion.37
  404.1 11.2 %fusion.27 = f32[2,17,64,1024]{3,2,1,0:T(8,128)} fusion(bf16[2,128,17,64]{1,0,3,2:T(2,128)(2,1)} %reshape.285, f32[2,17,128,1024]{3,2,1,0:T(8,128)} %get-tuple-element.75, f32[2,17,128]{2,1,0:T(8,128)S(1)} %get-tuple-element.74), kind=kOutput, calls=%fused_computation.43 | convolution fusion | flops 579338240 | bytes 27313152 | tf_op jit(solution)/shard_map/bhqk,bqhd->bkhd/dot_general | solution.py:137
  415.3 14.0 %multiply_reduce_fusion = (f32[2,17,128]{2,1,0:T(8,128)S(1)}, f32[2,17,128,1024]{3,2,1,0:T(8,128)}) fusion(f32[2,17,128,1024]{3,2,1,0:T(8,128)} %get-tuple-element.75, f32[2,17,128]{2,1,0:T(8,128)S(1)} %get-tuple-element.74, bf16[2,1024,17,64]{1,3,2,0:T(8,128)(2,1)} %bitcast.194, bf16[2,128,17,64]{1,0,3,2:T(2,128)(2,1)S(1)} %copy-done.12), kind=kOutput, calls=%fused_computation.5 | convolution fusion | flops 583790336 | bytes 40699904 | tf_op jit(solution)/shard_map/bqhd,bkhd->bhqk/dot_general | solution.py:128
  429.2 9.5 copy.87
  438.8 12.2 %multiply_convert_fusion = bf16[2,17,128,1024]{3,2,1,0:T(8,128)(2,1)S(1)} fusion(f32[2,17,128,1024]{3,2,1,0:T(8,128)} %get-tuple-element.80, f32[2,17,128]{2,1,0:T(8,128)S(1)} %get-tuple-element.79, f32[2,17,128,1024]{3,2,1,0:T(8,128)} %get-tuple-element.75, f32[2,17,128]{2,1,0:T(8,128)S(1)} %get-tuple-element.74), kind=kLoop, calls=%fused_computation.4 | loop fusion | flops 17825792 | bytes 44599296 | tf_op jit(solution)/shard_map/convert_element_type | solution.py:130
  450.9 5.6 broadcast_multiply_fusion
  457.3 9.4 copy.86
  466.7 13.3 %pad_maximum_fusion.1 = f32[2,1024,2176]{2,1,0:T(8,128)} fusion(f32[2,1024,1088]{2,1,0:T(8,128)} %copy.87, f32[2,1024,1088]{2,1,0:T(8,128)} %copy.86), kind=kLoop, calls=%fused_computation.3 | loop fusion | flops 4456448 | bytes 35651584 | tf_op jit(solution)/shard_map/concatenate | solution.py:140
  480.1 6.7 fusion.1
  487.3 9.0 convert_reduce_fusion.5
  500.4 5.9 fusion.4
  506.3 71.7 %reduce-scatter.9.cloned.1.call-done = f32[2,128,2176]{2,1,0:T(8,128)} async-done(((f32[2,1024,2176]{2,1,0:T(8,128)}), f32[2,128,2176]{2,1,0:T(8,128)}) %reduce-scatter.9.cloned.1.call-update) | async-done | bytes 2228240 | tf_op jit(solution)/shard_map/reduce_scatter | solution.py:141
  581.4 3.8 copy.89
  585.2 4.1 fusion.3
  589.3 14.0 %pad_maximum_fusion = bf16[8,1088,1088]{1,2,0:T(8,128)(2,1)} fusion(bf16[8,1088,544]{1,2,0:T(8,128)(2,1)} %fusion.4, bf16[8,1088,136]{1,2,0:T(8,128)(2,1)S(1)} %copy-done.1, bf16[8,1088,408]{1,2,0:T(8,128)(2,1)S(1)} %fusion.3), kind=kLoop, calls=%fused_computation.1 | loop fusion | flops 56819712 | bytes 37879808 | tf_op jit(solution)/shard_map/concatenate | solution.py:152
  603.4 34.3 %reduce-scatter.13.cloned.1.call-done = bf16[136,4352]{1,0:T(8,128)(2,1)} async-done(((bf16[1088,4352]{1,0:T(8,128)(2,1)}), bf16[136,4352]{1,0:T(8,128)(2,1)}) %reduce-scatter.13.cloned.1.call-update) | async-done | bytes 1183760 | tf_op jit(solution)/shard_map/reduce_scatter | solution.py:155
  637.7 4.3 reshape.290
  641.9 3.1 copy.165
  646.0 9.3 multiply_reduce_fusion.2
  659.4 87.6 %reduce-scatter.11.cloned.1.call-done = bf16[1,1088,1088]{1,2,0:T(8,128)(2,1)} async-done(((bf16[8,1088,1088]{1,2,0:T(8,128)(2,1)}), bf16[1,1088,1088]{1,2,0:T(8,128)(2,1)}) %reduce-scatter.11.cloned.1.call-update) | async-done | bytes 2367504 | tf_op jit(solution)/shard_map/reduce_scatter | solution.py:154
  747.0 7.9 fusion.55
  755.7 68.2 %reduce-scatter.17.cloned.1.call-done = bf16[1,136,272]{2,1,0:T(8,128)(2,1)} async-done(((bf16[16,136,272]{2,1,0:T(8,128)(2,1)}), bf16[1,136,272]{2,1,0:T(8,128)(2,1)}) %reduce-scatter.17.cloned.1.call-update) | async-done | bytes 74000
  825.6 3.2 copy_bitcast_fusion.1
  828.8 27.4 %reduce-scatter.15.cloned.1.call-done = f32[1,12,136]{2,1,0:T(8,128)} async-done(((f32[8,12,136]{2,1,0:T(8,128)}), f32[1,12,136]{2,1,0:T(8,128)}) %reduce-scatter.15.cloned.1.call-update) | async-done | bytes 6544 | tf_op jit(solution)/shard_map/reduce_scatter | solution.py:178
  856.2 74.7 %psum.7 = f32[12,136]{1,0:T(8,128)S(1)} all-reduce(f32[12,136]{1,0:T(8,128)} %bitcast.212), channel_id=1, replica_groups=mesh['batch'=16,'seq'=8] {'batch'}, use_global_device_ids=true, to_apply=%region_26.27 | all-reduce | flops 1632 | bytes 13056 | tf_op jit(solution)/shard_map/psum | solution.py:179
  932.2 19.3 %all-reduce.4.cloned.1.call-done = bf16[1088,1088]{0,1:T(8,128)(2,1)} async-done(((bf16[1088,1088]{0,1:T(8,128)(2,1)}), bf16[1088,1088]{0,1:T(8,128)(2,1)}) %all-reduce.4.cloned.1.call-update) | async-done | bytes 2367504
  (152 shorter events, 40.8 us)
Async XLA Ops:
  7.2 52.6 %all-gather.17.cloned.1.call-start = ((), (), s32[]{:S(2)}) async-start(), calls=%async_computation.12 | async-start | bytes 2820096 | tf_op jit(solution)/shard_map/all_gather | solution.py:60
  9.8 55.2 %copy-start.18 = (bf16[1,544]{1,0:T(2,128)(2,1)S(1)}, bf16[1,544]{1,0:T(2,128)(2,1)}, u32[]{:S(2)}) copy-start(bf16[1,544]{1,0:T(2,128)(2,1)} %param.23) | copy-start | bytes 3268
  9.9 55.3 %copy-start.19 = (bf16[2,136]{1,0:T(2,128)(2,1)S(1)}, bf16[2,136]{1,0:T(2,128)(2,1)}, u32[]{:S(2)}) copy-start(bf16[2,136]{1,0:T(2,128)(2,1)} %param.19) | copy-start | bytes 1636
  9.9 55.3 %copy-start.20 = (bf16[2,136]{1,0:T(2,128)(2,1)S(1)}, bf16[2,136]{1,0:T(2,128)(2,1)}, u32[]{:S(2)}) copy-start(bf16[2,136]{1,0:T(2,128)(2,1)} %param.20) | copy-start | bytes 1636
  9.9 55.3 %copy-start.21 = (bf16[2,136]{1,0:T(2,128)(2,1)S(1)}, bf16[2,136]{1,0:T(2,128)(2,1)}, u32[]{:S(2)}) copy-start(bf16[2,136]{1,0:T(2,128)(2,1)} %param.21) | copy-start | bytes 1636
  9.9 55.3 %copy-start.22 = (bf16[2,136]{1,0:T(2,128)(2,1)S(1)}, bf16[2,136]{1,0:T(2,128)(2,1)}, u32[]{:S(2)}) copy-start(bf16[2,136]{1,0:T(2,128)(2,1)} %param.22) | copy-start | bytes 1636
  9.9 152.4 %all-gather.15.cloned.1.call-start = ((), (), s32[]{:S(2)}) async-start(), calls=%async_computation.11 | async-start | bytes 22560768 | tf_op jit(solution)/shard_map/all_gather | solution.py:62
  64.2 14.9 %copy-start.4 = (bf16[2,128,1088]{1,2,0:T(8,128)(2,1)S(1)}, bf16[2,128,1088]{1,2,0:T(8,128)(2,1)}, u32[]{:S(2)}) copy-start(bf16[2,128,1088]{1,2,0:T(8,128)(2,1)} %param.12) | copy-start | bytes 1671172
  64.2 145.4 %all-gather.19.cloned.1.call-start = ((), (), s32[]{:S(2)}) async-start(), calls=%async_computation.13 | async-start | bytes 1775616 | tf_op jit(solution)/shard_map/all_gather | solution.py:61
  65.0 239.2 %all-gather.11.cloned.1.call-start = ((), (), s32[]{:S(2)}) async-start(), calls=%async_computation.5 | async-start | bytes 10027008 | tf_op jit(solution)/shard_map/all_gather | solution.py:79
  79.1 1.5 copy-start.13
  81.3 100.0 %copy-start.9 = (bf16[2,128,1088]{2,1,0:T(8,128)(2,1)}, bf16[2,128,1088]{2,1,0:T(8,128)(2,1)S(1)}, u32[]{:S(2)}) copy-start(bf16[2,128,1088]{2,1,0:T(8,128)(2,1)S(1)} %copy.69) | copy-start | bytes 1671172
  189.3 177.4 %all-gather.13.cloned.1.call-start = ((), (), s32[]{:S(2)}) async-start(), calls=%async_computation.6 | async-start | bytes 10653696 | tf_op jit(solution)/shard_map/all_gather | solution.py:63
  211.3 3.4 copy-start.23
  214.1 363.8 %reduce-scatter.9.cloned.1.call-start = ((), (), s32[]{:S(2)}) async-start(), calls=%async_computation.7 | async-start | bytes 20054016 | tf_op jit(solution)/shard_map/reduce_scatter | solution.py:141
  232.8 6.3 copy-start.11
  331.2 11.9 %copy-start.8 = (bf16[8,1088,136]{1,2,0:T(8,128)(2,1)S(1)}, bf16[8,1088,136]{1,2,0:T(8,128)(2,1)}, u32[]{:S(2)}) copy-start(bf16[8,1088,136]{1,2,0:T(8,128)(2,1)} %copy.100) | copy-start | bytes 7102468
  360.9 5.8 copy-start.2
  393.4 1.0 copy-start.6
  404.1 11.2 %copy-start.12 = (bf16[2,128,17,64]{1,0,3,2:T(2,128)(2,1)S(1)}, bf16[2,128,17,64]{1,0,3,2:T(2,128)(2,1)}, u32[]{:S(2)}) copy-start(bf16[2,128,17,64]{1,0,3,2:T(2,128)(2,1)} %reshape.285) | copy-start | bytes 1671172
  450.9 6.3 copy-start
  480.0 157.6 %reduce-scatter.13.cloned.1.call-start = ((), (), s32[]{:S(2)}) async-start(), calls=%async_computation.9 | async-start | bytes 10653696 | tf_op jit(solution)/shard_map/reduce_scatter | solution.py:155
  486.8 260.1 %reduce-scatter.11.cloned.1.call-start = ((), (), s32[]{:S(2)}) async-start(), calls=%async_computation.8 | async-start | bytes 22560768 | tf_op jit(solution)/shard_map/reduce_scatter | solution.py:154
  498.0 2.4 copy-start.3
  577.9 1.8 copy-start.10
  585.2 4.1 copy-start.1
  603.3 220.6 %reduce-scatter.17.cloned.1.call-start = ((), (), s32[]{:S(2)}) async-start(), calls=%async_computation.15 | async-start | bytes 1775616
  641.9 4.1 copy-start.5
  641.9 4.1 copy-start.14
  641.9 4.1 copy-start.16
  641.9 4.1 copy-start.17
  645.1 211.1 %reduce-scatter.15.cloned.1.call-start = ((), (), s32[]{:S(2)}) async-start(), calls=%async_computation.10 | async-start | bytes 147456 | tf_op jit(solution)/shard_map/reduce_scatter | solution.py:178
  655.3 2.7 copy-start.15
  655.3 2.8 copy-start.24
  656.7 294.9 %all-reduce.4.cloned.1.call-start = ((), (), s32[]{:S(2)}) async-start(), calls=%async_computation.14 | async-start | bytes 5013504
  747.0 78.6 %copy-start.7 = (f32[256,1088]{0,1:T(8,128)S(1)}, f32[256,1088]{0,1:T(8,128)}, u32[]{:S(2)}) copy-start(f32[256,1088]{0,1:T(8,128)} %copy-done.6) | copy-start | bytes 3342340
Sparse Core Ops, SparseCore 0:
  10.8 48.9 all-gather.16
  64.3 97.8 all-gather.14
  164.5 45.0 all-gather.18
  211.7 92.4 all-gather.10
  305.7 55.1 all-gather.12
  480.2 97.7 reduce-scatter.8
  580.3 57.2 reduce-scatter.12
  640.1 106.7 reduce-scatter.10
  750.3 73.6 reduce-scatter.16
  826.7 29.4 reduce-scatter.14
  860.1 91.4 all-reduce.3

commit v2 on v1

v2 whole, which is shorter than its diff:
```python
import jax
import jax.numpy as jnp
from jax import lax
from jax.experimental import pallas as pl
from jax.experimental.pallas import tpu as pltpu
from jax.sharding import PartitionSpec as P

D = 1088
F32 = jnp.float32
BF16 = jnp.bfloat16
MESH = pl.DeviceIdType.MESH
A_ROWS, B_ROWS = 272, 144
CUT = 208


class Place:
    def __init__(self):
        batch, seq = lax.axis_index("batch"), lax.axis_index("seq")
        self.y, self.z = batch // 4, batch % 4
        self.x, self.c = seq // 2, seq % 2
        self.sibling = {"batch": batch, "seq": self.x * 2 + 1 - self.c}

    def peer(self, axis, step):
        spot = {"x": self.x, "y": self.y, "z": self.z}
        spot[axis] = (spot[axis] + step + 4) % 4
        return {"batch": spot["y"] * 4 + spot["z"], "seq": spot["x"] * 2 + self.c}


def greet(peers):
    barrier = pltpu.get_barrier_semaphore()
    for peer in peers:
        pl.semaphore_signal(barrier, inc=1, device_id=peer, device_id_type=MESH)
    pl.semaphore_wait(barrier, len(peers))


def all_peers(me):
    return [me.sibling] + [me.peer(axis, step) for axis, step in (
        ("x", 1), ("x", 3), ("y", 1), ("y", 3), ("z", 1), ("z", 2), ("z", 3))]


class Sender:
    def __init__(self, send_sems, recv_sems):
        self.send_sems, self.recv_sems, self.made = send_sems, recv_sems, []

    def __call__(self, source, target, peer):
        index = len(self.made)
        copy = pltpu.make_async_remote_copy(
            src_ref=source, dst_ref=target, send_sem=self.send_sems.at[index],
            recv_sem=self.recv_sems.at[index], device_id=peer, device_id_type=MESH)
        copy.start()
        self.made.append(copy)
        return copy


def merge_rows(stacked):
    row = lax.broadcasted_iota(jnp.int32, (A_ROWS, 320), 0)
    col = lax.broadcasted_iota(jnp.int32, (A_ROWS, 320), 1)
    pick = jnp.where(col == row + 12 * (row // 68), 1.0, 0.0).astype(BF16)
    return jnp.dot(pick, stacked, preferred_element_type=F32).astype(BF16)


def merge_columns(slots):
    total = None
    for z in range(4):
        row = lax.broadcasted_iota(jnp.int32, (384, D), 0)
        col = lax.broadcasted_iota(jnp.int32, (384, D), 1)
        pick = jnp.where((col == row + 272 * z) & (row < 272), 1.0, 0.0).astype(BF16)
        term = jnp.dot(slots[z], pick, preferred_element_type=F32)
        total = term if total is None else total + term
    return total.astype(BF16)


GATHER_COPIES = 120


def gather_kernel(a_ref, b_ref, ga, gb, za, zb, mine_a, mine_b, send_sems, recv_sems, local_sems):
    me = Place()
    greet(all_peers(me))
    send = Sender(send_sems, recv_sems)
    first = []
    for step in (1, 2, 3):
        peer = me.peer("z", step)
        first.append(send(a_ref, za.at[me.z], peer))
        first.append(send(b_ref, zb.at[me.z], peer))
    za[me.z] = a_ref[...]
    zb[me.z] = b_ref[...]
    for copy in first:
        copy.wait_recv()
    mine_a[...] = merge_rows(za[...].reshape(320, D))
    mine_b[...] = merge_columns(zb)

    def spot(part, step_x, step_y):
        x, y = (me.x + step_x) % 4, (me.y + step_y) % 4
        if part == "b":
            return gb.at[y, 2 * x + me.c]
        low, rows = part
        return ga.at[2 * x + me.c, pl.ds(pl.multiple_of(y * A_ROWS + low, 16), rows)]

    own = [pltpu.make_async_copy(mine_a, spot((0, A_ROWS), 0, 0), local_sems.at[0]),
           pltpu.make_async_copy(mine_b, spot("b", 0, 0), local_sems.at[1])]
    for copy in own:
        copy.start()
    whole = {0: [(0, CUT)], 1: [(CUT, A_ROWS - CUT), "b"]}
    split = {0: [(0, 96), (96, CUT - 96)], 1: [(CUT, A_ROWS - CUT), "b"]}

    def source(part, steps):
        if steps != (0, 0):
            return spot(part, *steps)
        if part == "b":
            return mine_b
        return mine_a.at[pl.ds(part[0], part[1])]

    def move(axis, steps, by):
        return ((steps[0] + by) % 4, steps[1]) if axis == "x" else (steps[0], (steps[1] + by) % 4)

    crossed = []

    def to_sibling(part, steps):
        crossed.append(send(source(part, steps), spot(part, *steps), me.sibling))

    def begin(half, axis, steps):
        return {by: [send(source(part, steps), spot(part, *steps), me.peer(axis, by))
                     for part in whole[half]] for by in (1, 3)}

    def forward(half, axis, steps, sent, flip):
        ends = []
        for by, which in ((1, flip), (3, 1 - flip)):
            origin = move(axis, steps, -by)
            for copy in sent[by]:
                copy.wait_recv()
            part = split[half][which]
            ends.append((send(spot(part, *origin), spot(part, *origin), me.peer(axis, by)), part))
        return ends

    def arrived(half, axis, steps):
        for by in (1, 3):
            for part in whole[half]:
                to_sibling(part, move(axis, steps, by))

    def finish(half, axis, steps, ends):
        for copy, part in ends:
            copy.wait_recv()
        for part in whole[half]:
            to_sibling(part, move(axis, steps, 2))

    axes = {0: ("x", "y"), 1: ("y", "x")}
    first = {half: begin(half, axes[half][0], (0, 0)) for half in (0, 1)}
    second = {(half, 0): begin(half, axes[half][1], (0, 0)) for half in (0, 1)}
    to_sibling((0, A_ROWS), (0, 0))
    to_sibling("b", (0, 0))
    ends = {}
    for half in (0, 1):
        axis = axes[half][0]
        ends[half] = forward(half, axis, (0, 0), first[half], half)
        for by in (1, 3):
            second[half, by] = begin(half, axes[half][1], move(axis, (0, 0), by))
    for half in (0, 1):
        arrived(half, axes[half][0], (0, 0))
    tails = {}
    for half in (0, 1):
        tails[half, 0] = forward(half, axes[half][1], (0, 0), second[half, 0], 0)
        arrived(half, axes[half][1], (0, 0))
    for half in (0, 1):
        axis = axes[half][0]
        finish(half, axis, (0, 0), ends[half])
        second[half, 2] = begin(half, axes[half][1], move(axis, (0, 0), 2))
    order = [(half, by) for by in (1, 3, 2) for half in (0, 1)]
    done = [(half, 0) for half in (0, 1)]
    for half, by in order:
        steps = move(axes[half][0], (0, 0), by)
        tails[half, by] = forward(half, axes[half][1], steps, second[half, by], by % 2)
        arrived(half, axes[half][1], steps)
        if done:
            late, late_by = done.pop(0)
            finish(late, axes[late][1], move(axes[late][0], (0, 0), late_by), tails[late, late_by])
        done.append((half, by))
    for late, late_by in done:
        finish(late, axes[late][1], move(axes[late][0], (0, 0), late_by), tails[late, late_by])
    for copy in crossed:
        copy.wait_recv()
    for copy in send.made:
        copy.wait_send()
    for copy in own:
        copy.wait()


def gather_weights(blob_a, blob_b):
    return pl.pallas_call(
        gather_kernel,
        out_shape=(jax.ShapeDtypeStruct((8, D, D), BF16),
                   jax.ShapeDtypeStruct((4, 8, B_ROWS, D), BF16)),
        in_specs=[pl.BlockSpec(memory_space=pltpu.VMEM)] * 2,
        out_specs=(pl.BlockSpec(memory_space=pl.ANY),) * 2,
        scratch_shapes=[
            pltpu.VMEM((4, 80, D), BF16), pltpu.VMEM((4, B_ROWS, 384), BF16),
            pltpu.VMEM((A_ROWS, D), BF16), pltpu.VMEM((B_ROWS, D), BF16),
            pltpu.SemaphoreType.DMA((GATHER_COPIES,)), pltpu.SemaphoreType.DMA((GATHER_COPIES,)),
            pltpu.SemaphoreType.DMA((2,)),
        ],
        compiler_params=pltpu.CompilerParams(
            collective_id=0, has_side_effects=True, vmem_limit_bytes=40 * 2**20),
    )(blob_a, blob_b)


NT = (((1,), (1,)), ((), ()))


class Group:
    def __init__(self):
        self.batch, self.me = lax.axis_index("batch"), lax.axis_index("seq")

    def peer(self, seq):
        return {"batch": self.batch, "seq": seq}

    def other(self, step):
        return (self.me + step) % 8


def push(source, target, sems, index, peer):
    return pltpu.make_async_remote_copy(
        src_ref=source, dst_ref=target, send_sem=sems.at[(0,) + index],
        recv_sem=sems.at[(1,) + index], device_id=peer, device_id_type=MESH)


def turned(value):
    return value.astype(F32).T


def masked(scores, bounds, seq, block):
    rows = lax.broadcasted_iota(jnp.int32, scores.shape, 0)
    spot = block * 256 + lax.broadcasted_iota(jnp.int32, (1, 256), 1)
    start = jnp.zeros((1, 256), jnp.int32)
    for n in range(3):
        bound = bounds[seq, n]
        start = jnp.where(spot >= bound, bound, start)
    return jnp.where((rows <= spot) & (rows >= start), scores, -1e30)


def chances(keys, query, bounds, seq, block):
    scores = lax.dot_general(keys, query, NT, preferred_element_type=F32)
    scores = masked(scores, bounds, seq, block)
    powers = jnp.exp(scores - jnp.max(scores, axis=0, keepdims=True))
    return powers * (1.0 / jnp.sum(powers, axis=0, keepdims=True))


def head_part(value, head):
    lane = lax.broadcasted_iota(jnp.int32, value.shape, 1)
    return jnp.where((lane < 64) == (head == 0), value, jnp.zeros_like(value))


def attend(queries, keys, values, bounds, seq, heads, store):
    queries = queries * 0.125
    value_t = turned(values).astype(BF16)
    for block in range(4):
        rows = slice(block * 256, block * 256 + 256)
        size = block * 256 + 256
        parts = []
        for head in range(heads):
            low = chances(keys[:size], head_part(queries[rows], head), bounds, seq, block).astype(BF16)
            parts.append(jnp.dot(value_t[:, :size], low, preferred_element_type=F32))
        whole = parts[0] if heads == 1 else jnp.concatenate([parts[0][:64], parts[1][64:]], axis=0)
        store(block, whole.T.astype(BF16).reshape(2, 128, 128))


def attend_kernel(pack, bounds, att, got, got8, out, out8, in_sems, in8_sems, back_sems, back8_sems):
    g = Group()
    greet([g.peer(g.other(step)) for step in range(1, 8)])

    def in_copy(step):
        return push(pack.at[g.other(step)], got.at[g.me], in_sems, (step - 1,), g.peer(g.other(step)))

    def in8_copy(extra, source):
        return pltpu.make_async_remote_copy(
            src_ref=pack.at[8, :, extra], dst_ref=got8.at[source], send_sem=in8_sems.at[8 + extra],
            recv_sem=in8_sems.at[source], device_id=g.peer(4 * extra), device_id_type=MESH)

    for step in (4, 3, 5, 2, 6, 1, 7):
        in_copy(step).start()
    for extra in (0, 1):
        @pl.when(g.me != 4 * extra)
        def _():
            in8_copy(extra, g.me).start()

        @pl.when(g.me == 4 * extra)
        def _():
            got8[g.me] = pack[8, :, extra]
    got[g.me] = pack[g.me]
    for step in range(1, 8):
        in_copy(step).wait_recv()

    def back_copy(seq, step):
        return push(out.at[g.other(step), seq], att.at[g.me, seq], back_sems, (seq, step - 1),
                    g.peer(g.other(step)))

    def pair(seq, carry):
        def store(block, value):
            out[pl.ds(2 * block, 2), seq] = value
        part = lambda kind: got[:, kind, seq].reshape(1024, 128)
        attend(part(0), part(1), part(2), bounds, seq, 2, store)
        for step in (4, 3, 5, 2, 6, 1, 7):
            back_copy(seq, step).start()
        return carry

    lax.fori_loop(0, 2, pair, 0)
    att[g.me] = out[g.me]

    def back8_copy(extra, step):
        return pltpu.make_async_remote_copy(
            src_ref=out8.at[g.other(step)], dst_ref=att.at[8, extra], send_sem=back8_sems.at[1 + step],
            recv_sem=back8_sems.at[extra], device_id=g.peer(g.other(step)), device_id_type=MESH)

    for extra in (0, 1):
        @pl.when(g.me == 4 * extra)
        def _():
            for step in range(1, 8):
                in8_copy(extra, g.other(step)).wait_recv()

            def store(block, value):
                out8[pl.ds(2 * block, 2)] = value
            part = lambda kind: got8[:, kind].reshape(1024, 128)
            attend(part(0), part(1), part(2), bounds, extra, 1, store)
            for step in range(1, 8):
                back8_copy(extra, step).start()
            att[8, extra] = out8[g.me]
            for step in range(1, 8):
                back8_copy(extra, step).wait_send()

        @pl.when(g.me != 4 * extra)
        def _():
            in8_copy(extra, g.me).wait_send()
            back8_copy(extra, 1).wait_recv()
    for step in range(1, 8):
        in_copy(step).wait_send()
        for seq in (0, 1):
            back_copy(seq, step).wait_recv()
            back_copy(seq, step).wait_send()


def attend_forward(pack, bounds):
    tile = (128, 128)
    vmem = pltpu.VMEM
    return pl.pallas_call(
        attend_kernel,
        out_shape=(jax.ShapeDtypeStruct((9, 2) + tile, BF16),
                   jax.ShapeDtypeStruct((8, 3, 2) + tile, BF16),
                   jax.ShapeDtypeStruct((8, 3) + tile, BF16)),
        in_specs=[pl.BlockSpec(memory_space=vmem), pl.BlockSpec(memory_space=pltpu.SMEM)],
        out_specs=(pl.BlockSpec(memory_space=vmem),) * 3,
        scratch_shapes=[
            vmem((8, 2) + tile, BF16), vmem((8,) + tile, BF16),
            pltpu.SemaphoreType.DMA((2, 7)), pltpu.SemaphoreType.DMA((10,)),
            pltpu.SemaphoreType.DMA((2, 2, 7)), pltpu.SemaphoreType.DMA((9,))],
        compiler_params=pltpu.CompilerParams(
            collective_id=1, has_side_effects=True, vmem_limit_bytes=40 * 2**20),
    )(pack, bounds)


def attend_pull(queries, keys, values, grads, bounds, seq, heads, key_sum, value_sum, store):
    queries = queries * 0.125
    key_t = turned(keys).astype(BF16)
    key_sum[...] = jnp.zeros_like(key_sum)
    value_sum[...] = jnp.zeros_like(value_sum)
    for block in range(4):
        rows = slice(block * 256, block * 256 + 256)
        size = block * 256 + 256
        parts = []
        for head in range(heads):
            query, grad = head_part(queries[rows], head), head_part(grads[rows], head)
            probs = chances(keys[:size], query, bounds, seq, block)
            change = lax.dot_general(values[:size], grad, NT, preferred_element_type=F32)
            inner = jnp.sum(probs * change, axis=0, keepdims=True)
            slope = (probs * (change - inner)).astype(BF16)
            value_sum[:size] += jnp.dot(probs.astype(BF16), grad, preferred_element_type=F32)
            key_sum[:size] += jnp.dot(slope, query, preferred_element_type=F32)
            parts.append(jnp.dot(key_t[:, :size], slope, preferred_element_type=F32))
        whole = parts[0] if heads == 1 else jnp.concatenate([parts[0][:64], parts[1][64:]], axis=0)
        store(0, block, (whole.T * 0.125).astype(BF16).reshape(2, 128, 128))
    for kind, total in ((1, key_sum), (2, value_sum)):
        for block in range(4):
            store(kind, block, total[block * 256 : block * 256 + 256].astype(BF16).reshape(2, 128, 128))


def pull_kernel(pack, got, got8, bounds, back, grad, grad8, out, out8, key_sum, value_sum,
                in_sems, in8_sems, back_sems, back8_sems):
    g = Group()
    greet([g.peer(g.other(step)) for step in range(1, 8)])

    def in_copy(step):
        return push(pack.at[g.other(step)], grad.at[g.me], in_sems, (step - 1,), g.peer(g.other(step)))

    def in8_copy(extra, source):
        return pltpu.make_async_remote_copy(
            src_ref=pack.at[8, extra], dst_ref=grad8.at[source], send_sem=in8_sems.at[8 + extra],
            recv_sem=in8_sems.at[source], device_id=g.peer(4 * extra), device_id_type=MESH)

    for step in (4, 3, 5, 2, 6, 1, 7):
        in_copy(step).start()
    for extra in (0, 1):
        @pl.when(g.me != 4 * extra)
        def _():
            in8_copy(extra, g.me).start()

        @pl.when(g.me == 4 * extra)
        def _():
            grad8[g.me] = pack[8, extra]
    grad[g.me] = pack[g.me]
    for step in range(1, 8):
        in_copy(step).wait_recv()

    def back_copy(seq, step):
        return push(out.at[g.other(step), seq], back.at[g.me, seq], back_sems, (seq, step - 1),
                    g.peer(g.other(step)))

    def pair(seq, carry):
        def store(kind, block, value):
            out[pl.ds(2 * block, 2), seq, kind] = value
        part = lambda kind: got[:, kind, seq].reshape(1024, 128)
        attend_pull(part(0), part(1), part(2), grad[:, seq].reshape(1024, 128), bounds, seq, 2,
                    key_sum, value_sum, store)
        for step in (4, 3, 5, 2, 6, 1, 7):
            back_copy(seq, step).start()
        return carry

    lax.fori_loop(0, 2, pair, 0)
    back[g.me] = out[g.me]

    def back8_copy(extra, step):
        return pltpu.make_async_remote_copy(
            src_ref=out8.at[g.other(step)], dst_ref=back.at[8, extra], send_sem=back8_sems.at[1 + step],
            recv_sem=back8_sems.at[extra], device_id=g.peer(g.other(step)), device_id_type=MESH)

    for extra in (0, 1):
        @pl.when(g.me == 4 * extra)
        def _():
            for step in range(1, 8):
                in8_copy(extra, g.other(step)).wait_recv()

            def store(kind, block, value):
                out8[pl.ds(2 * block, 2), kind] = value
            part = lambda kind: got8[:, kind].reshape(1024, 128)
            attend_pull(part(0), part(1), part(2), grad8[...].reshape(1024, 128), bounds, extra, 1,
                        key_sum, value_sum, store)
            for step in range(1, 8):
                back8_copy(extra, step).start()
            back[8, extra] = out8[g.me]
            for step in range(1, 8):
                back8_copy(extra, step).wait_send()

        @pl.when(g.me != 4 * extra)
        def _():
            in8_copy(extra, g.me).wait_send()
            back8_copy(extra, 1).wait_recv()
    for step in range(1, 8):
        in_copy(step).wait_send()
        for seq in (0, 1):
            back_copy(seq, step).wait_recv()
            back_copy(seq, step).wait_send()


def attend_backward(pack, got, got8, bounds):
    tile = (128, 128)
    vmem = pltpu.VMEM
    return pl.pallas_call(
        pull_kernel,
        out_shape=jax.ShapeDtypeStruct((9, 2, 3) + tile, BF16),
        in_specs=[pl.BlockSpec(memory_space=vmem)] * 3 + [pl.BlockSpec(memory_space=pltpu.SMEM)],
        out_specs=pl.BlockSpec(memory_space=vmem),
        scratch_shapes=[
            vmem((8, 2) + tile, BF16), vmem((8,) + tile, BF16),
            vmem((8, 2, 3) + tile, BF16), vmem((8, 3) + tile, BF16),
            vmem((1024, 128), F32), vmem((1024, 128), F32),
            pltpu.SemaphoreType.DMA((2, 7)), pltpu.SemaphoreType.DMA((10,)),
            pltpu.SemaphoreType.DMA((2, 2, 7)), pltpu.SemaphoreType.DMA((9,))],
        compiler_params=pltpu.CompilerParams(
            collective_id=2, has_side_effects=True, vmem_limit_bytes=50 * 2**20),
    )(pack, got, got8, bounds)


def reduce_kernel(xt, yb, tt, act, extra, out_a, out_b,
                  sib_out1, sib_out2, sib_in1, sib_in2,
                  in_opp1, in_opp2, in_side1, in_side2,
                  acc1, acc2, end1, end2, in_end1, in_end2, in_mid1, in_mid2,
                  zout_a, zout_b, zin_a, zin_b,
                  sib_sems, opp_sems, side_sems, mid_sems, end_sems, z_sems):
    me = Place()
    greet(all_peers(me))

    def part1(xb, yy, parity):
        column = 2 * xb + parity
        rows = pl.ds(pl.multiple_of(yy * A_ROWS, 16), CUT)
        return outer(column, rows)

    def outer(column, rows):
        one = jnp.dot(xt[0, rows], yb[column, :, 0:512], preferred_element_type=F32)
        two = jnp.dot(xt[1, rows], yb[column, :, 384:640], preferred_element_type=F32)
        three = jnp.dot(xt[2, rows], yb[column, :, 512:], preferred_element_type=F32)
        lane = lax.broadcasted_iota(jnp.int32, (one.shape[0], 128), 1)
        return jnp.concatenate([
            one[:, :384],
            jnp.where(lane < 24, one[:, 384:512], two[:, :128]),
            jnp.where(lane < 32, two[:, 128:], three[:, :128]),
            three[:, 128:]], axis=1)

    def part2(xb, yy, parity):
        column = 2 * xb + parity
        rows = pl.ds(pl.multiple_of(yy * A_ROWS + CUT, 16), A_ROWS - CUT)
        lower = jnp.dot(tt[column], act[yy], preferred_element_type=F32)
        lower = jnp.concatenate([lower[:136], extra[column]], axis=0)
        return jnp.concatenate([outer(column, rows), lower], axis=0)

    def turn(value, by):
        return (value + by) % 4

    def copy(source, target, sems, index, peer):
        return pltpu.make_async_remote_copy(
            src_ref=source, dst_ref=target, send_sem=sems.at[(0,) + index],
            recv_sem=sems.at[(1,) + index], device_id=peer, device_id_type=MESH)

    blocks = {
        0: dict(part=lambda step, o, par: part1(turn(me.x, step), turn(me.y, o), par),
                axes=("x", "y"), cut=96, sib_out=sib_out1, sib_in=sib_in1, in_opp=in_opp1,
                in_side=in_side1, acc=acc1, end=end1, in_end=in_end1, in_mid=in_mid1),
        1: dict(part=lambda step, o, par: part2(turn(me.x, o), turn(me.y, step), par),
                axes=("y", "x"), cut=64, sib_out=sib_out2, sib_in=sib_in2, in_opp=in_opp2,
                in_side=in_side2, acc=acc2, end=end2, in_end=in_end2, in_mid=in_mid2),
    }

    def sib_copy(half, step, o):
        b = blocks[half]
        return copy(b["sib_out"].at[o], b["sib_in"].at[step, o], sib_sems, (half, step, o), me.sibling)

    def cross(step, before):
        def body(o, carry):
            for half in (0, 1):
                b = blocks[half]
                if before is not None:
                    sib_copy(half, before, o).wait_send()
                b["sib_out"][o] = b["part"](step, o, 1 - me.c).astype(BF16)
                sib_copy(half, step, o).start()
            return carry
        lax.fori_loop(0, 4, body, 0)

    def mine(half, step, o):
        b = blocks[half]
        value = b["part"](step, o, me.c)
        sib_copy(half, step, o).wait_recv()
        return value + b["sib_in"][step, o].astype(F32)

    def ends_of(half, which):
        b = blocks[half]
        total = CUT
        return pl.ds(0, b["cut"]) if which == 0 else pl.ds(b["cut"], total - b["cut"])

    def opp_copy(half, o, which):
        b = blocks[half]
        rows = ends_of(half, which)
        return copy(b["sib_in"].at[2, o, rows], b["in_opp"].at[o, rows], opp_sems, (half, o, which),
                    me.peer(b["axes"][0], 1 if which == 0 else 3))

    def side_copy(half, o, which):
        b = blocks[half]
        return copy(b["sib_in"].at[1 + 2 * which, o], b["in_side"].at[which, o], side_sems, (half, o, which),
                    me.peer(b["axes"][0], 1 if which == 0 else 3))

    def mid_copy(half, which):
        b = blocks[half]
        rows = ends_of(half, which)
        return copy(b["end"].at[2, rows], b["in_mid"].at[rows], mid_sems, (half, which),
                    me.peer(b["axes"][1], 1 if which == 0 else 3))

    def end_copy(half, which):
        b = blocks[half]
        return copy(b["end"].at[which], b["in_end"].at[which], end_sems, (half, which),
                    me.peer(b["axes"][1], 1 if which == 0 else 3))

    def loop(body):
        lax.fori_loop(0, 4, lambda o, carry: (body(o), carry)[1], 0)

    def opposite(o):
        for half in (0, 1):
            blocks[half]["sib_in"][2, o] = mine(half, 2, o).astype(BF16)
            for which in (0, 1):
                opp_copy(half, o, which).start()

    def sides(o):
        for half in (0, 1):
            b = blocks[half]
            cut = b["cut"]
            for which in (0, 1):
                value = mine(half, 1 if which == 0 else 3, o)
                opp_copy(half, o, which).wait_recv()
                if which == 0:
                    value = jnp.concatenate(
                        [value[:cut] + b["in_opp"][o, :cut].astype(F32), value[cut:]], axis=0)
                else:
                    value = jnp.concatenate(
                        [value[:cut], value[cut:] + b["in_opp"][o, cut:].astype(F32)], axis=0)
                b["sib_in"][1 + 2 * which, o] = value.astype(BF16)
                side_copy(half, o, which).start()

    def own(o):
        for half in (0, 1):
            b = blocks[half]
            value = mine(half, 0, o)
            for which in (0, 1):
                side_copy(half, o, which).wait_recv()
                value = value + b["in_side"][which, o].astype(F32)
            b["acc"][o] = value

    cross(2, None)
    loop(opposite)
    cross(1, 2)
    cross(3, 1)
    loop(sides)
    cross(0, 3)
    loop(own)
    for half in (0, 1):
        b = blocks[half]
        b["end"][2] = b["acc"][2].astype(BF16)
        for which in (0, 1):
            mid_copy(half, which).start()
    for half in (0, 1):
        b = blocks[half]
        cut = b["cut"]
        for which in (0, 1):
            value = b["acc"][1 if which == 0 else 3]
            mid_copy(half, which).wait_recv()
            if which == 0:
                value = jnp.concatenate([value[:cut] + b["in_mid"][:cut].astype(F32), value[cut:]], axis=0)
            else:
                value = jnp.concatenate([value[:cut], value[cut:] + b["in_mid"][cut:].astype(F32)], axis=0)
            b["end"][which] = value.astype(BF16)
            end_copy(half, which).start()
    final = []
    for half in (0, 1):
        b = blocks[half]
        value = b["acc"][0]
        for which in (0, 1):
            end_copy(half, which).wait_recv()
            value = value + b["in_end"][which].astype(F32)
        final.append(value.astype(BF16))
    block_a = jnp.concatenate([final[0], final[1][:64]], axis=0)
    block_b = final[1][64:]

    def slices(z):
        row = lax.broadcasted_iota(jnp.int32, (80, A_ROWS), 0)
        col = lax.broadcasted_iota(jnp.int32, (80, A_ROWS), 1)
        pick = jnp.where((col == row + 68 * z) & (row < 68), 1.0, 0.0).astype(BF16)
        row = lax.broadcasted_iota(jnp.int32, (D, 384), 0)
        col = lax.broadcasted_iota(jnp.int32, (D, 384), 1)
        pick_b = jnp.where((row == col + 272 * z) & (col < 272), 1.0, 0.0).astype(BF16)
        lower = jnp.dot(block_b, pick_b, preferred_element_type=F32)
        row = lax.broadcasted_iota(jnp.int32, (B_ROWS, 384), 0)
        lower = jnp.where(row < 136, lower, block_b[:, :384].astype(F32))
        return jnp.dot(pick, block_a, preferred_element_type=F32), lower

    def z_copies(step):
        peer = me.peer("z", step)
        return (copy(zout_a.at[step - 1], zin_a.at[step - 1], z_sems, (0, step - 1), peer),
                copy(zout_b.at[step - 1], zin_b.at[step - 1], z_sems, (1, step - 1), peer))

    for step in (2, 1, 3):
        upper, lower = slices(turn(me.z, step))
        zout_a[step - 1] = upper.astype(BF16)
        zout_b[step - 1] = lower.astype(BF16)
        for c in z_copies(step):
            c.start()
    upper, lower = slices(me.z)
    for step in (1, 2, 3):
        for c in z_copies(step):
            c.wait_recv()
        upper = upper + zin_a[step - 1].astype(F32)
        lower = lower + zin_b[step - 1].astype(F32)
    out_a[...] = upper
    out_b[...] = lower

    def drain(o):
        for half in (0, 1):
            sib_copy(half, 0, o).wait_send()
            for which in (0, 1):
                opp_copy(half, o, which).wait_send()
                side_copy(half, o, which).wait_send()

    loop(drain)
    for half in (0, 1):
        for which in (0, 1):
            mid_copy(half, which).wait_send()
            end_copy(half, which).wait_send()
    for step in (1, 2, 3):
        for c in z_copies(step):
            c.wait_send()


def reduce_weights(xt, yb, tt, act, extra):
    half = (CUT, D)
    vmem = pltpu.VMEM
    pair = lambda *lead: [vmem(lead + half, BF16), vmem(lead + half, BF16)]
    return pl.pallas_call(
        reduce_kernel,
        out_shape=(jax.ShapeDtypeStruct((80, D), F32), jax.ShapeDtypeStruct((B_ROWS, 384), F32)),
        in_specs=[pl.BlockSpec(memory_space=vmem)] * 5,
        out_specs=(pl.BlockSpec(memory_space=vmem),) * 2,
        scratch_shapes=(
            pair(4) + pair(4, 4) + pair(4) + pair(2, 4)
            + [vmem((4,) + half, F32)] * 2 + pair(3) + pair(2) + pair()
            + [vmem((3, 80, D), BF16), vmem((3, B_ROWS, 384), BF16)] * 2
            + [pltpu.SemaphoreType.DMA((2, 2, 4, 4)), pltpu.SemaphoreType.DMA((2, 2, 4, 2)),
               pltpu.SemaphoreType.DMA((2, 2, 4, 2)), pltpu.SemaphoreType.DMA((2, 2, 2)),
               pltpu.SemaphoreType.DMA((2, 2, 2)), pltpu.SemaphoreType.DMA((2, 2, 3))]),
        compiler_params=pltpu.CompilerParams(
            collective_id=3, has_side_effects=True, vmem_limit_bytes=63 * 2**20),
    )(xt, yb, tt, act, extra)


HEADS = 17
FF = 4352


def normalize(values):
    center = values - jnp.mean(values, axis=-1, keepdims=True)
    spread = jnp.mean(center * center, axis=-1, keepdims=True)
    scale = lax.rsqrt(spread + 1e-05)
    return center * scale, scale


def norm_pull(grad, gain, unit, scale):
    scaled = grad * gain
    return scale * (
        scaled
        - jnp.mean(scaled, axis=-1, keepdims=True)
        - unit * jnp.mean(scaled * unit, axis=-1, keepdims=True)
    )


def gelu_tanh(values):
    return jax.nn.gelu(values, approximate=True)


def dot(left, right):
    return jnp.dot(left, right, preferred_element_type=F32)


def pairs_out(rows):
    rows = jnp.pad(rows, [(0, 0)] * (rows.ndim - 1) + [(0, 64)])
    return jnp.moveaxis(rows.reshape(rows.shape[:-1] + (9, 128)), -2, 0)


def pairs_in(packed):
    rows = jnp.moveaxis(packed, 0, -2)
    return rows.reshape(rows.shape[:-2] + (1152,))[..., :D]


def per_device(
    inputs, out_grad, segment_ids, qkv_weight, out_weight, up_weight, down_weight,
    norm_gains, norm_shifts, qv_bias, proj_bias, up_bias,
):
    seqs, rows, _ = inputs.shape
    tokens = seqs * rows
    batch = lax.axis_index("batch")

    blob_a = jnp.concatenate([qkv_weight, out_weight, up_weight], axis=1)
    blob_a = jnp.pad(blob_a, ((0, 12), (0, 0)))
    counts = jnp.sum(segment_ids[:, :, None] < jnp.arange(1, 4)[None, None, :], axis=1)
    counts = jnp.pad(counts.astype(BF16).reshape(1, 6), ((0, 3), (0, 130)))
    vec = jnp.concatenate([norm_gains, norm_shifts, qv_bias, proj_bias], axis=0)
    vec = jnp.concatenate(
        [vec, jnp.concatenate([up_bias.reshape(4, 136), counts], axis=0)], axis=1
    )
    blob_b = jnp.concatenate([down_weight.T, vec], axis=0)
    blob_b = jnp.pad(blob_b, ((0, 0), (0, 112)))
    whole_a, whole_b = gather_weights(blob_a, blob_b)
    vec = lax.dynamic_slice(whole_b, (batch // 4, 0, 136, 272 * (batch % 4)), (1, 8, 8, 272))
    vec = vec[0].astype(F32)
    lines = vec[:, :, :136].transpose(1, 0, 2).reshape(8, D)
    gains, shifts, qv_rows, proj_rows = lines[0:2], lines[2:4], lines[4:6], lines[6:8]
    up_row = vec[:, :4, 136:].reshape(FF)
    bounds = jnp.sum(vec[:, 4, 136:142], axis=0).astype(jnp.int32).reshape(2, 3)
    w_qkv, w_out, w_up = whole_a[:, :, :408], whole_a[:, :, 408:544], whole_a[:, :, 544:]

    hidden = inputs.reshape(tokens, D).astype(F32)
    top_grad = out_grad.reshape(tokens, D)
    cotangent = top_grad.astype(F32)
    unit_one, scale_one = normalize(hidden)
    normed = (unit_one * gains[0] + shifts[0]).astype(BF16)
    projected = jnp.einsum("tk,skn->tsn", normed, w_qkv, preferred_element_type=F32).reshape(
        tokens, 3, D
    )
    shift = jnp.stack([qv_rows[0], jnp.zeros((D,), F32), qv_rows[1]])
    projected = (projected + shift).astype(BF16).reshape(seqs, rows, 3, D).transpose(2, 0, 1, 3)
    att, got, got8 = attend_forward(pairs_out(projected), bounds)
    attended = pairs_in(att).reshape(tokens, D)
    branch = jnp.einsum("tk,skn->tsn", attended, w_out, preferred_element_type=F32)
    middle = hidden + branch.reshape(tokens, D) + proj_rows[0]
    unit_two, scale_two = normalize(middle)
    normed_two = (unit_two * gains[1] + shifts[1]).astype(BF16)
    inner_pre = (
        jnp.einsum("tk,skn->tsn", normed_two, w_up, preferred_element_type=F32).reshape(tokens, FF)
        + up_row
    )
    active, gelu_pull = jax.vjp(gelu_tanh, inner_pre)
    active = active.astype(BF16).reshape(tokens, 4, D).transpose(1, 0, 2)
    downs = whole_b.reshape(4, 8 * B_ROWS, D)
    branch = sum(
        lax.dot_general(active[y], downs[y], (((1,), (1,)), ((), ())), preferred_element_type=F32)
        for y in range(4)
    )
    branch = branch.reshape(tokens, 8, B_ROWS)[:, :, :136].reshape(tokens, D)
    layer_out = (middle + branch + proj_rows[1]).astype(BF16)

    top_blocks = jnp.pad(top_grad.reshape(tokens, 8, 136), ((0, 0), (0, 0), (0, 8)))
    top_pad = top_blocks.reshape(tokens, 8 * B_ROWS)
    down_in = jnp.concatenate([dot(top_pad, downs[y]) for y in range(4)], axis=1)
    inner_grad = gelu_pull(down_in)[0].astype(BF16)
    inner_blocks = inner_grad.reshape(tokens, 8, 544)
    normed_two_grad = jnp.einsum("tsn,skn->tk", inner_blocks, w_up, preferred_element_type=F32)
    middle_grad = cotangent + norm_pull(normed_two_grad, gains[1], unit_two, scale_two)
    branch_grad = middle_grad.astype(BF16)
    branch_blocks = branch_grad.reshape(tokens, 8, 136)
    attended_grad = jnp.einsum(
        "tsn,skn->tk", branch_blocks, w_out, preferred_element_type=F32
    ).astype(BF16)
    back = attend_backward(
        pairs_out(attended_grad.reshape(seqs, rows, D)), got, got8, bounds
    )
    qkv_grad = pairs_in(back).transpose(0, 2, 1, 3).reshape(tokens, 3 * D)
    qkv_blocks = qkv_grad.reshape(tokens, 8, 408)
    normed_grad = jnp.einsum("tsn,skn->tk", qkv_blocks, w_qkv, preferred_element_type=F32)
    input_grad = middle_grad + norm_pull(normed_grad, gains[0], unit_one, scale_one)

    def column_sum(values):
        return jnp.sum(values, axis=0, dtype=F32)

    sums = jnp.stack(
        [
            column_sum(normed_grad * unit_one),
            column_sum(normed_two_grad * unit_two),
            column_sum(normed_grad),
            column_sum(normed_two_grad),
            column_sum(qkv_grad[:, :D]),
            column_sum(qkv_grad[:, 2 * D :]),
            column_sum(branch_grad),
            column_sum(top_grad),
        ]
    ).reshape(8, 8, 136)
    up_sums = jnp.pad(column_sum(inner_grad).reshape(8, 4, 136), ((0, 0), (0, 4), (0, 0)))
    extra = jnp.concatenate([sums.transpose(1, 0, 2), up_sums], axis=2)
    extra = jnp.pad(extra, ((0, 0), (0, 0), (0, D - 272)))
    left = jnp.stack([normed.T, attended.T, normed_two.T])
    right = jnp.concatenate([qkv_blocks, branch_blocks, inner_blocks], axis=2).transpose(1, 0, 2)
    out_a, out_b = reduce_weights(left, right, top_blocks.transpose(1, 2, 0), active, extra)
    return (
        layer_out.reshape(seqs, rows, D),
        input_grad.reshape(seqs, rows, D),
        out_a[:68, :408],
        out_a[:68, 408:544],
        out_a[:68, 544:],
        out_b[:136, :272].T,
        out_b[136:138, :136],
        out_b[138:140, :136],
        out_b[140:142, :136],
        out_b[142:144, :136],
        out_b[136:140, 136:272].reshape(1, 544),
    )


def solution(mesh):
    tokens = P("batch", "seq", None)
    matrix = P("batch", "seq")
    vector = P(None, "seq")
    return jax.shard_map(
        per_device,
        mesh=mesh,
        in_specs=(tokens, tokens, matrix, matrix, matrix, matrix, matrix) + (vector,) * 5,
        out_specs=(tokens, tokens, matrix, matrix, matrix, matrix) + (vector,) * 5,
        check_vma=False,
    )
```

time: 972 us -> 581 us (0.60)
  waiting for transfers between devices: 525 us -> 0 us
  Pallas kernels: 0 us -> 326 us
  blocking collectives: 98.3 us -> 0 us
  matrix products: 152 us -> 66.2 us
  local copies, waits for them, and re-layouts: 115 us -> 147 us
  other arithmetic: 55.5 us -> 30.5 us
  between operations: 15.6 us -> 1.67 us
    pallas_call x0 -> x4, Pallas kernels: none -> 326 us  [the longest x1 119 us: reduce_weights(): pl.pallas_call(reduce_kernel, out_shape=(jax.ShapeDtypeStruct((80, D), F3...]
    reduce_scatter x4 -> x0, waiting for transfers between devices: 221 us -> none  [the longest x1 87.6 us: per_device(): d_a = lax.psum_scatter(d_a, 'seq', scatter_dimension=0)]
    all_gather x5 -> x0, waiting for transfers between devices: 216 us -> none  [the longest x1 80.8 us: per_device(): whole_a = lax.all_gather(blob_a, 'seq', axis=0)]
    unnamed x13 -> x0, waiting for transfers between devices: 88.4 us -> none
    psum x1 -> x0, blocking collectives: 74.7 us -> none  [per_device(): sums = lax.psum(sums, 'batch')]
    dot_general x10 -> x4, matrix products: 78 us -> 4.43 us  [per_device(): lax.dot_general(active[y], downs[y], (((1,), (1,)), ((), ())), preferred_...]
    dot_general x0 -> x9, local copies, waits for them, and re-layouts: none -> 59.5 us  [the longest x4 21 us: dot(): return jnp.dot(left, right, preferred_element_type=F32)]
    unnamed x61 -> x84, local copies, waits for them, and re-layouts: 44.8 us -> 16 us
  transfers between devices with their start and end apart: 11 -> 0, of which waited for: 10 -> 0; matrix products, arithmetic and copies ran while one was open for 21% -> 0% of each run, Pallas kernels for 0% -> 0%
where the time goes in v2:
time: 581 us; the launch traced here: 571 us
  Pallas kernels  326 us (56%)
  local copies, waits for them, and re-layouts  147 us (25%)
  matrix products  66.2 us (11%)
  other arithmetic  30.5 us (5%)
    pallas_call x1, Pallas kernels, reduce_weights(): pl.pallas_call(reduce_kernel, out_shape=(jax.ShapeDtypeStruct((80, D), F3...  119 us
    pallas_call x1, Pallas kernels, gather_weights(): pl.pallas_call(gather_kernel, out_shape=(jax.ShapeDtypeStruct((8, D, D),...  109 us
    pallas_call x1, Pallas kernels, attend_backward(): pl.pallas_call(pull_kernel, out_shape=jax.ShapeDtypeStruct((9, 2, 3) + ti...  50.3 us
    pallas_call x1, Pallas kernels, attend_forward(): pl.pallas_call(attend_kernel, out_shape=(jax.ShapeDtypeStruct((9, 2) + ti...  47.2 us
    dot_general x4, local copies, waits for them, and re-layouts, dot(): return jnp.dot(left, right, preferred_element_type=F32)  21 us
    dot_general x2, local copies, waits for them, and re-layouts, per_device(): jnp.einsum('tk,skn->tsn', normed, w_qkv, preferred_element_type=F32)  19 us
    dot_general x1, matrix products, per_device(): jnp.einsum('tk,skn->tsn', normed_two, w_up, preferred_element_type=F32)  17.2 us
    transpose x2, local copies, waits for them, and re-layouts, per_device(): qkv_grad = pairs_in(back).transpose(0, 2, 1, 3).reshape(tokens, 3 * D)  16.1 us

profile of v2, /device:TPU:0, one launch (start us, length us, event | category | flops | bytes accessed | tf_op | source)
XLA Modules:
  0.0 571.3 jit_solution(2350072209402818857)
XLA Ops:
  5.7 109.5 %shard_map.203 = (bf16[8,1088,1088]{2,1,0:T(8,128)(2,1)}, bf16[4,8,144,1088]{3,2,1,0:T(8,128)(2,1)S(1)}) custom-call(bf16[80,1088]{1,0:T(8,128)(2,1)S(1)} %pad.32.a_ref, bf16[144,384]{1,0:T(8,128)(2,1)S(1)} %pad.34.b_ref), custom_call_target="tpu_custom_call" | custom-call | tf_op jit(solution)/shard_map/pallas_call | solution.py:188
  115.2 4.0 copy-done
  121.6 7.6 %slice_bitcast_fusion = bf16[8,408,1088]{1,2,0:T(8,128)(2,1)} fusion(bf16[8,1088,1088]{2,1,0:T(8,128)(2,1)} %get-tuple-element.19), kind=kLoop, calls=%fused_computation.6 | loop fusion | bytes 14204928 | tf_op jit(solution)/shard_map/tk,skn->tsn/dot_general | solution.py:785
  129.2 11.5 %copy.140 = bf16[8,408,1088]{2,1,0:T(8,128)(2,1)} copy(bf16[8,408,1088]{1,2,0:T(8,128)(2,1)} %slice_bitcast_fusion) | data formatting | bytes 14204928 | tf_op jit(solution)/shard_map/tk,skn->tsn/dot_general | solution.py:785
  140.7 5.5 fusion.38
  146.5 1.3 pad.35
  147.8 2.8 copy.143
  150.8 47.2 %shard_map.204 = (bf16[9,2,128,128]{3,2,1,0:T(8,128)(2,1)S(1)}, bf16[8,3,2,128,128]{4,3,2,1,0:T(8,128)(2,1)S(1)}, bf16[8,3,128,128]{3,2,1,0:T(8,128)(2,1)S(1)}) custom-call(bf16[9,3,2,128,128]{4,3,2,1,0:T(8,128)(2,1)S(1)} %bitcast.190, s32[2,3]{1,0:T(2,128)S(1)} %convert_element_type.123.bounds), custom_call_target="tpu_custom_call" | custom-call | tf_op jit(solution)/shard_map/pallas_call | solution.py:342
  199.8 1.4 copy.144
  201.2 2.0 convert_bitcast_fusion
  203.3 7.5 %slice_bitcast_fusion.1 = bf16[8,136,1088]{1,2,0:T(8,128)(2,1)} fusion(bf16[8,1088,1088]{2,1,0:T(8,128)(2,1)} %get-tuple-element.19), kind=kLoop, calls=%fused_computation.30 | loop fusion | bytes 4734976 | tf_op jit(solution)/shard_map/tk,skn->tsn/dot_general | solution.py:792
  210.8 6.2 %copy.146 = bf16[8,136,1088]{2,1,0:T(8,128)(2,1)} copy(bf16[8,136,1088]{1,2,0:T(8,128)(2,1)} %slice_bitcast_fusion.1) | data formatting | bytes 4734976 | tf_op jit(solution)/shard_map/tk,skn->tsn/dot_general | solution.py:792
  217.0 2.6 fusion.69
  221.0 17.2 %fusion.2 = f32[256,8,544]{0,2,1:T(8,128)} fusion(bf16[8,1088,1088]{2,1,0:T(8,128)(2,1)} %get-tuple-element.19, f32[256,1088]{0,1:T(8,128)} %copy-done.14, f32[1088]{0:T(1024)S(1)} %add.177, f32[1088]{0:T(1024)S(1)} %mul.192, f32[256]{0:T(256)S(1)} %add_rsqrt_fusion, f32[256]{0:T(256)S(1)} %broadcast_multiply_fusion.4), kind=kOutput, calls=%fused_computation.2 | convolution fusion | flops 2425700352 | bytes 16722432 | tf_op jit(solution)/shard_map/tk,skn->tsn/dot_general | solution.py:797
  238.2 6.3 %copy.148 = f32[256,4,1088]{2,0,1:T(8,128)} copy(f32[256,4,1088]{0,2,1:T(8,128)} %bitcast.200) | data formatting | bytes 8912896 | tf_op jit(solution)/shard_map/reshape | solution.py:797
  244.7 4.0 fusion.37.act
  248.6 5.3 fusion.67
  259.5 1.4 copy.149
  260.9 2.3 slice.199
  263.3 5.7 %copy.164 = f32[256,8,544]{2,0,1:T(8,128)} copy(f32[256,8,544]{0,2,1:T(8,128)} %fusion.2) | data formatting | bytes 8912896 | tf_op jit(solution)/shard_map/tk,skn->tsn/dot_general | solution.py:797
  269.1 5.2 copy.152
  274.4 4.6 copy.151
  280.3 4.1 fusion.70
  284.3 5.4 copy.154
  289.8 3.9 fusion.71
  293.6 5.2 copy.156
  298.8 3.9 fusion.72
  302.7 5.2 copy.158
  307.9 3.0 fusion.73
  310.9 6.5 %convert_reduce_fusion = (f32[8,544]{1,0:T(8,128)}, bf16[256,8,544]{2,0,1:T(8,128)(2,1)S(1)}) fusion(f32[256,8,544]{2,0,1:T(8,128)} %copy.164, f32[8,544]{1,0:T(8,128)S(1)} %add.192, f32[256,2,544]{2,0,1:T(8,128)S(1)} %fusion.73, f32[256,2,544]{2,0,1:T(8,128)S(1)} %copy-done.29, f32[256,2,544]{2,0,1:T(8,128)S(1)} %copy-done.28, f32[256,2,544]{2,0,1:T(8,128)S(1)} %copy-done.27), kind=kLoop, calls=%fused_computation.18 | loop fusion | flops 28962560 | bytes 11175936 | tf_op jit(solution)/shard_map/reduce_sum | solution.py:831
  317.4 8.4 %fusion.28 = f32[256,1088]{0,1:T(8,128)S(1)} fusion(bf16[256,8,544]{2,0,1:T(8,128)(2,1)S(1)} %get-tuple-element.91, bf16[8,1088,1088]{2,1,0:T(8,128)(2,1)} %get-tuple-element.19), kind=kOutput, calls=%fused_computation.38 | convolution fusion | flops 2424307712 | bytes 14483456 | tf_op jit(solution)/shard_map/tsn,skn->tk/dot_general | solution.py:815
  325.7 2.1 multiply_reduce_fusion
  327.9 4.1 convert_reduce_fusion.3
  332.0 5.9 %fusion.41 = bf16[136,2,8,128]{3,2,1,0:T(8,128)(2,1)S(1)} fusion(bf16[256,8,136]{0,2,1:T(8,128)(2,1)S(1)} %bitcast.220, bf16[8,1088,1088]{2,1,0:T(8,128)(2,1)} %get-tuple-element.19), kind=kOutput, calls=%fused_computation.54 | convolution fusion | flops 606355456 | bytes 5570560 | tf_op jit(solution)/shard_map/tsn,skn->tk/dot_general | solution.py:819
  339.0 50.3 %shard_map.205 = bf16[9,2,3,128,128]{4,3,2,1,0:T(8,128)(2,1)} custom-call(bf16[9,2,128,128]{3,2,1,0:T(8,128)(2,1)S(1)} %bitcast.191, bf16[8,3,2,128,128]{4,3,2,1,0:T(8,128)(2,1)S(1)} %get-tuple-element.21.got, bf16[8,3,128,128]{3,2,1,0:T(8,128)(2,1)S(1)} %copy-done.2, s32[2,3]{1,0:T(2,128)S(1)} %convert_element_type.123.bounds), custom_call_target="tpu_custom_call" | custom-call | tf_op jit(solution)/shard_map/pallas_call | solution.py:463
  389.4 2.8 copy.170
  392.3 16.0 %copy.171 = bf16[2,128,3,1088]{1,0,3,2:T(2,128)(2,1)S(1)} copy(bf16[2,128,3,1088]{1,3,2,0:T(8,128)(2,1)S(1)} %slice_bitcast_fusion.2) | data formatting | bytes 3342336 | tf_op jit(solution)/shard_map/transpose | solution.py:825
  409.4 7.3 %fusion.25 = f32[256,1088]{0,1:T(8,128)S(1)} fusion(bf16[256,8,408]{0,2,1:T(8,128)(2,1)S(1)} %reshape_reshape.7, bf16[8,1088,1088]{2,1,0:T(8,128)(2,1)} %get-tuple-element.19), kind=kOutput, calls=%fused_computation.37 | convolution fusion | flops 1818230784 | bytes 11698176 | tf_op jit(solution)/shard_map/tsn,skn->tk/dot_general | solution.py:827
  416.8 1.5 multiply_reduce_fusion.1
  421.0 3.9 copy.173
  426.2 9.0 %concatenate.33 = bf16[256,8,1088]{2,0,1:T(8,128)(2,1)} concatenate(bf16[256,8,408]{2,0,1:T(8,128)(2,1)} %copy.173, bf16[256,8,136]{2,0,1:T(8,128)(2,1)} %copy.174, bf16[256,8,544]{2,0,1:T(8,128)(2,1)S(1)} %copy-done.10), dimensions={2} | concatenate | bytes 8912896 | tf_op jit(solution)/shard_map/concatenate | solution.py:849
  436.4 2.4 pad_maximum_fusion.1.xt
  438.8 118.9 %shard_map.206 = (f32[80,1088]{1,0:T(8,128)}, f32[144,384]{1,0:T(8,128)}) custom-call(bf16[3,1088,256]{2,1,0:T(8,128)(2,1)} %pad_maximum_fusion.1.xt, bf16[8,256,1088]{2,1,0:T(8,128)(2,1)} %bitcast.199, bf16[8,144,256]{2,1,0:T(8,128)(2,1)} %get-tuple-element.99.tt, bf16[4,256,1088]{2,1,0:T(8,128)(2,1)} %copy-done.7, f32[8,8,1088]{2,1,0:T(8,128)} %pad.39.extra), custom_call_target="tpu_custom_call" | custom-call | tf_op jit(solution)/shard_map/pallas_call | solution.py:698
  557.7 1.7 slice_bitcast_fusion.12
  559.4 1.7 slice.177
  561.1 1.6 slice.175
  564.4 1.4 fusion.68
  567.3 3.0 copy_bitcast_fusion.1
  (155 shorter events, 29.5 us)
Async XLA Ops:
  0.6 119.0 %copy-start.16 = (bf16[2,128,1088]{1,2,0:T(8,128)(2,1)S(1)}, bf16[2,128,1088]{1,2,0:T(8,128)(2,1)}, u32[]{:S(2)}) copy-start(bf16[2,128,1088]{1,2,0:T(8,128)(2,1)} %param.12) | copy-start | bytes 1671172
  115.2 4.0 copy-start
  119.6 1.7 copy-start.33
  198.1 0.9 copy-start.1
  199.0 0.8 copy-start.3
  203.2 13.8 %copy-start.11 = (f32[2,136,8,128]{3,2,1,0:T(8,128)}, f32[2,136,8,128]{3,2,1,0:T(8,128)S(1)}, u32[]{:S(2)}) copy-start(f32[2,136,8,128]{3,2,1,0:T(8,128)S(1)} %get-tuple-element.111) | copy-start | bytes 3342340
  210.8 6.2 %copy-start.23 = (bf16[2,136,8,128]{3,2,1,0:T(8,128)(2,1)S(1)}, bf16[2,136,8,128]{3,2,1,0:T(8,128)(2,1)}, u32[]{:S(2)}) copy-start(bf16[2,136,8,128]{3,2,1,0:T(8,128)(2,1)} %get-tuple-element.112) | copy-start | bytes 1671172
  219.7 1.0 copy-start.14
  248.6 9.8 %copy-start.7 = (bf16[4,256,1088]{2,1,0:T(8,128)(2,1)}, bf16[4,256,1088]{2,1,0:T(8,128)(2,1)S(1)}, u32[]{:S(2)}) copy-start(bf16[4,256,1088]{2,1,0:T(8,128)(2,1)S(1)} %fusion.37.act) | copy-start | bytes 6684676
  254.0 2.3 copy-start.6
  254.0 2.3 copy-start.8
  254.0 3.3 copy-start.5
  254.0 4.4 copy-start.4
  269.1 5.2 copy-start.18
  280.3 4.1 copy-start.30
  284.3 5.4 copy-start.31
  307.9 3.0 copy-start.27
  307.9 3.0 copy-start.28
  307.9 3.0 copy-start.29
  317.4 8.4 %copy-start.9 = (bf16[256,8,544]{2,0,1:T(8,128)(2,1)}, bf16[256,8,544]{2,0,1:T(8,128)(2,1)S(1)}, u32[]{:S(2)}) copy-start(bf16[256,8,544]{2,0,1:T(8,128)(2,1)S(1)} %get-tuple-element.91) | copy-start | bytes 6684676
  317.4 8.4 %copy-start.15 = (f32[256,1088]{0,1:T(8,128)S(1)}, f32[256,1088]{0,1:T(8,128)}, u32[]{:S(2)}) copy-start(f32[256,1088]{0,1:T(8,128)} %copy-done.14) | copy-start | bytes 3342340
  325.7 2.1 copy-start.21
  332.0 5.9 %copy-start.25 = (bf16[256,1088]{0,1:T(8,128)(2,1)}, bf16[256,1088]{0,1:T(8,128)(2,1)S(1)}, u32[]{:S(2)}) copy-start(bf16[256,1088]{0,1:T(8,128)(2,1)S(1)} %get-tuple-element.88) | copy-start | bytes 1671172
  337.9 1.1 copy-start.2
  409.4 7.4 %copy-start.17 = (bf16[256,8,408]{0,2,1:T(8,128)(2,1)}, bf16[256,8,408]{0,2,1:T(8,128)(2,1)S(1)}, u32[]{:S(2)}) copy-start(bf16[256,8,408]{0,2,1:T(8,128)(2,1)S(1)} %reshape_reshape.7) | copy-start | bytes 5013508
  409.4 7.4 %copy-start.12 = (f32[2,136,8,128]{3,2,1,0:T(8,128)S(1)}, f32[2,136,8,128]{3,2,1,0:T(8,128)}, u32[]{:S(2)}) copy-start(f32[2,136,8,128]{3,2,1,0:T(8,128)} %copy-done.11) | copy-start | bytes 3342340
  409.4 7.4 %copy-start.34 = (f32[1088]{0:T(1024)S(1)}, f32[1088]{0:T(1024)}, u32[]{:S(2)}) copy-start(f32[1088]{0:T(1024)} %copy-done.33) | copy-start | bytes 13060
  409.4 7.4 %copy-start.38 = (f32[256]{0:T(256)S(1)}, f32[256]{0:T(256)}, u32[]{:S(2)}) copy-start(f32[256]{0:T(256)} %get-tuple-element.107) | copy-start | bytes 3076
  416.7 1.5 copy-start.20
  418.5 0.9 copy-start.37
  418.5 0.9 copy-start.36
  418.5 1.0 copy-start.35
  418.5 1.1 copy-start.19
  418.7 1.4 copy-start.32
  421.0 3.9 copy-start.26
  421.0 5.2 copy-start.10
  426.2 10.2 %copy-start.22 = (bf16[1,1088,256]{2,1,0:T(8,128)(2,1)S(1)}, bf16[1,1088,256]{2,1,0:T(8,128)(2,1)}, u32[]{:S(2)}) copy-start(bf16[1,1088,256]{2,1,0:T(8,128)(2,1)} %get-tuple-element.97) | copy-start | bytes 1671172
  557.7 9.6 %copy-start.13 = (f32[2,136,8,128]{3,2,1,0:T(8,128)S(1)}, f32[2,136,8,128]{3,2,1,0:T(8,128)}, u32[]{:S(2)}) copy-start(f32[2,136,8,128]{3,2,1,0:T(8,128)} %copy-done.11) | copy-start | bytes 3342340
  567.3 3.0 copy-start.24

commit v3 on v2

--- a/solution.py
+++ b/solution.py
@@ -6,6 +6,7 @@
 from jax.sharding import PartitionSpec as P
 
 D = 1088
+WIDE = 1152
 F32 = jnp.float32
 BF16 = jnp.bfloat16
 MESH = pl.DeviceIdType.MESH
@@ -86,7 +87,7 @@
     zb[me.z] = b_ref[...]
     for copy in first:
         copy.wait_recv()
-    mine_a[...] = merge_rows(za[...].reshape(320, D))
+    mine_a[...] = merge_rows(za[...].reshape(320, WIDE))
     mine_b[...] = merge_columns(zb)
 
     def spot(part, step_x, step_y):
@@ -187,13 +188,13 @@
 def gather_weights(blob_a, blob_b):
     return pl.pallas_call(
         gather_kernel,
-        out_shape=(jax.ShapeDtypeStruct((8, D, D), BF16),
+        out_shape=(jax.ShapeDtypeStruct((8, D, WIDE), BF16),
                    jax.ShapeDtypeStruct((4, 8, B_ROWS, D), BF16)),
         in_specs=[pl.BlockSpec(memory_space=pltpu.VMEM)] * 2,
         out_specs=(pl.BlockSpec(memory_space=pl.ANY),) * 2,
         scratch_shapes=[
-            pltpu.VMEM((4, 80, D), BF16), pltpu.VMEM((4, B_ROWS, 384), BF16),
-            pltpu.VMEM((A_ROWS, D), BF16), pltpu.VMEM((B_ROWS, D), BF16),
+            pltpu.VMEM((4, 80, WIDE), BF16), pltpu.VMEM((4, B_ROWS, 384), BF16),
+            pltpu.VMEM((A_ROWS, WIDE), BF16), pltpu.VMEM((B_ROWS, D), BF16),
             pltpu.SemaphoreType.DMA((GATHER_COPIES,)), pltpu.SemaphoreType.DMA((GATHER_COPIES,)),
             pltpu.SemaphoreType.DMA((2,)),
         ],
@@ -203,6 +204,68 @@
 
 
 NT = (((1,), (1,)), ((), ()))
+
+
+def normalize(values):
+    center = values - jnp.mean(values, axis=-1, keepdims=True)
+    spread = jnp.mean(center * center, axis=-1, keepdims=True)
+    scale = lax.rsqrt(spread + 1e-05)
+    return center * scale, scale
+
+
+def norm_pull(grad, gain, unit, scale):
+    scaled = grad * gain
+    return scale * (
+        scaled
+        - jnp.mean(scaled, axis=-1, keepdims=True)
+        - unit * jnp.mean(scaled * unit, axis=-1, keepdims=True)
+    )
+
+
+def dot(left, right):
+    return jnp.dot(left, right, preferred_element_type=F32)
+
+
+def dot_t(left, right):
+    return lax.dot_general(left, right, NT, preferred_element_type=F32)
+
+
+def widen(value):
+    return jnp.concatenate([value, jnp.zeros((value.shape[0], WIDE - D), value.dtype)], axis=1)
+
+
+def shift_lanes(tiles, value, source, width, target):
+    turn = (target - source) % 128
+    low, high = source // 128, -(-(source + width) // 128)
+    part = value[:, low * 128 : high * 128]
+    if turn:
+        part = jnp.concatenate([part, jnp.zeros((part.shape[0], 128), part.dtype)], axis=1)
+        part = pltpu.roll(part, turn, 1)
+    start = source - low * 128 + turn
+    for spot in range(start // 128, -(-(start + width) // 128)):
+        tile = part[:, spot * 128 : spot * 128 + 128]
+        first, last = start - spot * 128, start + width - spot * 128
+        if first > 0 or last < 128:
+            lane = lax.broadcasted_iota(jnp.int32, tile.shape, 1)
+            tile = jnp.where((lane >= first) & (lane < last), tile, 0.0)
+        place = (target - start) // 128 + spot
+        tiles[place] = tiles[place] + tile if place in tiles else tile
+
+
+def join_tiles(tiles, count):
+    rows = tiles[0].shape[0]
+    empty = jnp.zeros((rows, 128), F32)
+    return jnp.concatenate([tiles.get(k, empty) for k in range(count)], axis=1)
+
+
+def segments():
+    found = []
+    for s in range(8):
+        for kind in range(3):
+            low, high = max(408 * s, D * kind), min(408 * s + 408, D * kind + D)
+            if low < high:
+                found.append((s, low - 408 * s, high - low, kind, low - D * kind))
+    return found
 
 
 class Group:
@@ -262,8 +325,36 @@
         store(block, whole.T.astype(BF16).reshape(2, 128, 128))
 
 
-def attend_kernel(pack, bounds, att, got, got8, out, out8, in_sems, in8_sems, back_sems, back8_sems):
+def fetch_blocks(ga, held, sems, low, width):
+    copies = [pltpu.make_async_copy(ga.at[s, :, pl.ds(low, width)], held.at[s], sems.at[s])
+              for s in range(8)]
+    for copy in copies:
+        copy.start()
+    return copies
+
+
+def attend_kernel(hidden, lines, ga, bounds, att, got, got8, normed_t, weights, pack, out, out8,
+                  weight_sems, in_sems, in8_sems, back_sems, back8_sems):
     g = Group()
+    copies = fetch_blocks(ga, weights, weight_sems, 0, 512)
+    unit, _ = normalize(hidden[...].astype(F32).reshape(256, D))
+    normed = unit * lines[0:1, :D] + lines[2:3, :D]
+    normed_t[...] = normed.T.astype(BF16)
+    normed = normed.astype(BF16)
+    tiles = ({}, {}, {})
+    blocks = []
+    for s in range(8):
+        copies[s].wait()
+        blocks.append(dot(normed, weights[s]))
+        for seg, low, width, kind, spot in segments():
+            if seg == s:
+                shift_lanes(tiles[kind], blocks[s], low, width, spot)
+    for kind, row in ((0, 4), (1, None), (2, 5)):
+        for p in range(9):
+            tile = tiles[kind][p]
+            if row is not None:
+                tile = tile + lines[row : row + 1, 128 * p : 128 * p + 128]
+            pack[p, kind] = tile.astype(BF16).reshape(2, 128, 128)
     greet([g.peer(g.other(step)) for step in range(1, 8)])
 
     def in_copy(step):
@@ -336,23 +427,26 @@
             back_copy(seq, step).wait_send()
 
 
-def attend_forward(pack, bounds):
+def attend_forward(hidden, lines, ga, bounds):
     tile = (128, 128)
     vmem = pltpu.VMEM
     return pl.pallas_call(
         attend_kernel,
         out_shape=(jax.ShapeDtypeStruct((9, 2) + tile, BF16),
                    jax.ShapeDtypeStruct((8, 3, 2) + tile, BF16),
-                   jax.ShapeDtypeStruct((8, 3) + tile, BF16)),
-        in_specs=[pl.BlockSpec(memory_space=vmem), pl.BlockSpec(memory_space=pltpu.SMEM)],
-        out_specs=(pl.BlockSpec(memory_space=vmem),) * 3,
+                   jax.ShapeDtypeStruct((8, 3) + tile, BF16),
+                   jax.ShapeDtypeStruct((D, 256), BF16)),
+        in_specs=[pl.BlockSpec(memory_space=vmem)] * 2 + [
+            pl.BlockSpec(memory_space=pl.ANY), pl.BlockSpec(memory_space=pltpu.SMEM)],
+        out_specs=(pl.BlockSpec(memory_space=vmem),) * 4,
         scratch_shapes=[
-            vmem((8, 2) + tile, BF16), vmem((8,) + tile, BF16),
+            vmem((8, D, 512), BF16), vmem((9, 3, 2) + tile, BF16), vmem((8, 2) + tile, BF16), vmem((8,) + tile, BF16),
+            pltpu.SemaphoreType.DMA((8,)),
             pltpu.SemaphoreType.DMA((2, 7)), pltpu.SemaphoreType.DMA((10,)),
             pltpu.SemaphoreType.DMA((2, 2, 7)), pltpu.SemaphoreType.DMA((9,))],
         compiler_params=pltpu.CompilerParams(
-            collective_id=1, has_side_effects=True, vmem_limit_bytes=40 * 2**20),
-    )(pack, bounds)
+            collective_id=1, has_side_effects=True, vmem_limit_bytes=56 * 2**20),
+    )(hidden, lines, ga, bounds)
 
 
 def attend_pull(queries, keys, values, grads, bounds, seq, heads, key_sum, value_sum, store):
@@ -380,9 +474,11 @@
             store(kind, block, total[block * 256 : block * 256 + 256].astype(BF16).reshape(2, 128, 128))
 
 
-def pull_kernel(pack, got, got8, bounds, back, grad, grad8, out, out8, key_sum, value_sum,
-                in_sems, in8_sems, back_sems, back8_sems):
+def pull_kernel(pack, got, got8, hidden, middle_grad, lines, ga, bounds, placed, input_grad, sums,
+                weights, back, grad, grad8, out, out8, key_sum, value_sum,
+                weight_sems, in_sems, in8_sems, back_sems, back8_sems):
     g = Group()
+    copies = fetch_blocks(ga, weights, weight_sems, 0, 512)
     greet([g.peer(g.other(step)) for step in range(1, 8)])
 
     def in_copy(step):
@@ -456,27 +552,167 @@
             back_copy(seq, step).wait_recv()
             back_copy(seq, step).wait_send()
 
-
-def attend_backward(pack, got, got8, bounds):
+    natural = [jnp.concatenate([back[p, :, kind].reshape(256, 128) for p in range(9)],
+                               axis=1).astype(F32) for kind in range(3)]
+    total = None
+    for s in range(8):
+        tiles = {}
+        for seg, low, width, kind, spot in segments():
+            if seg == s:
+                shift_lanes(tiles, natural[kind], spot, width, low)
+        block = join_tiles(tiles, 4).astype(BF16)
+        placed[s] = block
+        copies[s].wait()
+        term = dot_t(block, weights[s])
+        total = term if total is None else total + term
+    unit, scale = normalize(hidden[...].astype(F32).reshape(256, D))
+    input_grad[...] = middle_grad[...] + norm_pull(total, lines[0:1, :D], unit, scale)
+    sums[0:1] = jnp.sum(widen(total * unit), axis=0, keepdims=True)
+    sums[1:2] = jnp.sum(widen(total), axis=0, keepdims=True)
+    sums[2:3] = jnp.sum(natural[0], axis=0, keepdims=True)
+    sums[3:4] = jnp.sum(natural[2], axis=0, keepdims=True)
+    sums[4:8] = jnp.zeros((4, WIDE), F32)
+
+
+def attend_backward(pack, got, got8, hidden, middle_grad, lines, ga, bounds):
     tile = (128, 128)
     vmem = pltpu.VMEM
     return pl.pallas_call(
         pull_kernel,
-        out_shape=jax.ShapeDtypeStruct((9, 2, 3) + tile, BF16),
-        in_specs=[pl.BlockSpec(memory_space=vmem)] * 3 + [pl.BlockSpec(memory_space=pltpu.SMEM)],
-        out_specs=pl.BlockSpec(memory_space=vmem),
+        out_shape=(jax.ShapeDtypeStruct((8, 256, 512), BF16),
+                   jax.ShapeDtypeStruct((256, D), F32), jax.ShapeDtypeStruct((8, WIDE), F32)),
+        in_specs=[pl.BlockSpec(memory_space=vmem)] * 6 + [
+            pl.BlockSpec(memory_space=pl.ANY), pl.BlockSpec(memory_space=pltpu.SMEM)],
+        out_specs=(pl.BlockSpec(memory_space=vmem),) * 3,
         scratch_shapes=[
-            vmem((8, 2) + tile, BF16), vmem((8,) + tile, BF16),
+            vmem((8, D, 512), BF16), vmem((9, 2, 3) + tile, BF16), vmem((8, 2) + tile, BF16), vmem((8,) + tile, BF16),
             vmem((8, 2, 3) + tile, BF16), vmem((8, 3) + tile, BF16),
             vmem((1024, 128), F32), vmem((1024, 128), F32),
+            pltpu.SemaphoreType.DMA((8,)),
             pltpu.SemaphoreType.DMA((2, 7)), pltpu.SemaphoreType.DMA((10,)),
             pltpu.SemaphoreType.DMA((2, 2, 7)), pltpu.SemaphoreType.DMA((9,))],
         compiler_params=pltpu.CompilerParams(
-            collective_id=2, has_side_effects=True, vmem_limit_bytes=50 * 2**20),
-    )(pack, got, got8, bounds)
-
-
-def reduce_kernel(xt, yb, tt, act, extra, out_a, out_b,
+            collective_id=2, has_side_effects=True, vmem_limit_bytes=60 * 2**20),
+    )(pack, got, got8, hidden, middle_grad, lines, ga, bounds)
+
+
+def middle_kernel(att, hidden, top, top_pad, lines, up_row, ga, gb,
+                  layer_out, middle_grad, att_grad, att_t, normed_t, active, y_o, y_u, sums, up_sums,
+                  held_o, held_u, held_b, normed, down_sum, norm_grad, sems_o, sems_u, sems_b):
+    copies_o = [pltpu.make_async_copy(ga.at[s, :, pl.ds(384, 256)], held_o.at[s], sems_o.at[s])
+                for s in range(8)]
+    for copy in copies_o:
+        copy.start()
+
+    def up_copy(s):
+        return pltpu.make_async_copy(ga.at[s, :, pl.ds(512, 640)], held_u.at[s], sems_u.at[s])
+
+    def down_copy(y):
+        return pltpu.make_async_copy(gb.at[y], held_b.at[y], sems_b.at[y])
+
+    for y in range(4):
+        up_copy(2 * y).start()
+        up_copy(2 * y + 1).start()
+        down_copy(y).start()
+
+    attended = jnp.concatenate([att[p].reshape(256, 128) for p in range(9)], axis=1)
+    att_t[...] = attended.astype(F32).T[:D].astype(BF16)
+    tiles = {}
+    for s in range(8):
+        copies_o[s].wait()
+        shift_lanes(tiles, dot(attended[:, :D], held_o[s]), 24, 136, 136 * s)
+    branch = join_tiles(tiles, 9)[:, :D]
+    middle = hidden[...].astype(F32).reshape(256, D) + branch + lines[6:7, :D]
+    unit, scale = normalize(middle)
+    value = unit * lines[1:2, :D] + lines[3:4, :D]
+    normed[...] = value.astype(BF16)
+    normed_t[...] = value.T.astype(BF16)
+    down_sum[...] = jnp.zeros_like(down_sum)
+    norm_grad[...] = jnp.zeros_like(norm_grad)
+
+    def step(y, carry):
+        tiles = {}
+        for odd in (0, 1):
+            up_copy(2 * y + odd).wait()
+            shift_lanes(tiles, dot(normed[...], held_u[2 * y + odd]), 32, 544, 544 * odd)
+        pre = join_tiles(tiles, 9)[:, :D] + up_row[y]
+        cube = 0.7978845608028654 * (pre + 0.044715 * (pre * pre * pre))
+        bend = jnp.tanh(cube)
+        half = 0.5 * (1.0 + bend)
+        acts = (pre * half).astype(BF16)
+        slope = half + 0.5 * pre * (1.0 - bend * bend) * (
+            0.7978845608028654 * (1.0 + 3 * 0.044715 * (pre * pre)))
+        active[y] = acts
+        down_copy(y).wait()
+        weights = held_b[y].reshape(8 * B_ROWS, D)
+        down_sum[...] += dot_t(acts, weights)
+        inner = dot(top_pad[...], weights) * slope
+        inner = widen(inner.astype(BF16).astype(F32))
+        total = None
+        for odd in (0, 1):
+            tiles = {}
+            shift_lanes(tiles, inner, 544 * odd, 544, 32)
+            block = join_tiles(tiles, 5)
+            up_sums[2 * y + odd] = jnp.sum(block, axis=0, keepdims=True)
+            block = block.astype(BF16)
+            y_u[2 * y + odd] = block
+            term = dot_t(block, held_u[2 * y + odd])
+            total = term if total is None else total + term
+        norm_grad[...] += total
+        return carry
+
+    lax.fori_loop(0, 4, step, 0)
+    tiles = {}
+    down = down_sum[...]
+    for s in range(8):
+        shift_lanes(tiles, down, 144 * s, 136, 136 * s)
+    out = middle + join_tiles(tiles, 9)[:, :D] + lines[7:8, :D]
+    layer_out[...] = out.astype(BF16).reshape(2, 128, D)
+    grad = norm_grad[...]
+    cotangent = top[...].astype(F32).reshape(256, D)
+    total = cotangent + norm_pull(grad, lines[1:2, :D], unit, scale)
+    middle_grad[...] = total
+    branch = widen(total.astype(BF16).astype(F32))
+    back = None
+    for s in range(8):
+        tiles = {}
+        shift_lanes(tiles, branch, 136 * s, 136, 24)
+        block = join_tiles(tiles, 2).astype(BF16)
+        y_o[s] = block
+        term = dot_t(block, held_o[s])
+        back = term if back is None else back + term
+    back = widen(back).astype(BF16)
+    for p in range(9):
+        att_grad[p] = back[:, 128 * p : 128 * p + 128].reshape(2, 128, 128)
+    sums[0:1] = jnp.sum(widen(grad * unit), axis=0, keepdims=True)
+    sums[1:2] = jnp.sum(widen(grad), axis=0, keepdims=True)
+    sums[2:3] = jnp.sum(branch, axis=0, keepdims=True)
+    sums[3:4] = jnp.sum(widen(cotangent), axis=0, keepdims=True)
+    sums[4:8] = jnp.zeros((4, WIDE), F32)
+
+
+def middle_block(*operands):
+    vmem = pltpu.VMEM
+    shape = jax.ShapeDtypeStruct
+    return pl.pallas_call(
+        middle_kernel,
+        out_shape=(
+            shape((2, 128, D), BF16), shape((256, D), F32), shape((9, 2, 128, 128), BF16),
+            shape((D, 256), BF16), shape((D, 256), BF16), shape((4, 256, D), BF16),
+            shape((8, 256, 256), BF16), shape((8, 256, 640), BF16), shape((8, WIDE), F32),
+            shape((8, 1, 640), F32)),
+        in_specs=[pl.BlockSpec(memory_space=vmem)] * 6 + [pl.BlockSpec(memory_space=pl.ANY)] * 2,
+        out_specs=(pl.BlockSpec(memory_space=vmem),) * 10,
+        scratch_shapes=[
+            vmem((8, D, 256), BF16), vmem((8, D, 640), BF16), vmem((4, 8, B_ROWS, D), BF16),
+            vmem((256, D), BF16), vmem((256, WIDE), F32), vmem((256, D), F32),
+            pltpu.SemaphoreType.DMA((8,)), pltpu.SemaphoreType.DMA((8,)),
+            pltpu.SemaphoreType.DMA((4,))],
+        compiler_params=pltpu.CompilerParams(vmem_limit_bytes=62 * 2**20),
+    )(*operands)
+
+
+def reduce_kernel(x_q, x_o, x_u, y_q, y_o, y_u, tt, act, extra, out_a, out_b,
                   sib_out1, sib_out2, sib_in1, sib_in2,
                   in_opp1, in_opp2, in_side1, in_side2,
                   acc1, acc2, end1, end2, in_end1, in_end2, in_mid1, in_mid2,
@@ -491,15 +727,12 @@
         return outer(column, rows)
 
     def outer(column, rows):
-        one = jnp.dot(xt[0, rows], yb[column, :, 0:512], preferred_element_type=F32)
-        two = jnp.dot(xt[1, rows], yb[column, :, 384:640], preferred_element_type=F32)
-        three = jnp.dot(xt[2, rows], yb[column, :, 512:], preferred_element_type=F32)
-        lane = lax.broadcasted_iota(jnp.int32, (one.shape[0], 128), 1)
+        one = dot(x_q[rows], y_q[column])
+        two = dot(x_o[rows], y_o[column])
+        three = dot(x_u[rows], y_u[column])
         return jnp.concatenate([
-            one[:, :384],
-            jnp.where(lane < 24, one[:, 384:512], two[:, :128]),
-            jnp.where(lane < 32, two[:, 128:], three[:, :128]),
-            three[:, 128:]], axis=1)
+            one[:, :384], one[:, 384:] + two[:, :128], two[:, 128:] + three[:, :128],
+            three[:, 128:576]], axis=1)
 
     def part2(xb, yy, parity):
         column = 2 * xb + parity
@@ -691,14 +924,14 @@
             c.wait_send()
 
 
-def reduce_weights(xt, yb, tt, act, extra):
+def reduce_weights(*operands):
     half = (CUT, D)
     vmem = pltpu.VMEM
     pair = lambda *lead: [vmem(lead + half, BF16), vmem(lead + half, BF16)]
     return pl.pallas_call(
         reduce_kernel,
         out_shape=(jax.ShapeDtypeStruct((80, D), F32), jax.ShapeDtypeStruct((B_ROWS, 384), F32)),
-        in_specs=[pl.BlockSpec(memory_space=vmem)] * 5,
+        in_specs=[pl.BlockSpec(memory_space=vmem)] * 9,
         out_specs=(pl.BlockSpec(memory_space=vmem),) * 2,
         scratch_shapes=(
             pair(4) + pair(4, 4) + pair(4) + pair(2, 4)
@@ -709,45 +942,7 @@
                pltpu.SemaphoreType.DMA((2, 2, 2)), pltpu.SemaphoreType.DMA((2, 2, 3))]),
         compiler_params=pltpu.CompilerParams(
             collective_id=3, has_side_effects=True, vmem_limit_bytes=63 * 2**20),
-    )(xt, yb, tt, act, extra)
-
-
-HEADS = 17
-FF = 4352
-
-
-def normalize(values):
-    center = values - jnp.mean(values, axis=-1, keepdims=True)
-    spread = jnp.mean(center * center, axis=-1, keepdims=True)
-    scale = lax.rsqrt(spread + 1e-05)
-    return center * scale, scale
-
-
-def norm_pull(grad, gain, unit, scale):
-    scaled = grad * gain
-    return scale * (
-        scaled
-        - jnp.mean(scaled, axis=-1, keepdims=True)
-        - unit * jnp.mean(scaled * unit, axis=-1, keepdims=True)
-    )
-
-
-def gelu_tanh(values):
-    return jax.nn.gelu(values, approximate=True)
-
-
-def dot(left, right):
-    return jnp.dot(left, right, preferred_element_type=F32)
-
-
-def pairs_out(rows):
-    rows = jnp.pad(rows, [(0, 0)] * (rows.ndim - 1) + [(0, 64)])
-    return jnp.moveaxis(rows.reshape(rows.shape[:-1] + (9, 128)), -2, 0)
-
-
-def pairs_in(packed):
-    rows = jnp.moveaxis(packed, 0, -2)
-    return rows.reshape(rows.shape[:-2] + (1152,))[..., :D]
+    )(*operands)
 
 
 def per_device(
@@ -759,7 +954,7 @@
     batch = lax.axis_index("batch")
 
     blob_a = jnp.concatenate([qkv_weight, out_weight, up_weight], axis=1)
-    blob_a = jnp.pad(blob_a, ((0, 12), (0, 0)))
+    blob_a = jnp.pad(blob_a, ((0, 12), (0, WIDE - D)))
     counts = jnp.sum(segment_ids[:, :, None] < jnp.arange(1, 4)[None, None, :], axis=1)
     counts = jnp.pad(counts.astype(BF16).reshape(1, 6), ((0, 3), (0, 130)))
     vec = jnp.concatenate([norm_gains, norm_shifts, qv_bias, proj_bias], axis=0)
@@ -771,85 +966,31 @@
     whole_a, whole_b = gather_weights(blob_a, blob_b)
     vec = lax.dynamic_slice(whole_b, (batch // 4, 0, 136, 272 * (batch % 4)), (1, 8, 8, 272))
     vec = vec[0].astype(F32)
-    lines = vec[:, :, :136].transpose(1, 0, 2).reshape(8, D)
-    gains, shifts, qv_rows, proj_rows = lines[0:2], lines[2:4], lines[4:6], lines[6:8]
-    up_row = vec[:, :4, 136:].reshape(FF)
+    lines = jnp.pad(vec[:, :, :136].transpose(1, 0, 2).reshape(8, D), ((0, 0), (0, WIDE - D)))
+    up_row = vec[:, :4, 136:].reshape(4, 1, D)
     bounds = jnp.sum(vec[:, 4, 136:142], axis=0).astype(jnp.int32).reshape(2, 3)
-    w_qkv, w_out, w_up = whole_a[:, :, :408], whole_a[:, :, 408:544], whole_a[:, :, 544:]
-
-    hidden = inputs.reshape(tokens, D).astype(F32)
-    top_grad = out_grad.reshape(tokens, D)
-    cotangent = top_grad.astype(F32)
-    unit_one, scale_one = normalize(hidden)
-    normed = (unit_one * gains[0] + shifts[0]).astype(BF16)
-    projected = jnp.einsum("tk,skn->tsn", normed, w_qkv, preferred_element_type=F32).reshape(
-        tokens, 3, D
+
+    top_blocks = jnp.pad(out_grad.reshape(tokens, 8, 136), ((0, 0), (0, 0), (0, 8)))
+    top_pad = top_blocks.reshape(tokens, 8 * B_ROWS)
+    top_t = top_pad.T.reshape(8, B_ROWS, tokens)
+
+    att, got, got8, normed_t = attend_forward(inputs, lines, whole_a, bounds)
+    (layer_out, middle_grad, att_grad, att_t, normed_two_t, active, y_o, y_u, sums, up_sums) = (
+        middle_block(att, inputs, out_grad, top_pad, lines, up_row, whole_a, whole_b)
     )
-    shift = jnp.stack([qv_rows[0], jnp.zeros((D,), F32), qv_rows[1]])
-    projected = (projected + shift).astype(BF16).reshape(seqs, rows, 3, D).transpose(2, 0, 1, 3)
-    att, got, got8 = attend_forward(pairs_out(projected), bounds)
-    attended = pairs_in(att).reshape(tokens, D)
-    branch = jnp.einsum("tk,skn->tsn", attended, w_out, preferred_element_type=F32)
-    middle = hidden + branch.reshape(tokens, D) + proj_rows[0]
-    unit_two, scale_two = normalize(middle)
-    normed_two = (unit_two * gains[1] + shifts[1]).astype(BF16)
-    inner_pre = (
-        jnp.einsum("tk,skn->tsn", normed_two, w_up, preferred_element_type=F32).reshape(tokens, FF)
-        + up_row
+    y_q, input_grad, more_sums = attend_backward(
+        att_grad, got, got8, inputs, middle_grad, lines, whole_a, bounds
     )
-    active, gelu_pull = jax.vjp(gelu_tanh, inner_pre)
-    active = active.astype(BF16).reshape(tokens, 4, D).transpose(1, 0, 2)
-    downs = whole_b.reshape(4, 8 * B_ROWS, D)
-    branch = sum(
-        lax.dot_general(active[y], downs[y], (((1,), (1,)), ((), ())), preferred_element_type=F32)
-        for y in range(4)
-    )
-    branch = branch.reshape(tokens, 8, B_ROWS)[:, :, :136].reshape(tokens, D)
-    layer_out = (middle + branch + proj_rows[1]).astype(BF16)
-
-    top_blocks = jnp.pad(top_grad.reshape(tokens, 8, 136), ((0, 0), (0, 0), (0, 8)))
-    top_pad = top_blocks.reshape(tokens, 8 * B_ROWS)
-    down_in = jnp.concatenate([dot(top_pad, downs[y]) for y in range(4)], axis=1)
-    inner_grad = gelu_pull(down_in)[0].astype(BF16)
-    inner_blocks = inner_grad.reshape(tokens, 8, 544)
-    normed_two_grad = jnp.einsum("tsn,skn->tk", inner_blocks, w_up, preferred_element_type=F32)
-    middle_grad = cotangent + norm_pull(normed_two_grad, gains[1], unit_two, scale_two)
-    branch_grad = middle_grad.astype(BF16)
-    branch_blocks = branch_grad.reshape(tokens, 8, 136)
-    attended_grad = jnp.einsum(
-        "tsn,skn->tk", branch_blocks, w_out, preferred_element_type=F32
-    ).astype(BF16)
-    back = attend_backward(
-        pairs_out(attended_grad.reshape(seqs, rows, D)), got, got8, bounds
-    )
-    qkv_grad = pairs_in(back).transpose(0, 2, 1, 3).reshape(tokens, 3 * D)
-    qkv_blocks = qkv_grad.reshape(tokens, 8, 408)
-    normed_grad = jnp.einsum("tsn,skn->tk", qkv_blocks, w_qkv, preferred_element_type=F32)
-    input_grad = middle_grad + norm_pull(normed_grad, gains[0], unit_one, scale_one)
-
-    def column_sum(values):
-        return jnp.sum(values, axis=0, dtype=F32)
-
-    sums = jnp.stack(
-        [
-            column_sum(normed_grad * unit_one),
-            column_sum(normed_two_grad * unit_two),
-            column_sum(normed_grad),
-            column_sum(normed_two_grad),
-            column_sum(qkv_grad[:, :D]),
-            column_sum(qkv_grad[:, 2 * D :]),
-            column_sum(branch_grad),
-            column_sum(top_grad),
-        ]
-    ).reshape(8, 8, 136)
-    up_sums = jnp.pad(column_sum(inner_grad).reshape(8, 4, 136), ((0, 0), (0, 4), (0, 0)))
+    sums = jnp.stack([more_sums[0], sums[0], more_sums[1], sums[1], more_sums[2], more_sums[3],
+                      sums[2], sums[3]])[:, :D].reshape(8, 8, 136)
+    up_sums = jnp.pad(up_sums[:, 0, 32:576].reshape(8, 4, 136), ((0, 0), (0, 4), (0, 0)))
     extra = jnp.concatenate([sums.transpose(1, 0, 2), up_sums], axis=2)
     extra = jnp.pad(extra, ((0, 0), (0, 0), (0, D - 272)))
-    left = jnp.stack([normed.T, attended.T, normed_two.T])
-    right = jnp.concatenate([qkv_blocks, branch_blocks, inner_blocks], axis=2).transpose(1, 0, 2)
-    out_a, out_b = reduce_weights(left, right, top_blocks.transpose(1, 2, 0), active, extra)
+    out_a, out_b = reduce_weights(
+        normed_t, att_t, normed_two_t, y_q, y_o, y_u, top_t, active, extra
+    )
     return (
-        layer_out.reshape(seqs, rows, D),
+        layer_out,
         input_grad.reshape(seqs, rows, D),
         out_a[:68, :408],
         out_a[:68, 408:544],

time: 581 us -> 422 us (0.73)
  the two profiles are of different devices: /device:TPU:0 before, /device:TPU:1 now
where the time goes in v3:
time: 422 us; the launch traced here: 414 us
  Pallas kernels  378 us (90%)
  local copies, waits for them, and re-layouts  32 us (8%)
    pallas_call x1, Pallas kernels, reduce_weights(): pl.pallas_call(reduce_kernel, out_shape=(jax.ShapeDtypeStruct((80, D), F3...  118 us
    pallas_call x1, Pallas kernels, gather_weights(): pl.pallas_call(gather_kernel, out_shape=(jax.ShapeDtypeStruct((8, D, WIDE...  111 us
    pallas_call x1, Pallas kernels, attend_backward(): pl.pallas_call(pull_kernel, out_shape=(jax.ShapeDtypeStruct((8, 256, 512)...  57.8 us
    pallas_call x1, Pallas kernels, attend_forward(): pl.pallas_call(attend_kernel, out_shape=(jax.ShapeDtypeStruct((9, 2) + ti...  55.6 us
    pallas_call x1, Pallas kernels, middle_block(): pl.pallas_call(middle_kernel, out_shape=(shape((2, 128, D), BF16), shape(...  35.3 us
    unnamed x22, local copies, waits for them, and re-layouts  16.3 us

profile of v3, /device:TPU:1, one launch (start us, length us, event | category | flops | bytes accessed | tf_op | source)
XLA Modules:
  0.0 414.1 jit_solution(5915230000924322643)
XLA Ops:
  0.6 0.0 copy-start.1
  0.7 1.0 fusion.6
  1.7 0.1 copy.71
  1.8 0.1 convert_element_type.45
  1.9 0.7 reduce.1
  2.6 0.1 reshape.71
  2.7 0.9 copy.58
  3.6 1.1 fusion.5
  4.6 1.1 concatenate.18
  5.7 4.7 %copy.62 = bf16[2,128,1088]{1,0,2:T(2,128)(2,1)S(1)} copy(bf16[2,128,1088]{1,2,0:T(8,128)(2,1)} %param.13) | data formatting | bytes 1114112 | tf_op args[1]
  10.5 0.4 reshape.73
  10.8 1.1 copy.61.hidden
  11.9 1.1 copy.64.top
  13.0 0.9 pad_bitcast_fusion
  13.9 1.1 copy.65.top_pad
  14.9 110.8 %shard_map.203 = (bf16[8,1088,1152]{2,1,0:T(8,128)(2,1)}, bf16[4,8,144,1088]{3,2,1,0:T(8,128)(2,1)S(1)}) custom-call(bf16[80,1152]{1,0:T(8,128)(2,1)S(1)} %pad.28.a_ref, bf16[144,384]{1,0:T(8,128)(2,1)S(1)} %pad.30.b_ref), custom_call_target="tpu_custom_call" | custom-call | tf_op jit(solution)/shard_map/pallas_call | solution.py:189
  125.8 4.0 copy-done
  129.8 0.1 bitcast_convert_fusion
  129.9 0.1 slice_reduce_fusion.1
  130.0 0.6 convert_element_type.49.bounds
  130.6 0.1 slice.86
  130.7 0.7 reshape.75.up_row
  131.5 0.1 reshape.72
  131.6 0.6 pad.31.lines
  132.2 55.6 %shard_map.204 = (bf16[9,2,128,128]{3,2,1,0:T(8,128)(2,1)}, bf16[8,3,2,128,128]{4,3,2,1,0:T(8,128)(2,1)}, bf16[8,3,128,128]{3,2,1,0:T(8,128)(2,1)}, bf16[1088,256]{1,0:T(8,128)(2,1)}) custom-call(bf16[2,128,1088]{2,1,0:T(8,128)(2,1)} %copy.61.hidden, f32[8,1152]{1,0:T(8,128)} %pad.31.lines, bf16[8,1088,1152]{2,1,0:T(8,128)(2,1)} %get-tuple-element.33.ga, ...), custom_call_target="tpu_custom_call" | custom-call | tf_op jit(solution)/shard_map/pallas_call | solution.py:433
  187.8 35.3 %shard_map.205 = (bf16[2,128,1088]{2,1,0:T(8,128)(2,1)}, f32[256,1088]{1,0:T(8,128)}, bf16[9,2,128,128]{3,2,1,0:T(8,128)(2,1)}, bf16[1088,256]{1,0:T(8,128)(2,1)...) custom-call(bf16[9,2,128,128]{3,2,1,0:T(8,128)(2,1)} %get-tuple-elem, ...), custom_call_target="tpu_custom_call" | custom-call | tf_op jit(solution)/shard_map/pallas_call | solution.py:697
  223.1 57.8 %shard_map.206 = (bf16[8,256,512]{2,1,0:T(8,128)(2,1)}, f32[256,1088]{1,0:T(8,128)}, f32[8,1152]{1,0:T(8,128)}) custom-call(bf16[9,2,128,128]{3,2,1,0:T(8,128)(2,1)} %get-tuple-element.36.pack, bf16[8,3,2,128,128]{4,3,2,1,0:T(8,128)(2,1)} %get-tuple-element.37.got, bf16[8,3,128,128]{3,2,1,0:T(8,128)(2,1)} %get-tuple-element.38.got8, ...), custom_call_target="tpu_custom_call" | custom-call | tf_op jit(solution)/shard_map/pallas_call | solution.py:580
  280.9 0.0 copy-start.6
  280.9 0.0 copy-start.5
  280.9 0.0 copy-start.4
  281.0 1.1 copy.68
  282.0 2.6 copy.69
  284.7 0.0 copy-done.5
  284.7 0.1 stack.4
  284.8 0.1 slice_reduce_fusion
  284.9 0.1 reshape_squeeze.3
  285.0 0.1 reshape.78
  285.1 0.1 select_maximum_fusion
  285.2 0.7 pad.34.extra
  285.9 118.2 %shard_map.207 = (f32[80,1088]{1,0:T(8,128)}, f32[144,384]{1,0:T(8,128)}) custom-call(bf16[1088,256]{1,0:T(8,128)(2,1)} %get-tuple-element.41.x_q, bf16[1088,256]{1,0:T(8,128)(2,1)} %get-tuple-element.42.x_o, bf16[1088,256]{1,0:T(8,128)(2,1)} %get-tuple-element.43.x_u, bf16[8,256,512]{2,1,0:T(8,128)(2,1)} %get-tuple-element.44.y_q, ...), custom_call_target="tpu_custom_call" | custom-call | tf_op jit(solution)/shard_map/pallas_call | solution.py:931
  404.2 0.8 slice.83
  404.9 0.7 reshape.79
  405.6 1.4 fusion.7
  407.0 1.6 slice_bitcast_fusion
  408.7 1.0 slice.76
  409.6 0.7 copy.70
  410.4 1.6 slice.75
  412.0 1.7 slice.77
  (19 shorter events, 0.2 us)
Async XLA Ops:
  0.6 11.3 %copy-start.1 = (bf16[2,128,1088]{1,2,0:T(8,128)(2,1)S(1)}, bf16[2,128,1088]{1,2,0:T(8,128)(2,1)}, u32[]{:S(2)}) copy-start(bf16[2,128,1088]{1,2,0:T(8,128)(2,1)} %param.13) | copy-start | bytes 1671172
  0.7 10.2 %copy-start.3 = (bf16[2,128,1088]{1,2,0:T(8,128)(2,1)S(1)}, bf16[2,128,1088]{1,2,0:T(8,128)(2,1)}, u32[]{:S(2)}) copy-start(bf16[2,128,1088]{1,2,0:T(8,128)(2,1)} %param.12) | copy-start | bytes 1671172
  125.8 4.0 copy-start
  223.1 57.9 %copy-start.2 = (bf16[2,128,1088]{2,1,0:T(8,128)(2,1)S(1)}, bf16[2,128,1088]{2,1,0:T(8,128)(2,1)}, u32[]{:S(2)}) copy-start(bf16[2,128,1088]{2,1,0:T(8,128)(2,1)} %get-tuple-element.86) | copy-start | bytes 1671172
  280.9 3.7 copy-start.6
  280.9 3.7 copy-start.5
  280.9 3.8 copy-start.4

commit v4 on v3

v4 whole, which is shorter than its diff:
```python
import jax
import jax.numpy as jnp
from jax import lax
from jax.experimental import pallas as pl
from jax.experimental.pallas import tpu as pltpu
from jax.sharding import PartitionSpec as P

D = 1088
WIDE = 1152
F32 = jnp.float32
BF16 = jnp.bfloat16
MESH = pl.DeviceIdType.MESH
A_ROWS, B_ROWS = 272, 144
CUT = 208


class Place:
    def __init__(self):
        batch, seq = lax.axis_index("batch"), lax.axis_index("seq")
        self.batch, self.seq = batch, seq
        self.y, self.z = batch // 4, batch % 4
        self.x, self.c = seq // 2, seq % 2
        self.sibling = {"batch": batch, "seq": self.x * 2 + 1 - self.c}

    def other(self, step):
        return (self.seq + step) % 8

    def member(self, seq):
        return {"batch": self.batch, "seq": seq}

    def peer(self, axis, step):
        spot = {"x": self.x, "y": self.y, "z": self.z}
        spot[axis] = (spot[axis] + step + 4) % 4
        return {"batch": spot["y"] * 4 + spot["z"], "seq": spot["x"] * 2 + self.c}


def greet(peers):
    barrier = pltpu.get_barrier_semaphore()
    for peer in peers:
        pl.semaphore_signal(barrier, inc=1, device_id=peer, device_id_type=MESH)
    pl.semaphore_wait(barrier, len(peers))


def all_peers(me):
    return [me.member(me.other(step)) for step in range(1, 8)] + [me.peer(axis, step) for axis, step in (
        ("y", 1), ("y", 3), ("z", 1), ("z", 2), ("z", 3))]


class Sender:
    def __init__(self, send_sems, recv_sems):
        self.send_sems, self.recv_sems, self.made = send_sems, recv_sems, []

    def __call__(self, source, target, peer):
        index = len(self.made)
        copy = pltpu.make_async_remote_copy(
            src_ref=source, dst_ref=target, send_sem=self.send_sems.at[index],
            recv_sem=self.recv_sems.at[index], device_id=peer, device_id_type=MESH)
        copy.start()
        self.made.append(copy)
        return copy


LATE = (
    [("relay", 0, 0)], [("relay", 1, 0)], [("close", 0, 0)],
    [("relay", 1, 1)], [("relay", 0, 1)], [("relay", 1, 3)], [("relay", 0, 3)], [("close", 1, 0)],
    [("relay", 1, 2)], [("relay", 0, 2)], [("close", 0, 1), ("close", 1, 1)],
    [("close", 0, 3), ("close", 1, 3)], [("close", 0, 2), ("close", 1, 2)], [("settle",)],
)


def merge_rows(stacked):
    row = lax.broadcasted_iota(jnp.int32, (A_ROWS, 320), 0)
    col = lax.broadcasted_iota(jnp.int32, (A_ROWS, 320), 1)
    pick = jnp.where(col == row + 12 * (row // 68), 1.0, 0.0).astype(BF16)
    return jnp.dot(pick, stacked, preferred_element_type=F32).astype(BF16)


def merge_columns(slots):
    total = None
    for z in range(4):
        row = lax.broadcasted_iota(jnp.int32, (384, D), 0)
        col = lax.broadcasted_iota(jnp.int32, (384, D), 1)
        pick = jnp.where((col == row + 272 * z) & (row < 272), 1.0, 0.0).astype(BF16)
        term = jnp.dot(slots[z], pick, preferred_element_type=F32)
        total = term if total is None else total + term
    return total.astype(BF16)

AXES = {0: ("x", "y"), 1: ("y", "x")}


class Rings:
    def __init__(self, me, send, whole, split, source, spot):
        self.me, self.send, self.whole, self.split = me, send, whole, split
        self.source, self.spot, self.crossed, self.sent = source, spot, [], {}

    def move(self, axis, steps, by):
        if axis == "x":
            return ((steps[0] + by) % 4, steps[1])
        return (steps[0], (steps[1] + by) % 4)

    def push(self, part, steps, peer):
        source = self.source if steps == (0, 0) else lambda part: self.spot(part, *steps)
        return self.send(source(part), self.spot(part, *steps), peer)

    def cross(self, half, steps):
        self.crossed.append(self.push(self.whole[half], steps, self.me.sibling))

    def begin(self, half, axis, steps):
        return {by: self.push(self.whole[half], steps, self.me.peer(axis, by)) for by in (1, 3)}

    def forward(self, half, axis, steps, sent, flip):
        ends = []
        for by, which in ((1, flip), (3, 1 - flip)):
            origin = self.move(axis, steps, -by)
            sent[by].wait_recv()
            ends.append(self.push(self.split[half][which], origin, self.me.peer(axis, by)))
        return ends

    def arrived(self, half, axis, steps):
        for by in (1, 3):
            self.cross(half, self.move(axis, steps, by))

    def finish(self, half, axis, steps, ends):
        for copy in ends:
            copy.wait_recv()
        self.cross(half, self.move(axis, steps, 2))

    def first(self, half):
        self.sent[half] = self.begin(half, AXES[half][0], (0, 0))

    def second(self, half):
        self.sent[half, 0] = self.begin(half, AXES[half][1], (0, 0))
        self.cross(half, (0, 0))

    def spread(self, half):
        axis = AXES[half][0]
        self.sent[half, "far"] = self.forward(half, axis, (0, 0), self.sent[half], half)
        for by in (1, 3):
            self.sent[half, by] = self.begin(half, AXES[half][1], self.move(axis, (0, 0), by))
        self.arrived(half, axis, (0, 0))

    def far(self, half):
        axis = AXES[half][0]
        self.finish(half, axis, (0, 0), self.sent[half, "far"])
        self.sent[half, 2] = self.begin(half, AXES[half][1], self.move(axis, (0, 0), 2))

    def relay(self, half, by):
        steps = self.move(AXES[half][0], (0, 0), by)
        self.sent[half, by, "end"] = self.forward(
            half, AXES[half][1], steps, self.sent[half, by], by % 2)
        self.arrived(half, AXES[half][1], steps)

    def close(self, half, by):
        steps = self.move(AXES[half][0], (0, 0), by)
        self.finish(half, AXES[half][1], steps, self.sent[half, by, "end"])

    def settle(self):
        for copy in self.crossed:
            copy.wait_recv()

    def run(self, *actions):
        for name, *rest in actions:
            getattr(self, name)(*rest)


NT = (((1,), (1,)), ((), ()))


def normalize(values):
    center = values - jnp.mean(values, axis=-1, keepdims=True)
    spread = jnp.mean(center * center, axis=-1, keepdims=True)
    scale = lax.rsqrt(spread + 1e-05)
    return center * scale, scale


def norm_pull(grad, gain, unit, scale):
    scaled = grad * gain
    return scale * (
        scaled
        - jnp.mean(scaled, axis=-1, keepdims=True)
        - unit * jnp.mean(scaled * unit, axis=-1, keepdims=True)
    )


def dot(left, right):
    return jnp.dot(left, right, preferred_element_type=F32)


def dot_t(left, right):
    return lax.dot_general(left, right, NT, preferred_element_type=F32)


def widen(value):
    return jnp.concatenate([value, jnp.zeros((value.shape[0], WIDE - D), value.dtype)], axis=1)


def shift_lanes(tiles, value, source, width, target):
    turn = (target - source) % 128
    low, high = source // 128, -(-(source + width) // 128)
    part = value[:, low * 128 : high * 128]
    if turn:
        part = jnp.concatenate([part, jnp.zeros((part.shape[0], 128), part.dtype)], axis=1)
        part = pltpu.roll(part, turn, 1)
    start = source - low * 128 + turn
    for spot in range(start // 128, -(-(start + width) // 128)):
        tile = part[:, spot * 128 : spot * 128 + 128]
        first, last = start - spot * 128, start + width - spot * 128
        if first > 0 or last < 128:
            lane = lax.broadcasted_iota(jnp.int32, tile.shape, 1)
            tile = jnp.where((lane >= first) & (lane < last), tile, 0.0)
        place = (target - start) // 128 + spot
        tiles[place] = tiles[place] + tile if place in tiles else tile


def join_tiles(tiles, count):
    rows = next(iter(tiles.values())).shape[0]
    empty = jnp.zeros((rows, 128), F32)
    return jnp.concatenate([tiles.get(k, empty) for k in range(count)], axis=1)


def segments():
    found = []
    for s in range(8):
        for kind in range(3):
            low, high = max(408 * s, D * kind), min(408 * s + 408, D * kind + D)
            if low < high:
                found.append((s, low - 408 * s, high - low, kind, low - D * kind))
    return found


class Reduce:
    def __init__(self, me, blocks, sib_sems, opp_sems, side_sems, mid_sems, end_sems):
        self.me, self.blocks = me, blocks
        self.sib_sems, self.opp_sems, self.side_sems = sib_sems, opp_sems, side_sems
        self.mid_sems, self.end_sems = mid_sems, end_sems

    def copy(self, source, target, sems, index, peer):
        return pltpu.make_async_remote_copy(
            src_ref=source, dst_ref=target, send_sem=sems.at[(0,) + index],
            recv_sem=sems.at[(1,) + index], device_id=peer, device_id_type=MESH)

    def part(self, half, step, o, parity):
        b = self.blocks[half]
        along, beside = (self.me.x, self.me.y) if half == 0 else (self.me.y, self.me.x)
        first, second = (along + step) % 4, (beside + o) % 4
        x, y = (first, second) if half == 0 else (second, first)
        return b["part"](2 * x + parity, y)

    def ends_of(self, half, which):
        b = self.blocks[half]
        return pl.ds(0, b["cut"]) if which == 0 else pl.ds(b["cut"], b["rows"] - b["cut"])

    def beside(self, half, stage, which):
        return self.me.peer(AXES[half][stage], 1 if which == 0 else 3)

    def sib_copy(self, half, step, o):
        b = self.blocks[half]
        return self.copy(b["sib_out"].at[o], b["sib_in"].at[step, o], self.sib_sems,
                         (half, step, o), self.me.sibling)

    def opp_copy(self, half, o, which):
        b = self.blocks[half]
        rows = self.ends_of(half, which)
        return self.copy(b["sib_in"].at[2, o, rows], b["in_opp"].at[o, rows], self.opp_sems,
                         (half, o, which), self.beside(half, 0, which))

    def side_copy(self, half, o, which):
        b = self.blocks[half]
        return self.copy(b["sib_in"].at[1 + 2 * which, o], b["in_side"].at[which, o],
                         self.side_sems, (half, o, which), self.beside(half, 0, which))

    def mid_copy(self, half, which):
        b = self.blocks[half]
        rows = self.ends_of(half, which)
        return self.copy(b["sib_out"].at[2, rows], b["in_mid"].at[rows], self.mid_sems,
                         (half, which), self.beside(half, 1, which))

    def end_copy(self, half, which):
        b = self.blocks[half]
        return self.copy(b["sib_out"].at[which], b["in_end"].at[which], self.end_sems,
                         (half, which), self.beside(half, 1, which))

    def loop(self, body):
        lax.fori_loop(0, 4, lambda o, carry: (body(o), carry)[1], 0)

    def cross(self, step, before):
        def body(o):
            for half in (0, 1):
                if before is not None:
                    self.sib_copy(half, before, o).wait_send()
                self.blocks[half]["sib_out"][o] = self.part(half, step, o, 1 - self.me.c).astype(BF16)
                self.sib_copy(half, step, o).start()
        self.loop(body)

    def mine(self, half, step, o):
        value = self.part(half, step, o, self.me.c)
        self.sib_copy(half, step, o).wait_recv()
        return value + self.blocks[half]["sib_in"][step, o].astype(F32)

    def opposite(self):
        def body(o):
            for half in (0, 1):
                self.blocks[half]["sib_in"][2, o] = self.mine(half, 2, o).astype(BF16)
                for which in (0, 1):
                    self.opp_copy(half, o, which).start()
        self.loop(body)

    def join(self, half, value, arrived, which):
        cut = self.blocks[half]["cut"]
        if which == 0:
            return jnp.concatenate([value[:cut] + arrived[:cut].astype(F32), value[cut:]], axis=0)
        return jnp.concatenate([value[:cut], value[cut:] + arrived[cut:].astype(F32)], axis=0)

    def sides(self, which):
        def body(o):
            for half in (0, 1):
                b = self.blocks[half]
                value = self.mine(half, 1 + 2 * which, o)
                self.opp_copy(half, o, which).wait_recv()
                value = self.join(half, value, b["in_opp"].at[o], which)
                b["sib_in"][1 + 2 * which, o] = value.astype(BF16)
                self.side_copy(half, o, which).start()
        self.loop(body)

    def own(self):
        def body(o):
            for half in (0, 1):
                b = self.blocks[half]
                value = self.mine(half, 0, o)
                for which in (0, 1):
                    self.side_copy(half, o, which).wait_recv()
                    value = value + b["in_side"][which, o].astype(F32)
                b["acc"][o] = value
        self.loop(body)

    def middle(self):
        def body(o):
            for half in (0, 1):
                self.sib_copy(half, 0, o).wait_send()
        self.loop(body)
        for half in (0, 1):
            b = self.blocks[half]
            b["sib_out"][2] = b["acc"][2].astype(BF16)
            for which in (0, 1):
                self.mid_copy(half, which).start()

    def last(self):
        for half in (0, 1):
            b = self.blocks[half]
            for which in (0, 1):
                value = b["acc"][1 + 2 * which]
                self.mid_copy(half, which).wait_recv()
                b["sib_out"][which] = self.join(half, value, b["in_mid"], which).astype(BF16)
                self.end_copy(half, which).start()

    def result(self, half):
        b = self.blocks[half]
        value = b["acc"][0]
        for which in (0, 1):
            self.end_copy(half, which).wait_recv()
            value = value + b["in_end"][which].astype(F32)
        return value

    def drain(self):
        def body(o):
            for half in (0, 1):
                for which in (0, 1):
                    self.opp_copy(half, o, which).wait_send()
                    self.side_copy(half, o, which).wait_send()
        self.loop(body)
        for half in (0, 1):
            for which in (0, 1):
                self.mid_copy(half, which).wait_send()
                self.end_copy(half, which).wait_send()


REDUCE_BUFFERS = ("sib_out", "sib_in", "in_opp", "in_side", "acc", "in_end", "in_mid")


def reduce_scratch(shapes):
    found = []
    for shape in shapes:
        for lead, kind in (((4,), BF16), ((4, 4), BF16), ((4,), BF16), ((2, 4), BF16), ((4,), F32),
                           ((2,), BF16), ((), BF16)):
            found.append(pltpu.VMEM(lead + shape, kind))
    return found + [pltpu.SemaphoreType.DMA((2, 2, 4, 4)), pltpu.SemaphoreType.DMA((2, 2, 4, 2)),
                    pltpu.SemaphoreType.DMA((2, 2, 4, 2)), pltpu.SemaphoreType.DMA((2, 2, 2)),
                    pltpu.SemaphoreType.DMA((2, 2, 2))]


REDUCE_REFS = 2 * len(REDUCE_BUFFERS) + 5


def make_reduce(me, refs, settings):
    blocks = {}
    count = len(REDUCE_BUFFERS)
    for half in (0, 1):
        part, rows, cut = settings[half]
        blocks[half] = dict(zip(REDUCE_BUFFERS, refs[half * count : half * count + count]))
        blocks[half].update(part=part, rows=rows, cut=cut)
    return Reduce(me, blocks, *refs[2 * count :])


def leave_kernel(x_q, x_o, y_q, y_o, extra, block_u, block_b, out_a, out_b,
                 zout_q, zout_u, zout_b, zin_q, zin_u, zin_b, z_sems, *refs):
    me = Place()
    greet(all_peers(me))

    def upper(column, y):
        return rows_of(column, pl.ds(pl.multiple_of(y * A_ROWS, 16), 144))

    def rows_of(column, rows):
        one = dot(x_q[rows], y_q[column])
        two = dot(x_o[rows], y_o[column, :, 0:128])
        return jnp.concatenate([one[:, :384], one[:, 384:] + two], axis=1)

    def lower(column, y):
        rows = pl.ds(pl.multiple_of(y * A_ROWS + 144, 16), 128)
        return jnp.concatenate([rows_of(column, rows), extra[column]], axis=0)

    reduce = make_reduce(me, refs, ((upper, 144, 64), (lower, 144, 64)))

    def pick_rows(z):
        row = lax.broadcasted_iota(jnp.int32, (80, A_ROWS), 0)
        col = lax.broadcasted_iota(jnp.int32, (80, A_ROWS), 1)
        return jnp.where((col == row + 68 * z) & (row < 68), 1.0, 0.0).astype(BF16)

    def pick_columns(z):
        row = lax.broadcasted_iota(jnp.int32, (D, 384), 0)
        col = lax.broadcasted_iota(jnp.int32, (D, 384), 1)
        return jnp.where((row == col + 272 * z) & (col < 272), 1.0, 0.0).astype(BF16)

    buffers = ((zout_q, zin_q), (zout_u, zin_u), (zout_b, zin_b))

    def z_copy(kind, step):
        source, target = buffers[kind]
        return reduce.copy(source.at[step - 1], target.at[step - 1], z_sems, (kind, step - 1),
                           me.peer("z", step))

    def early(step):
        z = (me.z + step) % 4
        zout_u[step - 1] = dot(pick_rows(z), block_u[...]).astype(BF16)
        zout_b[step - 1] = dot(block_b[...], pick_columns(z)).astype(BF16)
        z_copy(1, step).start()
        z_copy(2, step).start()

    reduce.cross(2, None)
    reduce.opposite()
    reduce.cross(1, 2)
    reduce.cross(3, 1)
    early(2)
    reduce.sides(0)
    reduce.sides(1)
    reduce.cross(0, 3)
    early(1)
    early(3)
    reduce.own()
    reduce.middle()
    reduce.last()
    first, second = reduce.result(0), reduce.result(1)
    block_q = jnp.concatenate([first, second[:128]], axis=0).astype(BF16)
    payload = second[128:]

    def slices(z):
        return jnp.concatenate([dot(pick_rows(z), block_q), payload], axis=0)

    for step in (2, 1, 3):
        zout_q[step - 1] = slices((me.z + step) % 4).astype(BF16)
        z_copy(0, step).start()
    near = slices(me.z)
    above = dot(pick_rows(me.z), block_u[...])
    below = dot(block_b[...], pick_columns(me.z))
    for step in (1, 2, 3):
        z_copy(1, step).wait_recv()
        z_copy(2, step).wait_recv()
        above = above + zin_u[step - 1].astype(F32)
        below = below + zin_b[step - 1].astype(F32)
    for step in (1, 2, 3):
        z_copy(0, step).wait_recv()
        near = near + zin_q[step - 1].astype(F32)
    out_a[:, :512] = near[:80]
    out_a[:, 512:] = above
    out_b[:136] = below[:136]
    out_b[136:] = near[80:88, :384]
    reduce.drain()
    for step in (1, 2, 3):
        for kind in range(3):
            z_copy(kind, step).wait_send()


def leave_block(*operands):
    vmem = pltpu.VMEM
    return pl.pallas_call(
        leave_kernel,
        out_shape=(jax.ShapeDtypeStruct((80, WIDE), F32), jax.ShapeDtypeStruct((B_ROWS, 384), F32)),
        in_specs=[pl.BlockSpec(memory_space=vmem)] * 7,
        out_specs=(pl.BlockSpec(memory_space=vmem),) * 2,
        scratch_shapes=(
            [vmem((3, 96, 512), BF16), vmem((3, 80, 640), BF16), vmem((3, B_ROWS, 384), BF16)] * 2
            + [pltpu.SemaphoreType.DMA((2, 3, 3))] + reduce_scratch(((144, 512), (144, 512)))),
        compiler_params=pltpu.CompilerParams(
            collective_id=3, has_side_effects=True, vmem_limit_bytes=60 * 2**20),
    )(*operands)


def push(source, target, sems, index, peer):
    return pltpu.make_async_remote_copy(
        src_ref=source, dst_ref=target, send_sem=sems.at[(0,) + index],
        recv_sem=sems.at[(1,) + index], device_id=peer, device_id_type=MESH)


def turned(value):
    return value.astype(F32).T


def masked(scores, bounds, seq, block):
    rows = lax.broadcasted_iota(jnp.int32, scores.shape, 0)
    spot = block * 256 + lax.broadcasted_iota(jnp.int32, (1, 256), 1)
    start = jnp.zeros((1, 256), jnp.int32)
    for n in range(3):
        bound = bounds[:, 3 * seq + n : 3 * seq + n + 1]
        start = jnp.where(spot >= bound, bound, start)
    return jnp.where((rows <= spot) & (rows >= start), scores, -1e30)


def chances(keys, query, bounds, seq, block):
    scores = lax.dot_general(keys, query, NT, preferred_element_type=F32)
    scores = masked(scores, bounds, seq, block)
    powers = jnp.exp(scores - jnp.max(scores, axis=0, keepdims=True))
    return powers * (1.0 / jnp.sum(powers, axis=0, keepdims=True))


def head_part(value, head):
    lane = lax.broadcasted_iota(jnp.int32, value.shape, 1)
    return jnp.where((lane < 64) == (head == 0), value, jnp.zeros_like(value))


def attend(queries, keys, values, bounds, seq, heads, store, pump):
    queries = queries * 0.125
    value_t = turned(values).astype(BF16)
    for block in range(4):
        rows = slice(block * 256, block * 256 + 256)
        size = block * 256 + 256
        parts = []
        for head in range(heads):
            low = chances(keys[:size], head_part(queries[rows], head), bounds, seq, block).astype(BF16)
            parts.append(dot(value_t[:, :size], low))
            pump()
        whole = parts[0] if heads == 1 else jnp.concatenate([parts[0][:64], parts[1][64:]], axis=0)
        store(block, whole.T.astype(BF16).reshape(2, 128, 128))


def fetch_blocks(source, held, sems):
    copies = [pltpu.make_async_copy(source.at[s], held.at[s], sems.at[s]) for s in range(8)]
    for copy in copies:
        copy.start()
    return copies


GATHER_COPIES = 160
COUNTS_ROW = 12


def enter_kernel(a_ref, b_ref, vec, hidden, gq, gu, gb, att, got, got8, normed_t, lines, up_row,
                 bound_row, weights, za, zb, mine_a, mine_b, vecs, pack, out, out8,
                 send_sems, recv_sems, local_sems, vec_sems, in_sems, in8_sems, back_sems, back8_sems):
    g = Place()
    greet(all_peers(g))
    send = Sender(send_sems, recv_sems)
    first = []
    left, right = pl.ds(0, 512), pl.ds(512, 640)
    for step in (2, 1, 3):
        first.append(send(a_ref.at[:, left], za.at[g.z, :, left], g.peer("z", step)))
    later = []
    for step in (2, 1, 3):
        later.append(send(a_ref.at[:, right], za.at[g.z, :, right], g.peer("z", step)))
        later.append(send(b_ref, zb.at[g.z], g.peer("z", step)))

    def vec_copy(step):
        return push(vec, vecs.at[g.seq], vec_sems, (step - 1,), g.member(g.other(step)))

    for step in range(1, 8):
        vec_copy(step).start()
    vecs[g.seq] = vec[...]
    za[g.z] = a_ref[...]
    zb[g.z] = b_ref[...]
    for copy in first:
        copy.wait_recv()
    mine_a[:, :512] = merge_rows(za[:, :, :512].reshape(320, 512))

    def spot(part, step_x, step_y):
        kind, low, rows = part
        x, y = (g.x + step_x) % 4, (g.y + step_y) % 4
        if kind == "b":
            return gb.at[y, 2 * x + g.c, pl.ds(low, rows)]
        span = pl.ds(pl.multiple_of(y * A_ROWS + low, 16), rows)
        return (weights if kind == "q" else gu).at[2 * x + g.c, span]

    def source(part):
        kind, low, rows = part
        if kind == "b":
            return mine_b.at[pl.ds(low, rows)]
        return mine_a.at[pl.ds(low, rows), left if kind == "q" else right]

    near = Rings(g, send, {0: ("q", 0, 144), 1: ("q", 144, 128)},
                 {0: [("q", 0, 64), ("q", 64, 80)], 1: [("q", 144, 64), ("q", 208, 64)]}, source, spot)
    rest = Rings(g, send, {0: ("u", 0, 272), 1: ("b", 0, 144)},
                 {0: [("u", 0, 128), ("u", 128, 144)], 1: [("b", 0, 64), ("b", 64, 80)]}, source, spot)
    near.run(("first", 0), ("first", 1), ("second", 0), ("second", 1))
    own = [pltpu.make_async_copy(source(part), spot(part, 0, 0), local_sems.at[k])
           for k, part in enumerate((("q", 0, A_ROWS), ("u", 0, A_ROWS), ("b", 0, B_ROWS)))]
    own[0].start()
    for step in range(1, 8):
        vec_copy(step).wait_recv()
    tiles = {}
    counts = jnp.zeros((1, 128), F32)
    for s in range(8):
        value = vecs[s].astype(F32)
        shift_lanes(tiles, value, 0, 136, 136 * s)
        counts = counts + value[COUNTS_ROW : COUNTS_ROW + 1, :128]
    table = join_tiles(tiles, 9)
    lines[...] = table[:8]
    bound_row[...] = counts.astype(jnp.int32)
    bounds = bound_row[...]
    for y in range(4):
        tiles = {}
        for odd in (0, 1):
            value = vecs[2 * y + odd].astype(F32)
            for row in range(4):
                shift_lanes(tiles, value[8 + row : 9 + row], 0, 136, 544 * odd + 136 * row)
        up_row[y] = join_tiles(tiles, 9)[:, :D]
    unit, _ = normalize(hidden[...].astype(F32).reshape(256, D))
    normed = unit * table[0:1, :D] + table[2:3, :D]
    normed_t[...] = normed.T.astype(BF16)
    normed = normed.astype(BF16)
    near.run(("spread", 0), ("spread", 1), ("relay", 0, 0), ("relay", 1, 0))
    for copy in later:
        copy.wait_recv()
    mine_a[:, 512:] = merge_rows(za[:, :, 512:].reshape(320, 640))
    mine_b[...] = merge_columns(zb)
    own[1].start()
    own[2].start()
    near.run(("far", 0), ("far", 1), ("relay", 0, 1), ("relay", 1, 1), ("close", 0, 0),
             ("close", 1, 0), ("relay", 0, 3), ("relay", 1, 3), ("relay", 0, 2), ("relay", 1, 2))
    rest.run(("first", 1), ("first", 0), ("second", 0))
    near.run(*[("close", half, by) for by in (1, 3, 2) for half in (0, 1)], ("settle",))
    own[0].wait()
    kept = pltpu.make_async_copy(weights, gq, local_sems.at[3])
    kept.start()
    tiles = ({}, {}, {})
    for s in range(8):
        block = dot(normed, weights[s])
        for seg, low, width, kind, place in segments():
            if seg == s:
                shift_lanes(tiles[kind], block, low, width, place)
    for kind, row in ((0, 4), (1, None), (2, 5)):
        for p in range(9):
            tile = tiles[kind][p]
            if row is not None:
                tile = tile + table[row : row + 1, 128 * p : 128 * p + 128]
            pack[p, kind] = tile.astype(BF16).reshape(2, 128, 128)

    rest_events = list(LATE)

    def pump():
        if rest_events:
            rest.run(*rest_events.pop(0))

    def in_copy(step):
        return push(pack.at[g.other(step)], got.at[g.seq], in_sems, (step - 1,), g.member(g.other(step)))

    def in8_copy(extra, source):
        return pltpu.make_async_remote_copy(
            src_ref=pack.at[8, :, extra], dst_ref=got8.at[source], send_sem=in8_sems.at[8 + extra],
            recv_sem=in8_sems.at[source], device_id=g.member(4 * extra), device_id_type=MESH)

    for step in (4, 3, 5, 2, 6, 1, 7):
        in_copy(step).start()
    for extra in (0, 1):
        @pl.when(g.seq != 4 * extra)
        def _():
            in8_copy(extra, g.seq).start()

        @pl.when(g.seq == 4 * extra)
        def _():
            got8[g.seq] = pack[8, :, extra]
    got[g.seq] = pack[g.seq]
    rest.run(("spread", 1), ("spread", 0), ("second", 1), ("far", 1), ("far", 0))
    for step in range(1, 8):
        in_copy(step).wait_recv()

    def back_copy(seq, step):
        return push(out.at[g.other(step), seq], att.at[g.seq, seq], back_sems, (seq, step - 1),
                    g.member(g.other(step)))

    def pair(seq):
        def store(block, value):
            out[pl.ds(2 * block, 2), seq] = value
        part = lambda kind: got[:, kind, seq].reshape(1024, 128)
        attend(part(0), part(1), part(2), bounds, seq, 2, store, pump)
        for step in (4, 3, 5, 2, 6, 1, 7):
            back_copy(seq, step).start()

    for seq in (0, 1):
        pair(seq)
    att[g.seq] = out[g.seq]

    def back8_copy(extra, step):
        return pltpu.make_async_remote_copy(
            src_ref=out8.at[g.other(step)], dst_ref=att.at[8, extra], send_sem=back8_sems.at[1 + step],
            recv_sem=back8_sems.at[extra], device_id=g.member(g.other(step)), device_id_type=MESH)

    for extra in (0, 1):
        @pl.when(g.seq == 4 * extra)
        def _():
            for step in range(1, 8):
                in8_copy(extra, g.other(step)).wait_recv()

            def store(block, value):
                out8[pl.ds(2 * block, 2)] = value
            part = lambda kind: got8[:, kind].reshape(1024, 128)
            attend(part(0), part(1), part(2), bounds, extra, 1, store, lambda: None)
            for step in range(1, 8):
                back8_copy(extra, step).start()
            att[8, extra] = out8[g.seq]
            for step in range(1, 8):
                back8_copy(extra, step).wait_send()

        @pl.when(g.seq != 4 * extra)
        def _():
            in8_copy(extra, g.seq).wait_send()
            back8_copy(extra, 1).wait_recv()
    for step in range(1, 8):
        in_copy(step).wait_send()
        for seq in (0, 1):
            back_copy(seq, step).wait_recv()
            back_copy(seq, step).wait_send()
    while rest_events:
        rest.run(*rest_events.pop(0))
    for copy in send.made:
        copy.wait_send()
    for step in range(1, 8):
        vec_copy(step).wait_send()
    own[1].wait()
    own[2].wait()
    kept.wait()


def enter_block(*operands):
    tile = (128, 128)
    vmem = pltpu.VMEM
    shape = jax.ShapeDtypeStruct
    return pl.pallas_call(
        enter_kernel,
        out_shape=(
            shape((8, D, 512), BF16), shape((8, D, 640), BF16), shape((4, 8, B_ROWS, D), BF16),
            shape((9, 2) + tile, BF16), shape((8, 3, 2) + tile, BF16), shape((8, 3) + tile, BF16),
            shape((D, 256), BF16), shape((8, WIDE), F32), shape((4, 1, D), F32),
            shape((1, 128), jnp.int32)),
        in_specs=[pl.BlockSpec(memory_space=vmem)] * 4,
        out_specs=(pl.BlockSpec(memory_space=pl.ANY),) * 3 + (pl.BlockSpec(memory_space=vmem),) * 7,
        scratch_shapes=[
            vmem((8, D, 512), BF16), vmem((4, 80, WIDE), BF16), vmem((4, B_ROWS, 384), BF16),
            vmem((A_ROWS, WIDE), BF16), vmem((B_ROWS, D), BF16), vmem((8, 16, 256), BF16),
            vmem((9, 3, 2) + tile, BF16), vmem((8, 2) + tile, BF16), vmem((8,) + tile, BF16),
            pltpu.SemaphoreType.DMA((GATHER_COPIES,)), pltpu.SemaphoreType.DMA((GATHER_COPIES,)),
            pltpu.SemaphoreType.DMA((4,)), pltpu.SemaphoreType.DMA((2, 7)),
            pltpu.SemaphoreType.DMA((2, 7)), pltpu.SemaphoreType.DMA((10,)),
            pltpu.SemaphoreType.DMA((2, 2, 7)), pltpu.SemaphoreType.DMA((9,))],
        compiler_params=pltpu.CompilerParams(
            collective_id=1, has_side_effects=True, vmem_limit_bytes=60 * 2**20),
    )(*operands)


def attend_pull(queries, keys, values, grads, bounds, seq, heads, key_sum, value_sum, store, pump):
    queries = queries * 0.125
    key_t = turned(keys).astype(BF16)
    key_sum[...] = jnp.zeros_like(key_sum)
    value_sum[...] = jnp.zeros_like(value_sum)
    for block in range(4):
        rows = slice(block * 256, block * 256 + 256)
        size = block * 256 + 256
        parts = []
        for head in range(heads):
            query, grad = head_part(queries[rows], head), head_part(grads[rows], head)
            probs = chances(keys[:size], query, bounds, seq, block)
            change = lax.dot_general(values[:size], grad, NT, preferred_element_type=F32)
            inner = jnp.sum(probs * change, axis=0, keepdims=True)
            slope = (probs * (change - inner)).astype(BF16)
            value_sum[:size] += jnp.dot(probs.astype(BF16), grad, preferred_element_type=F32)
            key_sum[:size] += jnp.dot(slope, query, preferred_element_type=F32)
            parts.append(dot(key_t[:, :size], slope))
            pump()
        whole = parts[0] if heads == 1 else jnp.concatenate([parts[0][:64], parts[1][64:]], axis=0)
        store(0, block, (whole.T * 0.125).astype(BF16).reshape(2, 128, 128))
    for kind, total in ((1, key_sum), (2, value_sum)):
        for block in range(4):
            store(kind, block, total[block * 256 : block * 256 + 256].astype(BF16).reshape(2, 128, 128))


def pull_kernel(pack, got, got8, hidden, middle_grad, lines, bound_row, x_o, x_u, y_o, y_u, tt, act,
                sums, up_sums, ga, placed, input_grad, extra, block_u, block_b,
                weights, back, grad, grad8, out, out8, key_sum, value_sum,
                weight_sems, in_sems, in8_sems, back_sems, back8_sems, *refs):
    g = Place()
    bounds = bound_row[...]
    greet(all_peers(g))

    def part_u(column, y):
        rows = pl.ds(pl.multiple_of(y * A_ROWS, 16), A_ROWS)
        three = dot(x_u[rows], y_u[column])
        two = dot(x_o[rows], y_o[column, :, 128:256])
        return jnp.concatenate([three[:, :128] + two, three[:, 128:]], axis=1)

    def part_b(column, y):
        return dot(tt[column], act[y])

    reduce = make_reduce(g, refs, ((part_u, A_ROWS, 128), (part_b, B_ROWS, 64)))
    plan = {1: lambda: reduce.cross(0, 3), 14: reduce.own}
    ticks = [0]

    def pump():
        ticks[0] += 1
        if ticks[0] in plan:
            plan[ticks[0]]()

    def fetch(s):
        return pltpu.make_async_copy(ga.at[s], weights.at[s % 2], weight_sems.at[s % 2])

    fetch(0).start()
    fetch(1).start()

    def in_copy(step):
        return push(pack.at[g.other(step)], grad.at[g.seq], in_sems, (step - 1,), g.member(g.other(step)))

    def in8_copy(which, source):
        return pltpu.make_async_remote_copy(
            src_ref=pack.at[8, which], dst_ref=grad8.at[source], send_sem=in8_sems.at[8 + which],
            recv_sem=in8_sems.at[source], device_id=g.member(4 * which), device_id_type=MESH)

    for step in (4, 3, 5, 2, 6, 1, 7):
        in_copy(step).start()
    for which in (0, 1):
        @pl.when(g.seq != 4 * which)
        def _():
            in8_copy(which, g.seq).start()

        @pl.when(g.seq == 4 * which)
        def _():
            grad8[g.seq] = pack[8, which]
    grad[g.seq] = pack[g.seq]
    reduce.cross(2, None)
    reduce.opposite()
    reduce.cross(1, 2)
    reduce.cross(3, 1)
    reduce.sides(0)
    reduce.sides(1)
    for step in range(1, 8):
        in_copy(step).wait_recv()

    def back_copy(seq, step):
        return push(out.at[g.other(step), seq], back.at[g.seq, seq], back_sems, (seq, step - 1),
                    g.member(g.other(step)))

    def pair(seq, carry):
        def store(kind, block, value):
            out[pl.ds(2 * block, 2), seq, kind] = value
        part = lambda kind: got[:, kind, seq].reshape(1024, 128)
        attend_pull(part(0), part(1), part(2), grad[:, seq].reshape(1024, 128), bounds, seq, 2,
                    key_sum, value_sum, store, pump)
        for step in (4, 3, 5, 2, 6, 1, 7):
            back_copy(seq, step).start()
        return carry

    for seq in (0, 1):
        pair(seq, 0)
    back[g.seq] = out[g.seq]

    def back8_copy(which, step):
        return pltpu.make_async_remote_copy(
            src_ref=out8.at[g.other(step)], dst_ref=back.at[8, which], send_sem=back8_sems.at[1 + step],
            recv_sem=back8_sems.at[which], device_id=g.member(g.other(step)), device_id_type=MESH)

    for which in (0, 1):
        @pl.when(g.seq == 4 * which)
        def _():
            for step in range(1, 8):
                in8_copy(which, g.other(step)).wait_recv()

            def store(kind, block, value):
                out8[pl.ds(2 * block, 2), kind] = value
            part = lambda kind: got8[:, kind].reshape(1024, 128)
            attend_pull(part(0), part(1), part(2), grad8[...].reshape(1024, 128), bounds, which, 1,
                        key_sum, value_sum, store, lambda: None)
            for step in range(1, 8):
                back8_copy(which, step).start()
            back[8, which] = out8[g.seq]
            for step in range(1, 8):
                back8_copy(which, step).wait_send()

        @pl.when(g.seq != 4 * which)
        def _():
            in8_copy(which, g.seq).wait_send()
            back8_copy(which, 1).wait_recv()
    reduce.middle()
    for step in range(1, 8):
        in_copy(step).wait_send()
        for seq in (0, 1):
            back_copy(seq, step).wait_recv()
            back_copy(seq, step).wait_send()

    natural = [jnp.concatenate([back[p, :, kind].reshape(256, 128) for p in range(9)],
                               axis=1).astype(F32) for kind in range(3)]
    total = None
    for s in range(8):
        tiles = {}
        for seg, low, width, kind, spot in segments():
            if seg == s:
                shift_lanes(tiles, natural[kind], spot, width, low)
        block = join_tiles(tiles, 4).astype(BF16)
        placed[s] = block
        fetch(s).wait()
        term = dot_t(block, weights[s % 2])
        if s < 6:
            fetch(s + 2).start()
        total = term if total is None else total + term
    reduce.last()
    unit, scale = normalize(hidden[...].astype(F32).reshape(256, D))
    input_grad[...] = middle_grad[...] + norm_pull(total, lines[0:1, :D], unit, scale)

    def column_sum(value):
        return jnp.sum(value, axis=0, keepdims=True)

    table = jnp.concatenate([
        column_sum(widen(total * unit)), sums[0:1], column_sum(widen(total)), sums[1:2],
        column_sum(natural[0]), column_sum(natural[2]), sums[2:4]], axis=0)
    for s in range(8):
        tiles = {}
        shift_lanes(tiles, table, 136 * s, 136, 0)
        first = join_tiles(tiles, 4)
        rows = []
        for row in range(4):
            tiles = {}
            shift_lanes(tiles, up_sums[s], 32 + 136 * row, 136, 136)
            rows.append(join_tiles(tiles, 4))
        second = jnp.concatenate(rows + [jnp.zeros((4, 512), F32)], axis=0)
        extra[s] = jnp.concatenate([first + second, jnp.zeros((8, 512), F32)], axis=0)
    block_u[...] = reduce.result(0).astype(BF16)
    block_b[...] = reduce.result(1).astype(BF16)
    reduce.drain()


def attend_backward(*operands):
    tile = (128, 128)
    vmem = pltpu.VMEM
    return pl.pallas_call(
        pull_kernel,
        out_shape=(jax.ShapeDtypeStruct((8, 256, 512), BF16),
                   jax.ShapeDtypeStruct((256, D), F32), jax.ShapeDtypeStruct((8, 16, 512), F32),
                   jax.ShapeDtypeStruct((A_ROWS, 640), BF16), jax.ShapeDtypeStruct((B_ROWS, D), BF16)),
        in_specs=[pl.BlockSpec(memory_space=vmem)] * 15 + [pl.BlockSpec(memory_space=pl.ANY)],
        out_specs=(pl.BlockSpec(memory_space=vmem),) * 5,
        scratch_shapes=[
            vmem((2, D, 512), BF16), vmem((9, 2, 3) + tile, BF16), vmem((8, 2) + tile, BF16), vmem((8,) + tile, BF16),
            vmem((8, 2, 3) + tile, BF16), vmem((8, 3) + tile, BF16),
            vmem((1024, 128), F32), vmem((1024, 128), F32),
            pltpu.SemaphoreType.DMA((2,)),
            pltpu.SemaphoreType.DMA((2, 7)), pltpu.SemaphoreType.DMA((10,)),
            pltpu.SemaphoreType.DMA((2, 2, 7)), pltpu.SemaphoreType.DMA((9,)),
        ] + reduce_scratch(((A_ROWS, 640), (B_ROWS, D))),
        compiler_params=pltpu.CompilerParams(
            collective_id=2, has_side_effects=True, vmem_limit_bytes=63 * 2**20),
    )(*operands)


def middle_kernel(att, hidden, top, lines, up_row, gq, gu, gb,
                  layer_out, middle_grad, att_grad, att_t, normed_t, active, y_o, y_u, sums, up_sums, top_t,
                  held_o, held_u, held_b, normed, down_sum, norm_grad, top_pad, sems_o, sems_u, sems_b):
    copies_o = []
    for s in range(8):
        copies_o.append(pltpu.make_async_copy(
            gq.at[s, :, pl.ds(384, 128)], held_o.at[s, :, pl.ds(0, 128)], sems_o.at[0, s]))
        copies_o.append(pltpu.make_async_copy(
            gu.at[s, :, pl.ds(0, 128)], held_o.at[s, :, pl.ds(128, 128)], sems_o.at[1, s]))
    for copy in copies_o:
        copy.start()

    def up_copy(s):
        return pltpu.make_async_copy(gu.at[s], held_u.at[s], sems_u.at[s])

    def down_copy(y):
        return pltpu.make_async_copy(gb.at[y], held_b.at[y], sems_b.at[y])

    for y in range(4):
        up_copy(2 * y).start()
        up_copy(2 * y + 1).start()
        down_copy(y).start()

    tiles = {}
    for s in range(8):
        shift_lanes(tiles, widen(top[...].reshape(256, D)).astype(F32), 136 * s, 136, 144 * s)
    padded = join_tiles(tiles, 9)
    top_pad[...] = padded.astype(BF16)
    top_t[...] = padded.T.astype(BF16).reshape(8, B_ROWS, 256)
    attended = jnp.concatenate([att[p].reshape(256, 128) for p in range(9)], axis=1)
    att_t[...] = attended.astype(F32).T[:D].astype(BF16)
    tiles = {}
    for s in range(8):
        copies_o[2 * s].wait()
        copies_o[2 * s + 1].wait()
        shift_lanes(tiles, dot(attended[:, :D], held_o[s]), 24, 136, 136 * s)
    branch = join_tiles(tiles, 9)[:, :D]
    middle = hidden[...].astype(F32).reshape(256, D) + branch + lines[6:7, :D]
    unit, scale = normalize(middle)
    value = unit * lines[1:2, :D] + lines[3:4, :D]
    normed[...] = value.astype(BF16)
    normed_t[...] = value.T.astype(BF16)
    down_sum[...] = jnp.zeros_like(down_sum)
    norm_grad[...] = jnp.zeros_like(norm_grad)

    def step(y, carry):
        tiles = {}
        for odd in (0, 1):
            up_copy(2 * y + odd).wait()
            shift_lanes(tiles, dot(normed[...], held_u[2 * y + odd]), 32, 544, 544 * odd)
        pre = join_tiles(tiles, 9)[:, :D] + up_row[y]
        cube = 0.7978845608028654 * (pre + 0.044715 * (pre * pre * pre))
        bend = jnp.tanh(cube)
        half = 0.5 * (1.0 + bend)
        acts = (pre * half).astype(BF16)
        slope = half + 0.5 * pre * (1.0 - bend * bend) * (
            0.7978845608028654 * (1.0 + 3 * 0.044715 * (pre * pre)))
        active[y] = acts
        down_copy(y).wait()
        weights = held_b[y].reshape(8 * B_ROWS, D)
        down_sum[...] += dot_t(acts, weights)
        inner = dot(top_pad[...], weights) * slope
        inner = widen(inner.astype(BF16).astype(F32))
        total = None
        for odd in (0, 1):
            tiles = {}
            shift_lanes(tiles, inner, 544 * odd, 544, 32)
            block = join_tiles(tiles, 5)
            up_sums[2 * y + odd] = jnp.sum(block, axis=0, keepdims=True)
            block = block.astype(BF16)
            y_u[2 * y + odd] = block
            term = dot_t(block, held_u[2 * y + odd])
            total = term if total is None else total + term
        norm_grad[...] += total
        return carry

    lax.fori_loop(0, 4, step, 0)
    tiles = {}
    down = down_sum[...]
    for s in range(8):
        shift_lanes(tiles, down, 144 * s, 136, 136 * s)
    out = middle + join_tiles(tiles, 9)[:, :D] + lines[7:8, :D]
    layer_out[...] = out.astype(BF16).reshape(2, 128, D)
    grad = norm_grad[...]
    cotangent = top[...].astype(F32).reshape(256, D)
    total = cotangent + norm_pull(grad, lines[1:2, :D], unit, scale)
    middle_grad[...] = total
    branch = widen(total.astype(BF16).astype(F32))
    back = None
    for s in range(8):
        tiles = {}
        shift_lanes(tiles, branch, 136 * s, 136, 24)
        block = join_tiles(tiles, 2).astype(BF16)
        y_o[s] = block
        term = dot_t(block, held_o[s])
        back = term if back is None else back + term
    back = widen(back).astype(BF16)
    for p in range(9):
        att_grad[p] = back[:, 128 * p : 128 * p + 128].reshape(2, 128, 128)
    sums[0:1] = jnp.sum(widen(grad * unit), axis=0, keepdims=True)
    sums[1:2] = jnp.sum(widen(grad), axis=0, keepdims=True)
    sums[2:3] = jnp.sum(branch, axis=0, keepdims=True)
    sums[3:4] = jnp.sum(widen(cotangent), axis=0, keepdims=True)
    sums[4:8] = jnp.zeros((4, WIDE), F32)


def middle_block(*operands):
    vmem = pltpu.VMEM
    shape = jax.ShapeDtypeStruct
    return pl.pallas_call(
        middle_kernel,
        out_shape=(
            shape((2, 128, D), BF16), shape((256, D), F32), shape((9, 2, 128, 128), BF16),
            shape((D, 256), BF16), shape((D, 256), BF16), shape((4, 256, D), BF16),
            shape((8, 256, 256), BF16), shape((8, 256, 640), BF16), shape((8, WIDE), F32),
            shape((8, 1, 640), F32), shape((8, B_ROWS, 256), BF16)),
        in_specs=[pl.BlockSpec(memory_space=vmem)] * 5 + [pl.BlockSpec(memory_space=pl.ANY)] * 3,
        out_specs=(pl.BlockSpec(memory_space=vmem),) * 11,
        scratch_shapes=[
            vmem((8, D, 256), BF16), vmem((8, D, 640), BF16), vmem((4, 8, B_ROWS, D), BF16),
            vmem((256, D), BF16), vmem((256, WIDE), F32), vmem((256, D), F32), vmem((256, WIDE), BF16),
            pltpu.SemaphoreType.DMA((2, 8)), pltpu.SemaphoreType.DMA((8,)),
            pltpu.SemaphoreType.DMA((4,))],
        compiler_params=pltpu.CompilerParams(vmem_limit_bytes=62 * 2**20),
    )(*operands)


def per_device(
    inputs, out_grad, segment_ids, qkv_weight, out_weight, up_weight, down_weight,
    norm_gains, norm_shifts, qv_bias, proj_bias, up_bias,
):
    seqs, rows, _ = inputs.shape

    blob_a = jnp.concatenate([qkv_weight, out_weight, up_weight], axis=1)
    blob_a = jnp.pad(blob_a, ((0, 12), (0, WIDE - D)))
    counts = jnp.sum(segment_ids[:, :, None] < jnp.arange(1, 4)[None, None, :], axis=1)
    counts = jnp.pad(counts.astype(BF16).reshape(1, 6), ((0, 3), (0, 130)))
    vec = jnp.concatenate(
        [norm_gains, norm_shifts, qv_bias, proj_bias, up_bias.reshape(4, 136), counts], axis=0
    )
    vec = jnp.pad(vec, ((0, 0), (0, 120)))
    blob_b = jnp.pad(down_weight.T, ((0, 8), (0, 112)))

    (w_q, w_u, w_b, att, got, got8, normed_t, lines, up_row, bounds) = enter_block(
        blob_a, blob_b, vec, inputs
    )
    (layer_out, middle_grad, att_grad, att_t, normed_two_t, active, y_o, y_u, sums, up_sums, top_t) = (
        middle_block(att, inputs, out_grad, lines, up_row, w_q, w_u, w_b)
    )
    y_q, input_grad, extra, block_u, block_b = attend_backward(
        att_grad, got, got8, inputs, middle_grad, lines, bounds, att_t, normed_two_t, y_o, y_u,
        top_t, active, sums, up_sums, w_q
    )
    out_a, out_b = leave_block(normed_t, att_t, y_q, y_o, extra, block_u, block_b)
    return (
        layer_out,
        input_grad.reshape(seqs, rows, D),
        out_a[:68, :408],
        out_a[:68, 408:544],
        out_a[:68, 544:D],
        out_b[:136, :272].T,
        out_b[136:138, :136],
        out_b[138:140, :136],
        out_b[140:142, :136],
        out_b[142:144, :136],
        out_b[136:140, 136:272].reshape(1, 544),
    )


def solution(mesh):
    tokens = P("batch", "seq", None)
    matrix = P("batch", "seq")
    vector = P(None, "seq")
    return jax.shard_map(
        per_device,
        mesh=mesh,
        in_specs=(tokens, tokens, matrix, matrix, matrix, matrix, matrix) + (vector,) * 5,
        out_specs=(tokens, tokens, matrix, matrix, matrix, matrix) + (vector,) * 5,
        check_vma=False,
    )
```

time: 422 us -> 364 us (0.86)
  the two profiles are of different devices: /device:TPU:1 before, /device:TPU:0 now
where the time goes in v4:
time: 364 us; the launch traced here: 359 us
  Pallas kernels  339 us (93%)
  local copies, waits for them, and re-layouts  17.3 us (5%)
    pallas_call x1, Pallas kernels, enter_block(): pl.pallas_call(enter_kernel, out_shape=(shape((8, D, 512), BF16), shape((...  142 us
    pallas_call x1, Pallas kernels, attend_backward(): pl.pallas_call(pull_kernel, out_shape=(jax.ShapeDtypeStruct((8, 256, 512)...  114 us
    pallas_call x1, Pallas kernels, leave_block(): pl.pallas_call(leave_kernel, out_shape=(jax.ShapeDtypeStruct((80, WIDE),...  47.3 us
    pallas_call x1, Pallas kernels, middle_block(): pl.pallas_call(middle_kernel, out_shape=(shape((2, 128, D), BF16), shape(...  35.4 us
    unnamed x17, local copies, waits for them, and re-layouts  7.31 us

profile of v4, /device:TPU:0, one launch (start us, length us, event | category | flops | bytes accessed | tf_op | source)
XLA Modules:
  0.0 359.0 jit_solution(4472325312656243041)
XLA Ops:
  0.6 0.0 copy-start.2
  0.7 0.9 fusion
  1.6 0.1 copy.49
  1.7 0.1 convert_element_type.26
  1.8 0.7 reduce
  2.5 0.1 reshape.48
  2.6 0.8 concatenate.7
  3.4 0.6 pad.19.vec
  4.0 0.9 copy.40
  4.9 1.6 pad.17.b_ref
  6.4 1.1 concatenate.6
  7.5 0.7 pad.16.a_ref
  8.2 2.1 copy.42.hidden
  10.3 0.0 copy-done.2
  10.3 1.1 copy.44.top
  11.3 142.2 %shard_map.203 = (bf16[8,1088,512]{2,1,0:T(8,128)(2,1)}, bf16[8,1088,640]{2,1,0:T(8,128)(2,1)}, bf16[4,8,144,1088]{3,2,1,0:T(8,128)(2,1)}, bf16[9,2,128,128]{3,2...) custom-call(bf16[80,1152]{1,0:T(8,128)(2,1)} %pad.16.a_ref, ...), custom_call_target="tpu_custom_call" | custom-call | tf_op jit(solution)/shard_map/pallas_call | solution.py:753
  153.6 35.4 %shard_map.204 = (bf16[2,128,1088]{2,1,0:T(8,128)(2,1)}, f32[256,1088]{1,0:T(8,128)}, bf16[9,2,128,128]{3,2,1,0:T(8,128)(2,1)}, bf16[1088,256]{1,0:T(8,128)(2,1)...) custom-call(bf16[9,2,128,128]{3,2,1,0:T(8,128)(2,1)} %get-tuple-elem, ...), custom_call_target="tpu_custom_call" | custom-call | tf_op jit(solution)/shard_map/pallas_call | solution.py:1085
  189.0 0.0 copy-start.1
  189.0 113.8 %shard_map.205 = (bf16[8,256,512]{2,1,0:T(8,128)(2,1)}, f32[256,1088]{1,0:T(8,128)}, f32[8,16,512]{2,1,0:T(8,128)}, bf16[272,640]{1,0:T(8,128)(2,1)}, bf16[144,1088]{1,0:T(8,128)(2,1)}) custom-call(bf16[9,2,128,128]{3,2,1,0:T(8,128)(2,1)} %get-tuple-element.46.pack, bf16[8,3,2,128,128]{4,3,2,1,0:T(8,128)(2,1)} %get-tuple-element.47.got, ...), custom_call_target="tpu_custom_call" | custom-call | tf_op jit(solution)/shard_map/pallas_call | solution.py:956
  302.8 0.0 copy-done.1
  302.9 1.1 copy.46
  303.9 0.0 copy-start
  303.9 47.3 %shard_map.206 = (f32[80,1152]{1,0:T(8,128)}, f32[144,384]{1,0:T(8,128)}) custom-call(bf16[1088,256]{1,0:T(8,128)(2,1)} %get-tuple-element.60.x_q, bf16[1088,256]{1,0:T(8,128)(2,1)} %get-tuple-element.51.x_o, bf16[8,256,512]{2,1,0:T(8,128)(2,1)} %get-tuple-element.61.y_q, bf16[8,256,256]{2,1,0:T(8,128)(2,1)} %get-tuple-element.53.y_o, ...), custom_call_target="tpu_custom_call" | custom-call | tf_op jit(solution)/shard_map/pallas_call | solution.py:493
  351.3 0.0 copy-start.4
  351.3 0.0 copy-start.3
  351.3 0.0 copy-done
  351.3 1.4 copy.47
  352.7 0.8 slice.35
  353.4 0.7 reshape.50
  354.1 1.4 fusion.1
  355.5 0.0 copy-done.4
  355.5 0.7 slice_bitcast_fusion
  356.2 0.0 copy-done.3
  356.2 0.1 slice.28
  356.3 0.7 copy.48
  357.1 0.7 slice.27
  357.7 0.8 slice.29
  (3 shorter events, 0.0 us)
Async XLA Ops:
  0.6 9.6 %copy-start.2 = (bf16[2,128,1088]{1,2,0:T(8,128)(2,1)S(1)}, bf16[2,128,1088]{1,2,0:T(8,128)(2,1)}, u32[]{:S(2)}) copy-start(bf16[2,128,1088]{1,2,0:T(8,128)(2,1)} %param.13) | copy-start | bytes 1671172
  189.0 113.9 %copy-start.1 = (bf16[2,128,1088]{2,1,0:T(8,128)(2,1)S(1)}, bf16[2,128,1088]{2,1,0:T(8,128)(2,1)}, u32[]{:S(2)}) copy-start(bf16[2,128,1088]{2,1,0:T(8,128)(2,1)} %get-tuple-element.89) | copy-start | bytes 1671172
  303.9 47.4 %copy-start = (f32[256,1088]{1,0:T(8,128)S(1)}, f32[256,1088]{1,0:T(8,128)}, u32[]{:S(2)}) copy-start(f32[256,1088]{1,0:T(8,128)} %get-tuple-element.59) | copy-start | bytes 3342340
  351.3 4.3 %copy-start.4 = (f32[144,384]{1,0:T(8,128)S(1)}, f32[144,384]{1,0:T(8,128)}, u32[]{:S(2)}) copy-start(f32[144,384]{1,0:T(8,128)} %get-tuple-element.66) | copy-start | bytes 663556
  351.3 5.0 %copy-start.3 = (f32[80,1152]{1,0:T(8,128)S(1)}, f32[80,1152]{1,0:T(8,128)}, u32[]{:S(2)}) copy-start(f32[80,1152]{1,0:T(8,128)} %get-tuple-element.65) | copy-start | bytes 1105924

commit v5 on v4

--- a/solution.py
+++ b/solution.py
@@ -60,12 +60,21 @@
         return copy
 
 
-LATE = (
-    [("relay", 0, 0)], [("relay", 1, 0)], [("close", 0, 0)],
-    [("relay", 1, 1)], [("relay", 0, 1)], [("relay", 1, 3)], [("relay", 0, 3)], [("close", 1, 0)],
-    [("relay", 1, 2)], [("relay", 0, 2)], [("close", 0, 1), ("close", 1, 1)],
-    [("close", 0, 3), ("close", 1, 3)], [("close", 0, 2), ("close", 1, 2)], [("settle",)],
-)
+EARLY = [("first", 1), ("first", 0), ("second", 0)]
+LATE = {
+    0: [("spread", 1), ("second", 2), ("first", 2), ("second", 1), ("spread", 0), ("relay", 0, 0), ("far", 1), ("relay", 2, 0), ("relay", 0, 1)],
+    4: [("relay", 1, 1)],
+    5: [("relay", 0, 3)],
+    6: [("relay", 1, 3), ("spread", 2), ("close", 0, 0), ("close", 2, 0)],
+    7: [("close", 0, 1), ("relay", 1, 0)],
+    8: [("close", 0, 3)],
+    9: [("far", 0), ("relay", 2, 1)],
+    11: [("relay", 1, 2), ("relay", 2, 3)],
+    12: [("close", 1, 1)],
+    13: [("close", 1, 3)],
+    14: [("far", 2), ("relay", 0, 2), ("close", 2, 1), ("close", 1, 0), ("close", 2, 3)],
+    16: [("relay", 2, 2), ("close", 1, 2), ("close", 0, 2), ("close", 2, 2)],
+}
 
 
 def merge_rows(stacked):
@@ -89,8 +98,8 @@
 
 
 class Rings:
-    def __init__(self, me, send, whole, split, source, spot):
-        self.me, self.send, self.whole, self.split = me, send, whole, split
+    def __init__(self, me, send, axes, whole, split, source, spot):
+        self.me, self.send, self.axes, self.whole, self.split = me, send, axes, whole, split
         self.source, self.spot, self.crossed, self.sent = source, spot, [], {}
 
     def move(self, axis, steps, by):
@@ -126,33 +135,33 @@
         self.cross(half, self.move(axis, steps, 2))
 
     def first(self, half):
-        self.sent[half] = self.begin(half, AXES[half][0], (0, 0))
+        self.sent[half] = self.begin(half, self.axes[half][0], (0, 0))
 
     def second(self, half):
-        self.sent[half, 0] = self.begin(half, AXES[half][1], (0, 0))
+        self.sent[half, 0] = self.begin(half, self.axes[half][1], (0, 0))
         self.cross(half, (0, 0))
 
     def spread(self, half):
-        axis = AXES[half][0]
-        self.sent[half, "far"] = self.forward(half, axis, (0, 0), self.sent[half], half)
+        axis = self.axes[half][0]
+        self.sent[half, "far"] = self.forward(half, axis, (0, 0), self.sent[half], half % 2)
         for by in (1, 3):
-            self.sent[half, by] = self.begin(half, AXES[half][1], self.move(axis, (0, 0), by))
+            self.sent[half, by] = self.begin(half, self.axes[half][1], self.move(axis, (0, 0), by))
         self.arrived(half, axis, (0, 0))
 
     def far(self, half):
-        axis = AXES[half][0]
+        axis = self.axes[half][0]
         self.finish(half, axis, (0, 0), self.sent[half, "far"])
-        self.sent[half, 2] = self.begin(half, AXES[half][1], self.move(axis, (0, 0), 2))
+        self.sent[half, 2] = self.begin(half, self.axes[half][1], self.move(axis, (0, 0), 2))
 
     def relay(self, half, by):
-        steps = self.move(AXES[half][0], (0, 0), by)
+        steps = self.move(self.axes[half][0], (0, 0), by)
         self.sent[half, by, "end"] = self.forward(
-            half, AXES[half][1], steps, self.sent[half, by], by % 2)
-        self.arrived(half, AXES[half][1], steps)
+            half, self.axes[half][1], steps, self.sent[half, by], by % 2)
+        self.arrived(half, self.axes[half][1], steps)
 
     def close(self, half, by):
-        steps = self.move(AXES[half][0], (0, 0), by)
-        self.finish(half, AXES[half][1], steps, self.sent[half, by, "end"])
+        steps = self.move(self.axes[half][0], (0, 0), by)
+        self.finish(half, self.axes[half][1], steps, self.sent[half, by, "end"])
 
     def settle(self):
         for copy in self.crossed:
@@ -557,7 +566,7 @@
     return copies
 
 
-GATHER_COPIES = 160
+GATHER_COPIES = 200
 COUNTS_ROW = 12
 
 
@@ -602,10 +611,12 @@
             return mine_b.at[pl.ds(low, rows)]
         return mine_a.at[pl.ds(low, rows), left if kind == "q" else right]
 
-    near = Rings(g, send, {0: ("q", 0, 144), 1: ("q", 144, 128)},
+    near = Rings(g, send, AXES, {0: ("q", 0, 144), 1: ("q", 144, 128)},
                  {0: [("q", 0, 64), ("q", 64, 80)], 1: [("q", 144, 64), ("q", 208, 64)]}, source, spot)
-    rest = Rings(g, send, {0: ("u", 0, 272), 1: ("b", 0, 144)},
-                 {0: [("u", 0, 128), ("u", 128, 144)], 1: [("b", 0, 64), ("b", 64, 80)]}, source, spot)
+    rest = Rings(g, send, {0: ("x", "y"), 1: ("y", "x"), 2: ("x", "y")},
+                 {0: ("u", 0, 272), 1: ("b", 48, 96), 2: ("b", 0, 48)},
+                 {0: [("u", 0, 128), ("u", 128, 144)], 1: [("b", 48, 48), ("b", 96, 48)],
+                  2: [("b", 0, 16), ("b", 16, 32)]}, source, spot)
     near.run(("first", 0), ("first", 1), ("second", 0), ("second", 1))
     own = [pltpu.make_async_copy(source(part), spot(part, 0, 0), local_sems.at[k])
            for k, part in enumerate((("q", 0, A_ROWS), ("u", 0, A_ROWS), ("b", 0, B_ROWS)))]
@@ -642,7 +653,7 @@
     own[2].start()
     near.run(("far", 0), ("far", 1), ("relay", 0, 1), ("relay", 1, 1), ("close", 0, 0),
              ("close", 1, 0), ("relay", 0, 3), ("relay", 1, 3), ("relay", 0, 2), ("relay", 1, 2))
-    rest.run(("first", 1), ("first", 0), ("second", 0))
+    rest.run(*EARLY)
     near.run(*[("close", half, by) for by in (1, 3, 2) for half in (0, 1)], ("settle",))
     own[0].wait()
     kept = pltpu.make_async_copy(weights, gq, local_sems.at[3])
@@ -660,11 +671,11 @@
                 tile = tile + table[row : row + 1, 128 * p : 128 * p + 128]
             pack[p, kind] = tile.astype(BF16).reshape(2, 128, 128)
 
-    rest_events = list(LATE)
+    ticks = [0]
 
     def pump():
-        if rest_events:
-            rest.run(*rest_events.pop(0))
+        ticks[0] += 1
+        rest.run(*LATE.get(ticks[0], ()))
 
     def in_copy(step):
         return push(pack.at[g.other(step)], got.at[g.seq], in_sems, (step - 1,), g.member(g.other(step)))
@@ -685,7 +696,7 @@
         def _():
             got8[g.seq] = pack[8, :, extra]
     got[g.seq] = pack[g.seq]
-    rest.run(("spread", 1), ("spread", 0), ("second", 1), ("far", 1), ("far", 0))
+    rest.run(*LATE[0])
     for step in range(1, 8):
         in_copy(step).wait_recv()
 
@@ -735,8 +746,7 @@
         for seq in (0, 1):
             back_copy(seq, step).wait_recv()
             back_copy(seq, step).wait_send()
-    while rest_events:
-        rest.run(*rest_events.pop(0))
+    rest.run(("settle",))
     for copy in send.made:
         copy.wait_send()
     for step in range(1, 8):

time: 364 us -> 353 us (0.970)
  Pallas kernels: 339 us -> 328 us
    pallas_call x1, Pallas kernels: 142 us -> 132 us  [enter_block(): pl.pallas_call(enter_kernel, out_shape=(shape((8, D, 512), BF16), shape((...]
where the time goes in v5:
time: 353 us; the launch traced here: 348 us
  Pallas kernels  328 us (93%)
  local copies, waits for them, and re-layouts  17.3 us (5%)
    pallas_call x1, Pallas kernels, enter_block(): pl.pallas_call(enter_kernel, out_shape=(shape((8, D, 512), BF16), shape((...  132 us
    pallas_call x1, Pallas kernels, attend_backward(): pl.pallas_call(pull_kernel, out_shape=(jax.ShapeDtypeStruct((8, 256, 512)...  114 us
    pallas_call x1, Pallas kernels, leave_block(): pl.pallas_call(leave_kernel, out_shape=(jax.ShapeDtypeStruct((80, WIDE),...  47.1 us
    pallas_call x1, Pallas kernels, middle_block(): pl.pallas_call(middle_kernel, out_shape=(shape((2, 128, D), BF16), shape(...  35.4 us
    unnamed x17, local copies, waits for them, and re-layouts  7.31 us

profile of v5, /device:TPU:0, one launch (start us, length us, event | category | flops | bytes accessed | tf_op | source)
XLA Modules:
  0.0 347.9 jit_solution(5821056113252541358)
XLA Ops:
  0.6 0.0 copy-start.2
  0.7 0.9 fusion
  1.6 0.1 copy.49
  1.7 0.1 convert_element_type.26
  1.8 0.7 reduce
  2.5 0.1 reshape.48
  2.6 0.8 concatenate.7
  3.4 0.6 pad.19.vec
  4.0 0.9 copy.40
  4.9 1.6 pad.17.b_ref
  6.4 1.1 concatenate.6
  7.5 0.7 pad.16.a_ref
  8.2 2.1 copy.42.hidden
  10.3 0.0 copy-done.2
  10.3 1.1 copy.44.top
  11.3 131.7 %shard_map.203 = (bf16[8,1088,512]{2,1,0:T(8,128)(2,1)}, bf16[8,1088,640]{2,1,0:T(8,128)(2,1)}, bf16[4,8,144,1088]{3,2,1,0:T(8,128)(2,1)}, bf16[9,2,128,128]{3,2...) custom-call(bf16[80,1152]{1,0:T(8,128)(2,1)} %pad.16.a_ref, ...), custom_call_target="tpu_custom_call" | custom-call | tf_op jit(solution)/shard_map/pallas_call | solution.py:763
  143.0 35.4 %shard_map.204 = (bf16[2,128,1088]{2,1,0:T(8,128)(2,1)}, f32[256,1088]{1,0:T(8,128)}, bf16[9,2,128,128]{3,2,1,0:T(8,128)(2,1)}, bf16[1088,256]{1,0:T(8,128)(2,1)...) custom-call(bf16[9,2,128,128]{3,2,1,0:T(8,128)(2,1)} %get-tuple-elem, ...), custom_call_target="tpu_custom_call" | custom-call | tf_op jit(solution)/shard_map/pallas_call | solution.py:1095
  178.4 0.0 copy-start.1
  178.4 113.6 %shard_map.205 = (bf16[8,256,512]{2,1,0:T(8,128)(2,1)}, f32[256,1088]{1,0:T(8,128)}, f32[8,16,512]{2,1,0:T(8,128)}, bf16[272,640]{1,0:T(8,128)(2,1)}, bf16[144,1088]{1,0:T(8,128)(2,1)}) custom-call(bf16[9,2,128,128]{3,2,1,0:T(8,128)(2,1)} %get-tuple-element.46.pack, bf16[8,3,2,128,128]{4,3,2,1,0:T(8,128)(2,1)} %get-tuple-element.47.got, ...), custom_call_target="tpu_custom_call" | custom-call | tf_op jit(solution)/shard_map/pallas_call | solution.py:966
  292.1 0.0 copy-done.1
  292.1 1.1 copy.46
  293.1 0.0 copy-start
  293.1 47.1 %shard_map.206 = (f32[80,1152]{1,0:T(8,128)}, f32[144,384]{1,0:T(8,128)}) custom-call(bf16[1088,256]{1,0:T(8,128)(2,1)} %get-tuple-element.60.x_q, bf16[1088,256]{1,0:T(8,128)(2,1)} %get-tuple-element.51.x_o, bf16[8,256,512]{2,1,0:T(8,128)(2,1)} %get-tuple-element.61.y_q, bf16[8,256,256]{2,1,0:T(8,128)(2,1)} %get-tuple-element.53.y_o, ...), custom_call_target="tpu_custom_call" | custom-call | tf_op jit(solution)/shard_map/pallas_call | solution.py:502
  340.2 0.0 copy-start.4
  340.2 0.0 copy-start.3
  340.2 0.0 copy-done
  340.2 1.4 copy.47
  341.6 0.8 slice.35
  342.3 0.7 reshape.50
  343.0 1.4 fusion.1
  344.5 0.0 copy-done.4
  344.5 0.7 slice_bitcast_fusion
  345.2 0.0 copy-done.3
  345.2 0.1 slice.28
  345.2 0.7 copy.48
  346.0 0.7 slice.27
  346.7 0.8 slice.29
  (3 shorter events, 0.0 us)
Async XLA Ops:
  0.6 9.6 %copy-start.2 = (bf16[2,128,1088]{1,2,0:T(8,128)(2,1)S(1)}, bf16[2,128,1088]{1,2,0:T(8,128)(2,1)}, u32[]{:S(2)}) copy-start(bf16[2,128,1088]{1,2,0:T(8,128)(2,1)} %param.13) | copy-start | bytes 1671172
  178.4 113.6 %copy-start.1 = (bf16[2,128,1088]{2,1,0:T(8,128)(2,1)S(1)}, bf16[2,128,1088]{2,1,0:T(8,128)(2,1)}, u32[]{:S(2)}) copy-start(bf16[2,128,1088]{2,1,0:T(8,128)(2,1)} %get-tuple-element.89) | copy-start | bytes 1671172
  293.1 47.1 %copy-start = (f32[256,1088]{1,0:T(8,128)S(1)}, f32[256,1088]{1,0:T(8,128)}, u32[]{:S(2)}) copy-start(f32[256,1088]{1,0:T(8,128)} %get-tuple-element.59) | copy-start | bytes 3342340
  340.2 4.3 %copy-start.4 = (f32[144,384]{1,0:T(8,128)S(1)}, f32[144,384]{1,0:T(8,128)}, u32[]{:S(2)}) copy-start(f32[144,384]{1,0:T(8,128)} %get-tuple-element.66) | copy-start | bytes 663556
  340.2 5.0 %copy-start.3 = (f32[80,1152]{1,0:T(8,128)S(1)}, f32[80,1152]{1,0:T(8,128)}, u32[]{:S(2)}) copy-start(f32[80,1152]{1,0:T(8,128)} %get-tuple-element.65) | copy-start | bytes 1105924

commit v6 on v5

--- a/solution.py
+++ b/solution.py
@@ -320,15 +320,16 @@
             return jnp.concatenate([value[:cut] + arrived[:cut].astype(F32), value[cut:]], axis=0)
         return jnp.concatenate([value[:cut], value[cut:] + arrived[cut:].astype(F32)], axis=0)
 
-    def sides(self, which):
+    def sides(self):
         def body(o):
             for half in (0, 1):
                 b = self.blocks[half]
-                value = self.mine(half, 1 + 2 * which, o)
-                self.opp_copy(half, o, which).wait_recv()
-                value = self.join(half, value, b["in_opp"].at[o], which)
-                b["sib_in"][1 + 2 * which, o] = value.astype(BF16)
-                self.side_copy(half, o, which).start()
+                for which in (0, 1):
+                    value = self.mine(half, 1 + 2 * which, o)
+                    self.opp_copy(half, o, which).wait_recv()
+                    value = self.join(half, value, b["in_opp"].at[o], which)
+                    b["sib_in"][1 + 2 * which, o] = value.astype(BF16)
+                    self.side_copy(half, o, which).start()
         self.loop(body)
 
     def own(self):
@@ -458,8 +459,7 @@
     reduce.cross(1, 2)
     reduce.cross(3, 1)
     early(2)
-    reduce.sides(0)
-    reduce.sides(1)
+    reduce.sides()
     reduce.cross(0, 3)
     early(1)
     early(3)
@@ -863,8 +863,7 @@
     reduce.opposite()
     reduce.cross(1, 2)
     reduce.cross(3, 1)
-    reduce.sides(0)
-    reduce.sides(1)
+    reduce.sides()
     for step in range(1, 8):
         in_copy(step).wait_recv()
 

time: 353 us -> 352 us (level)
  no operation moved by 1% of the time
where the time goes in v6:
time: 352 us; the launch traced here: 346 us
  Pallas kernels  326 us (93%)
  local copies, waits for them, and re-layouts  17.3 us (5%)
    pallas_call x1, Pallas kernels, enter_block(): pl.pallas_call(enter_kernel, out_shape=(shape((8, D, 512), BF16), shape((...  132 us
    pallas_call x1, Pallas kernels, attend_backward(): pl.pallas_call(pull_kernel, out_shape=(jax.ShapeDtypeStruct((8, 256, 512)...  114 us
    pallas_call x1, Pallas kernels, leave_block(): pl.pallas_call(leave_kernel, out_shape=(jax.ShapeDtypeStruct((80, WIDE),...  45.4 us
    pallas_call x1, Pallas kernels, middle_block(): pl.pallas_call(middle_kernel, out_shape=(shape((2, 128, D), BF16), shape(...  35.4 us
    unnamed x17, local copies, waits for them, and re-layouts  7.31 us

profile of v6, /device:TPU:0, one launch (start us, length us, event | category | flops | bytes accessed | tf_op | source)
XLA Modules:
  0.0 346.2 jit_solution(10559085528333773836)
XLA Ops:
  0.6 0.0 copy-start.2
  0.7 0.9 fusion
  1.6 0.1 copy.49
  1.7 0.1 convert_element_type.26
  1.8 0.7 reduce
  2.5 0.1 reshape.48
  2.6 0.8 concatenate.7
  3.4 0.6 pad.19.vec
  4.0 0.9 copy.40
  4.9 1.6 pad.17.b_ref
  6.4 1.1 concatenate.6
  7.5 0.7 pad.16.a_ref
  8.2 2.1 copy.42.hidden
  10.3 0.0 copy-done.2
  10.3 1.1 copy.44.top
  11.3 131.7 %shard_map.203 = (bf16[8,1088,512]{2,1,0:T(8,128)(2,1)}, bf16[8,1088,640]{2,1,0:T(8,128)(2,1)}, bf16[4,8,144,1088]{3,2,1,0:T(8,128)(2,1)}, bf16[9,2,128,128]{3,2...) custom-call(bf16[80,1152]{1,0:T(8,128)(2,1)} %pad.16.a_ref, ...), custom_call_target="tpu_custom_call" | custom-call | tf_op jit(solution)/shard_map/pallas_call | solution.py:763
  143.0 35.4 %shard_map.204 = (bf16[2,128,1088]{2,1,0:T(8,128)(2,1)}, f32[256,1088]{1,0:T(8,128)}, bf16[9,2,128,128]{3,2,1,0:T(8,128)(2,1)}, bf16[1088,256]{1,0:T(8,128)(2,1)...) custom-call(bf16[9,2,128,128]{3,2,1,0:T(8,128)(2,1)} %get-tuple-elem, ...), custom_call_target="tpu_custom_call" | custom-call | tf_op jit(solution)/shard_map/pallas_call | solution.py:1094
  178.4 0.0 copy-start.1
  178.4 113.6 %shard_map.205 = (bf16[8,256,512]{2,1,0:T(8,128)(2,1)}, f32[256,1088]{1,0:T(8,128)}, f32[8,16,512]{2,1,0:T(8,128)}, bf16[272,640]{1,0:T(8,128)(2,1)}, bf16[144,1088]{1,0:T(8,128)(2,1)}) custom-call(bf16[9,2,128,128]{3,2,1,0:T(8,128)(2,1)} %get-tuple-element.46.pack, bf16[8,3,2,128,128]{4,3,2,1,0:T(8,128)(2,1)} %get-tuple-element.47.got, ...), custom_call_target="tpu_custom_call" | custom-call | tf_op jit(solution)/shard_map/pallas_call | solution.py:965
  292.1 0.0 copy-done.1
  292.1 1.1 copy.46
  293.1 0.0 copy-start
  293.1 45.4 %shard_map.206 = (f32[80,1152]{1,0:T(8,128)}, f32[144,384]{1,0:T(8,128)}) custom-call(bf16[1088,256]{1,0:T(8,128)(2,1)} %get-tuple-element.60.x_q, bf16[1088,256]{1,0:T(8,128)(2,1)} %get-tuple-element.51.x_o, bf16[8,256,512]{2,1,0:T(8,128)(2,1)} %get-tuple-element.61.y_q, bf16[8,256,256]{2,1,0:T(8,128)(2,1)} %get-tuple-element.53.y_o, ...), custom_call_target="tpu_custom_call" | custom-call | tf_op jit(solution)/shard_map/pallas_call | solution.py:502
  338.5 0.0 copy-start.4
  338.5 0.0 copy-start.3
  338.5 0.0 copy-done
  338.5 1.4 copy.47
  339.9 0.8 slice.35
  340.7 0.7 reshape.50
  341.3 1.4 fusion.1
  342.8 0.0 copy-done.4
  342.8 0.7 slice_bitcast_fusion
  343.5 0.0 copy-done.3
  343.5 0.1 slice.28
  343.6 0.7 copy.48
  344.3 0.7 slice.27
  345.0 0.8 slice.29
  (3 shorter events, 0.0 us)
Async XLA Ops:
  0.6 9.6 %copy-start.2 = (bf16[2,128,1088]{1,2,0:T(8,128)(2,1)S(1)}, bf16[2,128,1088]{1,2,0:T(8,128)(2,1)}, u32[]{:S(2)}) copy-start(bf16[2,128,1088]{1,2,0:T(8,128)(2,1)} %param.13) | copy-start | bytes 1671172
  178.4 113.6 %copy-start.1 = (bf16[2,128,1088]{2,1,0:T(8,128)(2,1)S(1)}, bf16[2,128,1088]{2,1,0:T(8,128)(2,1)}, u32[]{:S(2)}) copy-start(bf16[2,128,1088]{2,1,0:T(8,128)(2,1)} %get-tuple-element.89) | copy-start | bytes 1671172
  293.1 45.4 %copy-start = (f32[256,1088]{1,0:T(8,128)S(1)}, f32[256,1088]{1,0:T(8,128)}, u32[]{:S(2)}) copy-start(f32[256,1088]{1,0:T(8,128)} %get-tuple-element.59) | copy-start | bytes 3342340
  338.5 4.3 %copy-start.4 = (f32[144,384]{1,0:T(8,128)S(1)}, f32[144,384]{1,0:T(8,128)}, u32[]{:S(2)}) copy-start(f32[144,384]{1,0:T(8,128)} %get-tuple-element.66) | copy-start | bytes 663556
  338.5 5.0 %copy-start.3 = (f32[80,1152]{1,0:T(8,128)S(1)}, f32[80,1152]{1,0:T(8,128)}, u32[]{:S(2)}) copy-start(f32[80,1152]{1,0:T(8,128)} %get-tuple-element.65) | copy-start | bytes 1105924
